TPU v7x, 256 devices: a whole 4x4x8 slice. The times are simulated.
256 devices in a mesh: wide: 16 (over x, y), narrow: 16 (over z, core).
Axes of the slice: x: 4, y: 4, z: 8, core: 2. Of those that a mesh axis runs over, the one named last changes fastest.
Arguments:
- features: bfloat16 [512, 16, 256, 128], P(('wide', 'narrow'))
- out_cotangent: bfloat16 [512, 16, 256, 128], P(('wide', 'narrow'))
- occupancy: int32 [512, 16, 16], P(('wide', 'narrow')), may hold values from 0 to 65535, as said below
- live_slots: int32 [16, 16], P('wide'), may hold values from 0 to 31, as said below
- neighbours: int32 [256, 27], P('wide'), may hold values from -1 to 255, as said below
- timestep: int32 [1], replicated, may hold values from 0 to 999
- norm_gain: float32 [128], replicated, may hold values from 0.1 to 1.9
- norm_bias: float32 [128], replicated, may hold values from -3 to 3
- film_weight: float32 [256, 256], replicated, may hold values from -0.375 to 0.375
- conv_weight: bfloat16 [27, 128, 128], replicated, may hold values from -0.15625 to 0.15625
- conv_bias: float32 [128], replicated, may hold values from -3 to 3
Outputs:
- mixed: bfloat16 [512, 16, 256, 128], P(('wide', 'narrow'))
- feature_grad: bfloat16 [512, 16, 256, 128], P(('wide', 'narrow'))
- weight_step: float32 [27, 128, 128], replicated
Inputs may be any that keep to these rules, and one draw needn't show every extreme that they name: `live_slots`: each row lists 16 distinct slots in rising order; slots not listed have all occupancy words zero. `occupancy`: bit x of a word marks voxel x of that row; every listed block has its centre voxel occupied. `neighbours`: entry 9 (dz + 1) + 3 (dy + 1) + (dx + 1) of a row is the live number of the live block at that block offset, or -1 where no live block lies there; entry 13 is the block itself; the relation is symmetric; the coarse group of a block is its x coordinate among blocks: entries with dx = -1 or dx = 1 name blocks of coarse group w - 1 or w + 1, all other entries name blocks of the same coarse group.
All inputs are finite; a program needn't handle non-finite values.
Results may differ from a plain program's by a relative error of at most 0.0029.
Values may be sent and summed in bfloat16 or wider, within the bound.
No kernel may reach another device: no remote copies, remote signals or barrier semaphores. Data moves between devices by JAX's collectives and lax.ppermute only.
A program may use at most 256 MiB of HBM per device.

v0:
```python
import jax
import jax.numpy as jnp
from jax import lax
from jax.sharding import PartitionSpec as P

G = 32
EDGE = 16


norm_eps = 1e-05
step_eps = 1e-06


def passed_along(block, axis, distance):
    devices = range(lax.axis_size(axis))
    route = [((i - distance) % len(devices), i) for i in devices]
    return lax.ppermute(block, axis, route)


def padded_2(cells, sides, width):
    for axis, dim in sides:
        count = lax.axis_size(axis)
        ends = count - 1
        head = lax.slice_in_dim(cells, 0, width, axis=dim)
        tail = lax.slice_in_dim(cells, cells.shape[dim] - width, cells.shape[dim], axis=dim)
        cells = jnp.concatenate(
            [
                lax.ppermute(tail, axis, [(i, (i + 1) % count) for i in range(ends)]),
                cells,
                lax.ppermute(head, axis, [((i + 1) % count, i) for i in range(ends)]),
            ],
            axis=dim,
        )
    return cells


def film_terms(timestep, film_weight):
    half_width = film_weight.shape[0] // 2
    channels = film_weight.shape[1] // 2
    frequencies = jnp.exp(
        -jnp.log(10000.0) * jnp.arange(half_width).astype(jnp.float32) / half_width
    )
    angles = timestep.astype(jnp.float32)[0] * frequencies
    embedding = jax.nn.silu(jnp.concatenate([jnp.cos(angles), jnp.sin(angles)]))
    film_out = jnp.dot(embedding[None, :], film_weight, precision=lax.Precision.HIGHEST)[0]
    return (film_out[:channels], film_out[channels:])


def unpack_mask(packed):
    bit_width = packed.shape[-1]
    shifts = jnp.arange(bit_width)
    bit_values = jnp.bitwise_and(jnp.right_shift(packed[..., None], shifts), 1)
    return bit_values.reshape(packed.shape[:-1] + (bit_width * bit_width, 1)).astype(jnp.float32)


def pick_rows(source, wanted, first_live):
    local_index = wanted - first_live
    usable = (wanted >= 0) & (local_index >= 0) & (local_index < source.shape[0])
    picked = source[jnp.clip(local_index, 0, source.shape[0] - 1)]
    return jnp.where(
        usable.reshape((-1,) + (1,) * (picked.ndim - 1)), picked, jnp.zeros_like(picked)
    )


def neighbourhood(values, neighbours):
    live_count, slab_depth, plane_cells, channels = values.shape
    lower_plane = passed_along(values, "narrow", 1)
    upper_plane = passed_along(values, "narrow", -1)
    stacked = jnp.concatenate([lower_plane, values, upper_plane], axis=1)
    lookup = padded_2(stacked, (("wide", 0),), live_count)
    lookup = lookup.reshape(3 * live_count, slab_depth + 2, EDGE, EDGE, channels)
    first_live = (lax.axis_index("wide") - 1) * live_count
    at_bottom = lax.axis_index("narrow") == 0
    at_top = lax.axis_index("narrow") == lax.axis_size("narrow") - 1
    rim_spans = (slice(EDGE - 1, EDGE), slice(0, EDGE), slice(0, 1))
    row_parts = []
    for off_y in range(3):
        col_parts = []
        for off_x in range(3):
            centre = 9 + 3 * off_y + off_x
            middle = neighbours[:, centre]
            lower_ids = jnp.where(at_bottom, neighbours[:, centre - 9], middle)
            upper_ids = jnp.where(at_top, neighbours[:, centre + 9], middle)
            rim_cells = lookup[:, :, rim_spans[off_y], rim_spans[off_x]]
            low_part = pick_rows(rim_cells[:, :1], lower_ids, first_live)
            mid_part = pick_rows(rim_cells[:, 1 : slab_depth + 1], middle, first_live)
            high_part = pick_rows(rim_cells[:, slab_depth + 1 :], upper_ids, first_live)
            col_parts.append(jnp.concatenate([low_part, mid_part, high_part], axis=1))
        row_parts.append(jnp.concatenate(col_parts, axis=3))
    return jnp.concatenate(row_parts, axis=2)


def tap_offsets(offset, flipped):
    off_z, off_y, off_x = (offset // 9, offset // 3 % 3, offset % 3)
    if flipped:
        return (2 - off_z, 2 - off_y, 2 - off_x)
    return (off_z, off_y, off_x)


def tap_columns(padded, layer, flipped):
    slab_depth = padded.shape[1] - 2
    channels = padded.shape[-1]
    pieces = []
    for offset in range(9 * layer, 9 * layer + 9):
        off_z, off_y, off_x = tap_offsets(offset, flipped)
        pieces.append(
            padded[:, off_z : off_z + slab_depth, off_y : off_y + EDGE, off_x : off_x + EDGE]
        )
    return jnp.concatenate(pieces, axis=-1).reshape(-1, 9 * channels)


def layer_kernel(weight, layer, flipped):
    kernels = [
        weight[offset].T if flipped else weight[offset]
        for offset in range(9 * layer, 9 * layer + 9)
    ]
    return jnp.concatenate(kernels, axis=0)


def apply_taps(padded, weight):
    slab_depth = padded.shape[1] - 2
    running = jnp.zeros((padded.shape[0] * slab_depth * EDGE * EDGE, weight.shape[-1]), jnp.float32)
    for layer in range(3):
        columns = tap_columns(padded, layer, True)
        running = running + jnp.dot(
            columns, layer_kernel(weight, layer, True), preferred_element_type=jnp.float32
        )
    return running


def conv_with_grads(padded, weight, upstream_rows):
    slab_depth = padded.shape[1] - 2
    channels = padded.shape[-1]
    running = jnp.zeros((padded.shape[0] * slab_depth * EDGE * EDGE, weight.shape[-1]), jnp.float32)
    grads = []
    for layer in range(3):
        columns = tap_columns(padded, layer, False)
        running = running + jnp.dot(
            columns, layer_kernel(weight, layer, False), preferred_element_type=jnp.float32
        )
        layer_grad = lax.dot_general(
            columns, upstream_rows, (((0,), (0,)), ((), ())), preferred_element_type=jnp.float32
        )
        grads.append(layer_grad.reshape(9, channels, channels))
    return (running, jnp.concatenate(grads, axis=0))


def local(
    features,
    out_cotangent,
    occupancy,
    live_slots,
    neighbours,
    timestep,
    norm_gain,
    norm_bias,
    film_weight,
    conv_weight,
    conv_bias,
):
    channels = features.shape[-1]
    group_width = channels // G
    slab_feats, slab_cotan, slab_packed = (
        lax.all_to_all(features, "narrow", split_axis=1, concat_axis=0, tiled=True),
        lax.all_to_all(out_cotangent, "narrow", split_axis=1, concat_axis=0, tiled=True),
        lax.all_to_all(occupancy, "narrow", split_axis=1, concat_axis=0, tiled=True),
    )
    live_order = live_slots[0]
    blocks = slab_feats[live_order]
    cotan = slab_cotan[live_order]
    occupied = unpack_mask(slab_packed[live_order])
    upstream = cotan * occupied.astype(jnp.bfloat16)
    masked = blocks.astype(jnp.float32) * occupied
    first_sums = jnp.sum(masked.reshape(-1, G, group_width), axis=(0, 2))
    squares = jnp.sum(
        (masked * blocks.astype(jnp.float32)).reshape(-1, G, group_width), axis=(0, 2)
    )
    first_sums, squares, voxel_total = lax.psum(
        (first_sums, squares, jnp.sum(occupied).reshape(1)), ("wide", "narrow")
    )
    voxel_count = voxel_total[0] * group_width
    group_mean = first_sums / voxel_count
    group_rstd = lax.rsqrt(squares / voxel_count - group_mean * group_mean + norm_eps)
    mean_chan = jnp.repeat(group_mean, group_width)
    rstd_chan = jnp.repeat(group_rstd, group_width)
    film_scale, film_shift = film_terms(timestep, film_weight)
    normed = (blocks.astype(jnp.float32) - mean_chan) * rstd_chan
    pre_act = (normed * norm_gain + norm_bias) * (1.0 + film_scale) + film_shift
    hidden = (jax.nn.silu(pre_act) * occupied).astype(jnp.bfloat16)
    padded = neighbourhood(hidden, neighbours)
    conv_flat, local_grads = conv_with_grads(padded, conv_weight, upstream.reshape(-1, channels))
    conv_out = conv_flat.reshape(blocks.shape)
    mixed_live = (blocks.astype(jnp.float32) + (conv_out + conv_bias) * occupied).astype(
        jnp.bfloat16
    )
    weight_total = lax.psum(local_grads, ("wide", "narrow"))
    weight_step = weight_total * lax.rsqrt(jnp.mean(weight_total * weight_total) + step_eps)
    back_grad = apply_taps(neighbourhood(upstream, neighbours), conv_weight).reshape(blocks.shape)
    gate_sig = jax.nn.sigmoid(pre_act)
    grad_hat = (
        back_grad
        * occupied
        * gate_sig
        * (1.0 + pre_act * (1.0 - gate_sig))
        * (1.0 + film_scale)
        * norm_gain
    )
    first_grad = jnp.sum(grad_hat.reshape(-1, G, group_width), axis=(0, 2))
    second_grad = jnp.sum((grad_hat * normed).reshape(-1, G, group_width), axis=(0, 2))
    first_grad, second_grad = lax.psum((first_grad, second_grad), ("wide", "narrow"))
    first_chan = jnp.repeat(first_grad, group_width)
    second_chan = jnp.repeat(second_grad, group_width)
    correction = (
        rstd_chan
        * (grad_hat - first_chan / voxel_count - normed * second_chan / voxel_count)
        * occupied
    )
    grad_live = (cotan.astype(jnp.float32) + correction).astype(jnp.bfloat16)
    mixed_slab = slab_feats.at[live_order].set(mixed_live)
    grad_slab = slab_cotan.at[live_order].set(grad_live)
    mixed, feature_grad = (
        lax.all_to_all(mixed_slab, "narrow", split_axis=0, concat_axis=1, tiled=True),
        lax.all_to_all(grad_slab, "narrow", split_axis=0, concat_axis=1, tiled=True),
    )
    return (mixed, feature_grad, weight_step)


def solution(mesh):
    return jax.shard_map(
        local,
        mesh=mesh,
        in_specs=(
            P(("wide", "narrow"), None, None, None),
            P(("wide", "narrow"), None, None, None),
            P(("wide", "narrow"), None, None),
            P("wide", None),
            P("wide", None),
            P(),
            P(),
            P(),
            P(),
            P(),
            P(),
        ),
        out_specs=(
            P(("wide", "narrow"), None, None, None),
            P(("wide", "narrow"), None, None, None),
            P(),
        ),
        check_vma=False,
    )
```

profile of v0, /device:TPU:1, one launch (start us, length us, event | category | flops | bytes accessed | tf_op | source)
XLA Modules:
  0.0 1135.1 jit_solution(8033152780149589591)
XLA Ops:
  8.7 10.0 all-to-all-start.1
  29.5 3.1 copy.269
  34.1 7.2 all-to-all-start.3
  55.1 35.3 %all-to-all-done.3 = bf16[2,16,256,128]{3,2,0,1:T(8,128)(2,1)} async-done(((bf16[2,16,256,128]{3,2,0,1:T(8,128)(2,1)}), bf16[2,16,256,128]{3,2,0,1:T(8,128)(2,1)}, u32[]{:S(2)}, u32[]{:S(2)}) %all-to-all-start.3) | async-done | bytes 2097184 | tf_op jit(solution)/shard_map/all_to_all | solution.py:165
  90.4 5.0 all-to-all-start
  106.2 46.2 %collective-permute-done.4 = bf16[16,1,256,128]{3,2,0,1:T(8,128)(2,1)S(1)} collective-permute-done((bf16[16,1,256,128]{3,2,0,1:T(8,128)(2,1)S(1)}, bf16[16,1,256,128]{3,2,0,1:T(8,128)(2,1)S(1)}, u32[]{:S(2)}, u32[]{:S(2)}) %collective-permute-start.4) | collective-permute-done | bytes 1048608 | tf_op jit(solution)/shard_map/ppermute | solution.py:17
  157.5 4.8 collective-permute-start.6
  183.2 119.2 %all-reduce.1 = (f32[32]{0:T(128)S(1)}, f32[1]{0:T(128)}, f32[32]{0:T(128)S(1)}) all-reduce(f32[32]{0:T(128)S(1)} %reduce_sum.67, f32[1]{0:T(128)} %bitcast.12, f32[32]{0:T(128)S(1)} %reduce_sum.88), channel_id=1, replica_groups=mesh['wide'=16,'narrow'=16] {'wide','narrow'}, use_global_device_ids=true, to_apply=%region_2.0 | all-reduce | flops 65 | bytes 520 | tf_op jit(solution)/shard_map/psum | solution.py:178
  304.5 7.3 pad_maximum_fusion.1
  311.8 10.9 copy.270
  326.7 4.8 fusion.56
  331.7 6.8 slice_bitcast_fusion.2
  355.6 2.6 gather_fusion.35
  359.2 2.6 gather_fusion.34
  362.9 3.5 gather_fusion.33
  367.8 4.0 pad_maximum_fusion.10
  371.8 2.6 pad_maximum_fusion.7
  389.1 8.1 maximum_maximum_fusion.1
  406.5 3.0 constant_dynamic-update-slice_fusion.94
  414.8 3.0 constant_dynamic-update-slice_fusion.76
  419.7 3.4 constant_dynamic-update-slice_fusion.58
  424.2 2.6 fusion.65
  426.9 3.7 convolution_add_fusion.1
  430.8 4.9 fusion.53
  436.1 72.7 %all-reduce = (f32[32]{0:T(128)S(1)}, f32[32]{0:T(128)S(1)}) all-reduce(f32[32]{0:T(128)S(1)} %reduce_sum.94, f32[32]{0:T(128)S(1)} %reduce_sum.91), channel_id=1, replica_groups=mesh['wide'=16,'narrow'=16] {'wide','narrow'}, use_global_device_ids=true, to_apply=%region_14.15 | all-reduce | flops 64 | bytes 512 | tf_op jit(solution)/shard_map/psum | solution.py:210
  509.1 4.2 fusion.22
  515.5 11.7 %collective-permute-done = bf16[16,1,256,128]{3,2,0,1:T(8,128)(2,1)S(1)} collective-permute-done((bf16[16,1,256,128]{3,2,0,1:T(8,128)(2,1)S(1)}, bf16[16,1,256,128]{3,2,0,1:T(8,128)(2,1)S(1)}, u32[]{:S(2)}, u32[]{:S(2)}) %collective-permute-start) | collective-permute-done | bytes 1048608 | tf_op jit(solution)/shard_map/ppermute | solution.py:17
  527.2 2.5 collective-permute-done.1
  531.7 4.3 collective-permute-start.2
  550.2 3.4 scatter_fusion.1
  553.6 5.3 all-to-all-start.4
  558.9 43.7 %collective-permute-done.2 = bf16[16,3,256,128]{3,2,0,1:T(8,128)(2,1)} collective-permute-done((bf16[16,3,256,128]{3,2,0,1:T(8,128)(2,1)}, bf16[16,3,256,128]{3,2,0,1:T(8,128)(2,1)}, u32[]{:S(2)}, u32[]{:S(2)}) %collective-permute-start.2) | collective-permute-done | bytes 3145760 | tf_op jit(solution)/shard_map/ppermute | solution.py:28
  602.5 5.5 collective-permute-done.3
  608.0 7.0 pad_maximum_fusion
  615.0 13.4 %copy.217 = bf16[48,3,256,128]{3,0,2,1:T(8,128)(2,1)} copy(bf16[48,3,256,128]{3,2,0,1:T(8,128)(2,1)} %pad_maximum_fusion) | data formatting | bytes 18874368 | tf_op jit(solution)/shard_map/concatenate | solution.py:26
  634.5 6.9 slice_bitcast_fusion.5
  679.4 2.5 copy.239
  681.9 2.8 gather_fusion.15
  685.5 4.4 copy.238
  689.9 2.8 gather_fusion.14
  693.4 4.4 copy.241
  697.8 3.7 gather_fusion.16
  747.4 2.7 pad_maximum_fusion.20
  752.7 6.7 pad_maximum_fusion.2
  759.5 3.8 fusion.60
  764.5 3.0 constant_dynamic-update-slice_fusion.40
  767.5 2.9 fusion.59
  775.3 3.0 constant_dynamic-update-slice_fusion.22
  779.3 3.0 constant_dynamic-update-slice_fusion.4
  785.5 3.9 fusion.64
  791.3 3.9 convolution_add_fusion.3
  795.2 3.7 convolution_add_fusion.2
  799.7 3.0 scatter_fusion
  802.7 5.6 all-to-all-start.2
  808.3 12.9 %copy.293 = bf16[1152,4096]{1,0:T(8,128)(2,1)} copy(bf16[1152,4096]{0,1:T(8,128)(2,1)} %bitcast.684) | data formatting | bytes 18874368 | tf_op jit(solution)/shard_map/dot_general | solution.py:141
  821.2 12.1 %copy.292 = bf16[1152,4096]{1,0:T(8,128)(2,1)} copy(bf16[1152,4096]{0,1:T(8,128)(2,1)} %bitcast.685) | data formatting | bytes 18874368 | tf_op jit(solution)/shard_map/dot_general | solution.py:141
  833.2 12.7 %copy.291 = bf16[1152,4096]{1,0:T(8,128)(2,1)} copy(bf16[1152,4096]{0,1:T(8,128)(2,1)} %bitcast.686) | data formatting | bytes 18874368 | tf_op jit(solution)/shard_map/dot_general | solution.py:141
  846.0 5.3 fusion.68
  851.3 5.3 fusion.67
  856.6 2.6 fusion.66
  860.6 3.2 copy.295
  863.8 256.6 %all-reduce.4.cloned.1.call-done = f32[27,128,128]{2,1,0:T(8,128)} async-done(((f32[27,128,128]{2,1,0:T(8,128)}), f32[27,128,128]{2,1,0:T(8,128)}) %all-reduce.4.cloned.1.call-update) | async-done | bytes 1769488 | tf_op jit(solution)/shard_map/psum | solution.py:196
  1120.4 2.5 multiply_reduce_fusion.1
  1123.6 2.9 broadcast_multiply_fusion
  (619 shorter events, 249.0 us)
Async XLA Ops:
  7.2 47.0 %copy-start = (f32[256,256]{1,0:T(8,128)S(1)}, f32[256,256]{1,0:T(8,128)}, u32[]{:S(2)}) copy-start(f32[256,256]{1,0:T(8,128)} %param.19) | copy-start | bytes 786436
  7.2 25.5 %copy-start.36 = (bf16[2,16,256,128]{3,2,1,0:T(8,128)(2,1)S(1)}, bf16[2,16,256,128]{3,2,1,0:T(8,128)(2,1)}, u32[]{:S(2)}) copy-start(bf16[2,16,256,128]{3,2,1,0:T(8,128)(2,1)} %param.11) | copy-start | bytes 6291460
  8.7 25.4 %all-to-all-start.1 = ((s32[2,16,16]{2,0,1:T(2,128)}), s32[2,16,16]{2,0,1:T(2,128)S(1)}, u32[]{:S(2)}, u32[]{:S(2)}) async-start(s32[2,16,16]{2,0,1:T(2,128)} %copy.216), calls=%async_computation.1 | async-start | bytes 32768 | tf_op jit(solution)/shard_map/all_to_all | solution.py:166
  26.7 311.9 %copy-start.59 = (s32[1024]{0:T(1024)}, s32[1024]{0:T(1024)S(1)}, u32[]{:S(2)}) copy-start(s32[1024]{0:T(1024)S(1)} %get-tuple-element.261) | copy-start | bytes 12292
  26.7 327.1 %copy-start.64 = (s32[1024]{0:T(1024)}, s32[1024]{0:T(1024)S(1)}, u32[]{:S(2)}) copy-start(s32[1024]{0:T(1024)S(1)} %get-tuple-element.262) | copy-start | bytes 12292
  26.7 312.5 %copy-start.61 = (s32[1024]{0:T(1024)}, s32[1024]{0:T(1024)S(1)}, u32[]{:S(2)}) copy-start(s32[1024]{0:T(1024)S(1)} %get-tuple-element.260) | copy-start | bytes 12292
  26.7 313.2 %copy-start.63 = (s32[1024]{0:T(1024)}, s32[1024]{0:T(1024)S(1)}, u32[]{:S(2)}) copy-start(s32[1024]{0:T(1024)S(1)} %get-tuple-element.259) | copy-start | bytes 12292
  26.8 314.4 %copy-start.57 = (s32[1024]{0:T(1024)}, s32[1024]{0:T(1024)S(1)}, u32[]{:S(2)}) copy-start(s32[1024]{0:T(1024)S(1)} %get-tuple-element.255) | copy-start | bytes 12292
  26.8 350.9 %copy-start.58 = (s32[1024]{0:T(1024)}, s32[1024]{0:T(1024)S(1)}, u32[]{:S(2)}) copy-start(s32[1024]{0:T(1024)S(1)} %get-tuple-element.256) | copy-start | bytes 12292
  26.8 315.1 %copy-start.56 = (s32[1024]{0:T(1024)}, s32[1024]{0:T(1024)S(1)}, u32[]{:S(2)}) copy-start(s32[1024]{0:T(1024)S(1)} %get-tuple-element.254) | copy-start | bytes 12292
  26.8 315.7 %copy-start.55 = (s32[1024]{0:T(1024)}, s32[1024]{0:T(1024)S(1)}, u32[]{:S(2)}) copy-start(s32[1024]{0:T(1024)S(1)} %get-tuple-element.253) | copy-start | bytes 12292
  26.8 347.6 %copy-start.60 = (s32[1024]{0:T(1024)}, s32[1024]{0:T(1024)S(1)}, u32[]{:S(2)}) copy-start(s32[1024]{0:T(1024)S(1)} %get-tuple-element.257) | copy-start | bytes 12292
  26.9 349.2 %copy-start.62 = (s32[1024]{0:T(1024)}, s32[1024]{0:T(1024)S(1)}, u32[]{:S(2)}) copy-start(s32[1024]{0:T(1024)S(1)} %get-tuple-element.258) | copy-start | bytes 12292
  26.9 317.0 %copy-start.70 = (s32[1024]{0:T(1024)}, s32[1024]{0:T(1024)S(1)}, u32[]{:S(2)}) copy-start(s32[1024]{0:T(1024)S(1)} %get-tuple-element.278) | copy-start | bytes 12292
  26.9 317.6 %copy-start.71 = (s32[1024]{0:T(1024)}, s32[1024]{0:T(1024)S(1)}, u32[]{:S(2)}) copy-start(s32[1024]{0:T(1024)S(1)} %get-tuple-element.277) | copy-start | bytes 12292
  26.9 319.5 %copy-start.67 = (s32[1024]{0:T(1024)}, s32[1024]{0:T(1024)S(1)}, u32[]{:S(2)}) copy-start(s32[1024]{0:T(1024)S(1)} %get-tuple-element.272) | copy-start | bytes 12292
  26.9 320.2 %copy-start.69 = (s32[1024]{0:T(1024)}, s32[1024]{0:T(1024)S(1)}, u32[]{:S(2)}) copy-start(s32[1024]{0:T(1024)S(1)} %get-tuple-element.271) | copy-start | bytes 12292
  27.6 320.2 %copy-start.68 = (s32[1024]{0:T(1024)}, s32[1024]{0:T(1024)S(1)}, u32[]{:S(2)}) copy-start(s32[1024]{0:T(1024)S(1)} %get-tuple-element.273) | copy-start | bytes 12292
  28.8 320.4 %copy-start.65 = (s32[1024]{0:T(1024)}, s32[1024]{0:T(1024)S(1)}, u32[]{:S(2)}) copy-start(s32[1024]{0:T(1024)S(1)} %get-tuple-element.270) | copy-start | bytes 12292
  28.8 321.1 %copy-start.66 = (s32[1024]{0:T(1024)}, s32[1024]{0:T(1024)S(1)}, u32[]{:S(2)}) copy-start(s32[1024]{0:T(1024)S(1)} %get-tuple-element.269) | copy-start | bytes 12292
  34.1 56.3 %all-to-all-start.3 = ((bf16[2,16,256,128]{3,2,0,1:T(8,128)(2,1)}), bf16[2,16,256,128]{3,2,0,1:T(8,128)(2,1)}, u32[]{:S(2)}, u32[]{:S(2)}) async-start(bf16[2,16,256,128]{3,2,0,1:T(8,128)(2,1)} %copy.269), calls=%async_computation.3 | async-start | bytes 4194304 | tf_op jit(solution)/shard_map/all_to_all | solution.py:165
  42.0 311.0 %copy-start.82 = (pred[16]{0:T(512)(128)(4,1)}, pred[16]{0:T(512)(128)(4,1)S(1)}, u32[]{:S(2)}) copy-start(pred[16]{0:T(512)(128)(4,1)S(1)} %get-tuple-element.290) | copy-start | bytes 52
  42.6 333.4 %copy-start.80 = (pred[16]{0:T(512)(128)(4,1)}, pred[16]{0:T(512)(128)(4,1)S(1)}, u32[]{:S(2)}) copy-start(pred[16]{0:T(512)(128)(4,1)S(1)} %get-tuple-element.285) | copy-start | bytes 52
  42.6 335.0 %copy-start.81 = (pred[16]{0:T(512)(128)(4,1)}, pred[16]{0:T(512)(128)(4,1)S(1)}, u32[]{:S(2)}) copy-start(pred[16]{0:T(512)(128)(4,1)S(1)} %get-tuple-element.287) | copy-start | bytes 52
  42.6 336.6 %copy-start.79 = (pred[16]{0:T(512)(128)(4,1)}, pred[16]{0:T(512)(128)(4,1)S(1)}, u32[]{:S(2)}) copy-start(pred[16]{0:T(512)(128)(4,1)S(1)} %get-tuple-element.286) | copy-start | bytes 52
  43.8 314.5 %copy-start.52 = (pred[16]{0:T(512)(128)(4,1)}, pred[16]{0:T(512)(128)(4,1)S(1)}, u32[]{:S(2)}) copy-start(pred[16]{0:T(512)(128)(4,1)S(1)} %get-tuple-element.237) | copy-start | bytes 52
  43.8 318.1 %copy-start.54 = (pred[16]{0:T(512)(128)(4,1)}, pred[16]{0:T(512)(128)(4,1)S(1)}, u32[]{:S(2)}) copy-start(pred[16]{0:T(512)(128)(4,1)S(1)} %get-tuple-element.238) | copy-start | bytes 52
  43.8 322.6 %copy-start.53 = (pred[16]{0:T(512)(128)(4,1)}, pred[16]{0:T(512)(128)(4,1)S(1)}, u32[]{:S(2)}) copy-start(pred[16]{0:T(512)(128)(4,1)S(1)} %get-tuple-element.236) | copy-start | bytes 52
  51.4 46.4 %copy-start.110 = (bf16[1152,128]{0,1:T(8,128)(2,1)}, bf16[1152,128]{0,1:T(8,128)(2,1)S(1)}, u32[]{:S(2)}) copy-start(bf16[1152,128]{0,1:T(8,128)(2,1)S(1)} %get-tuple-element.133) | copy-start | bytes 884740
  90.4 89.2 %all-to-all-start = ((bf16[2,16,256,128]{3,2,0,1:T(8,128)(2,1)}), bf16[2,16,256,128]{3,2,0,1:T(8,128)(2,1)}, u32[]{:S(2)}, u32[]{:S(2)}) async-start(bf16[2,16,256,128]{3,2,0,1:T(8,128)(2,1)} %copy.213), calls=%async_computation | async-start | bytes 4194304 | tf_op jit(solution)/shard_map/all_to_all | solution.py:164
  95.4 69.0 %copy-start.116 = (s32[16]{0:T(128)S(1)}, s32[16]{0:T(128)}, u32[]{:S(2)}) copy-start(s32[16]{0:T(128)} %get-tuple-element.240) | copy-start | bytes 196
  95.4 69.0 %copy-start.117 = (s32[16]{0:T(128)S(1)}, s32[16]{0:T(128)}, u32[]{:S(2)}) copy-start(s32[16]{0:T(128)} %get-tuple-element.241) | copy-start | bytes 196
  97.7 81.9 %copy-start.20 = (bf16[16,256,128]{2,1,0:T(8,128)(2,1)}, bf16[16,256,128]{2,1,0:T(8,128)(2,1)S(1)}, u32[]{:S(2)}) copy-start(bf16[16,256,128]{2,1,0:T(8,128)(2,1)S(1)} %gather_fusion.29) | copy-start | bytes 3145732
  98.5 206.0 %copy-start.18 = (bf16[16,1,256,128]{3,2,0,1:T(8,128)(2,1)}, bf16[16,1,256,128]{3,2,0,1:T(8,128)(2,1)S(1)}, u32[]{:S(2)}) copy-start(bf16[16,1,256,128]{3,2,0,1:T(8,128)(2,1)S(1)} %bitcast_multiply_fusion) | copy-start | bytes 3145732
  98.5 53.9 %collective-permute-start.4 = (bf16[16,1,256,128]{3,2,0,1:T(8,128)(2,1)S(1)}, bf16[16,1,256,128]{3,2,0,1:T(8,128)(2,1)S(1)}, u32[]{:S(2)}, u32[]{:S(2)}) collective-permute-start(bf16[16,1,256,128]{3,2,0,1:T(8,128)(2,1)S(1)} %bitcast_multiply_fusion), channel_id=1, source_target_pairs={{15,0},{0,1},{1,2},{2,3},{3,4},{4,5},{5,6},{6,7},{7,8},{8,9},{9,10... | collective-permute-start | bytes 3145736 | tf_op jit(solution)/shard_map/ppermute | solution.py:17
  100.1 54.4 %collective-permute-start.5 = (bf16[16,1,256,128]{3,2,0,1:T(8,128)(2,1)S(1)}, bf16[16,1,256,128]{3,2,0,1:T(8,128)(2,1)S(1)}, u32[]{:S(2)}, u32[]{:S(2)}) collective-permute-start(bf16[16,1,256,128]{3,2,0,1:T(8,128)(2,1)S(1)} %bitcast_multiply_fusion), channel_id=1, source_target_pairs={{1,0},{2,1},{3,2},{4,3},{5,4},{6,5},{7,6},{8,7},{9,8},{10,9},{11,1... | collective-permute-start | bytes 3145736 | tf_op jit(solution)/shard_map/ppermute | solution.py:17
  100.8 249.8 %copy-start.75 = (s32[1024]{0:T(1024)}, s32[1024]{0:T(1024)S(1)}, u32[]{:S(2)}) copy-start(s32[1024]{0:T(1024)S(1)} %get-tuple-element.268) | copy-start | bytes 12292
  100.8 261.2 %copy-start.74 = (s32[1024]{0:T(1024)}, s32[1024]{0:T(1024)S(1)}, u32[]{:S(2)}) copy-start(s32[1024]{0:T(1024)S(1)} %get-tuple-element.267) | copy-start | bytes 12292
  101.5 250.9 %copy-start.72 = (s32[1024]{0:T(1024)}, s32[1024]{0:T(1024)S(1)}, u32[]{:S(2)}) copy-start(s32[1024]{0:T(1024)S(1)} %get-tuple-element.264) | copy-start | bytes 12292
  101.5 251.6 %copy-start.73 = (s32[1024]{0:T(1024)}, s32[1024]{0:T(1024)S(1)}, u32[]{:S(2)}) copy-start(s32[1024]{0:T(1024)S(1)} %get-tuple-element.263) | copy-start | bytes 12292
  157.5 146.9 %collective-permute-start.6 = (bf16[16,3,256,128]{3,2,0,1:T(8,128)(2,1)}, bf16[16,3,256,128]{3,2,0,1:T(8,128)(2,1)}, u32[]{:S(2)}, u32[]{:S(2)}) collective-permute-start(bf16[16,3,256,128]{3,2,0,1:T(8,128)(2,1)} %pad_maximum_fusion.5), channel_id=1, source_target_pairs={{0,16},{16,32},{32,48},{48,64},{64,80},{80,96},{96,112},{112,128},... | collective-permute-start | bytes 9437192 | tf_op jit(solution)/shard_map/ppermute | solution.py:28
  162.4 142.1 %collective-permute-start.7 = (bf16[16,3,256,128]{3,2,0,1:T(8,128)(2,1)}, bf16[16,3,256,128]{3,2,0,1:T(8,128)(2,1)}, u32[]{:S(2)}, u32[]{:S(2)}) collective-permute-start(bf16[16,3,256,128]{3,2,0,1:T(8,128)(2,1)} %pad_maximum_fusion.5), channel_id=1, source_target_pairs={{16,0},{32,16},{48,32},{64,48},{80,64},{96,80},{112,96},{128,112},... | collective-permute-start | bytes 9437192 | tf_op jit(solution)/shard_map/ppermute | solution.py:30
  163.7 181.5 %copy-start.78 = (s32[1024]{0:T(1024)}, s32[1024]{0:T(1024)S(1)}, u32[]{:S(2)}) copy-start(s32[1024]{0:T(1024)S(1)} %pad_clamp_fusion.26) | copy-start | bytes 12292
  164.1 250.7 %copy-start.47 = (pred[4096]{0:T(1024)(128)(4,1)}, pred[4096]{0:T(1024)(128)(4,1)S(1)}, u32[]{:S(2)}) copy-start(pred[4096]{0:T(1024)(128)(4,1)S(1)} %broadcast_in_dim.361) | copy-start | bytes 12292
  164.3 255.3 %copy-start.49 = (pred[4096]{0:T(1024)(128)(4,1)}, pred[4096]{0:T(1024)(128)(4,1)S(1)}, u32[]{:S(2)}) copy-start(pred[4096]{0:T(1024)(128)(4,1)S(1)} %broadcast_in_dim.364) | copy-start | bytes 12292
  164.4 191.2 %copy-start.76 = (s32[1024]{0:T(1024)}, s32[1024]{0:T(1024)S(1)}, u32[]{:S(2)}) copy-start(s32[1024]{0:T(1024)S(1)} %get-tuple-element.265) | copy-start | bytes 12292
  164.4 194.0 %copy-start.77 = (s32[1024]{0:T(1024)}, s32[1024]{0:T(1024)S(1)}, u32[]{:S(2)}) copy-start(s32[1024]{0:T(1024)S(1)} %get-tuple-element.266) | copy-start | bytes 12292
  182.0 129.8 %copy-start.5 = (bf16[16,256,128]{2,1,0:T(8,128)(2,1)}, bf16[16,256,128]{2,1,0:T(8,128)(2,1)S(1)}, u32[]{:S(2)}) copy-start(bf16[16,256,128]{2,1,0:T(8,128)(2,1)S(1)} %gather_fusion) | copy-start | bytes 3145732
  331.6 16.7 %copy-start.101 = (pred[16]{0:T(512)(128)(4,1)S(1)}, pred[16]{0:T(512)(128)(4,1)}, u32[]{:S(2)}) copy-start(pred[16]{0:T(512)(128)(4,1)} %get-tuple-element.224) | copy-start | bytes 52
  331.7 18.1 %copy-start.85 = (pred[16]{0:T(512)(128)(4,1)S(1)}, pred[16]{0:T(512)(128)(4,1)}, u32[]{:S(2)}) copy-start(pred[16]{0:T(512)(128)(4,1)} %get-tuple-element.293) | copy-start | bytes 52
  331.7 18.8 %copy-start.86 = (pred[16]{0:T(512)(128)(4,1)S(1)}, pred[16]{0:T(512)(128)(4,1)}, u32[]{:S(2)}) copy-start(pred[16]{0:T(512)(128)(4,1)} %get-tuple-element.291) | copy-start | bytes 52
  331.7 19.5 %copy-start.88 = (pred[16]{0:T(512)(128)(4,1)S(1)}, pred[16]{0:T(512)(128)(4,1)}, u32[]{:S(2)}) copy-start(pred[16]{0:T(512)(128)(4,1)} %get-tuple-element.292) | copy-start | bytes 52
  371.8 16.2 %copy-start.43 = (bf16[16,3,1,1,128]{4,3,0,2,1:T(2,128)(2,1)S(1)}, bf16[16,3,1,1,128]{4,3,0,2,1:T(2,128)(2,1)}, u32[]{:S(2)}) copy-start(bf16[16,3,1,1,128]{4,3,0,2,1:T(2,128)(2,1)} %copy.282) | copy-start | bytes 36868
  371.8 16.2 %copy-start.45 = (bf16[16,3,1,1,128]{4,3,0,2,1:T(2,128)(2,1)S(1)}, bf16[16,3,1,1,128]{4,3,0,2,1:T(2,128)(2,1)}, u32[]{:S(2)}) copy-start(bf16[16,3,1,1,128]{4,3,0,2,1:T(2,128)(2,1)} %copy.283) | copy-start | bytes 36868
  430.8 78.4 %copy-start.21 = (bf16[16,256,128]{2,1,0:T(8,128)(2,1)S(1)}, bf16[16,256,128]{2,1,0:T(8,128)(2,1)}, u32[]{:S(2)}) copy-start(bf16[16,256,128]{2,1,0:T(8,128)(2,1)} %copy-done.20) | copy-start | bytes 3145732
  513.4 36.8 %copy-start.108 = (s32[16]{0:T(128)S(1)}, s32[16]{0:T(128)}, u32[]{:S(2)}) copy-start(s32[16]{0:T(128)} %copy-done.107) | copy-start | bytes 196
  513.4 13.9 %collective-permute-start = (bf16[16,1,256,128]{3,2,0,1:T(8,128)(2,1)S(1)}, bf16[16,1,256,128]{3,2,0,1:T(8,128)(2,1)S(1)}, u32[]{:S(2)}, u32[]{:S(2)}) collective-permute-start(bf16[16,1,256,128]{3,2,0,1:T(8,128)(2,1)S(1)} %get-tuple-element.132), channel_id=1, source_target_pairs={{15,0},{0,1},{1,2},{2,3},{3,4},{4,5},{5,6},{6,7},{7,8},{8,9},{9,10... | collective-permute-start | bytes 3145736 | tf_op jit(solution)/shard_map/ppermute | solution.py:17
  515.5 14.2 %collective-permute-start.1 = (bf16[16,1,256,128]{3,2,0,1:T(8,128)(2,1)S(1)}, bf16[16,1,256,128]{3,2,0,1:T(8,128)(2,1)S(1)}, u32[]{:S(2)}, u32[]{:S(2)}) collective-permute-start(bf16[16,1,256,128]{3,2,0,1:T(8,128)(2,1)S(1)} %get-tuple-element.132), channel_id=1, source_target_pairs={{1,0},{2,1},{3,2},{4,3},{5,4},{6,5},{7,6},{8,7},{9,8},{10,9},{11,1... | collective-permute-start | bytes 3145736 | tf_op jit(solution)/shard_map/ppermute | solution.py:17
  531.7 70.8 %collective-permute-start.2 = (bf16[16,3,256,128]{3,2,0,1:T(8,128)(2,1)}, bf16[16,3,256,128]{3,2,0,1:T(8,128)(2,1)}, u32[]{:S(2)}, u32[]{:S(2)}) collective-permute-start(bf16[16,3,256,128]{3,2,0,1:T(8,128)(2,1)} %pad_maximum_fusion.4), channel_id=1, source_target_pairs={{0,16},{16,32},{32,48},{48,64},{64,80},{80,96},{96,112},{112,128},... | collective-permute-start | bytes 9437192 | tf_op jit(solution)/shard_map/ppermute | solution.py:28
  536.0 72.0 %collective-permute-start.3 = (bf16[16,3,256,128]{3,2,0,1:T(8,128)(2,1)}, bf16[16,3,256,128]{3,2,0,1:T(8,128)(2,1)}, u32[]{:S(2)}, u32[]{:S(2)}) collective-permute-start(bf16[16,3,256,128]{3,2,0,1:T(8,128)(2,1)} %pad_maximum_fusion.4), channel_id=1, source_target_pairs={{16,0},{32,16},{48,32},{64,48},{80,64},{96,80},{112,96},{128,112},... | collective-permute-start | bytes 9437192 | tf_op jit(solution)/shard_map/ppermute | solution.py:30
  553.6 249.1 %all-to-all-start.4 = ((bf16[32,1,256,128]{3,2,1,0:T(8,128)(2,1)}), bf16[32,1,256,128]{3,2,1,0:T(8,128)(2,1)}, u32[]{:S(2)}, u32[]{:S(2)}) async-start(bf16[32,1,256,128]{3,2,1,0:T(8,128)(2,1)} %bitcast.307), calls=%async_computation.4 | async-start | bytes 4194304 | tf_op jit(solution)/shard_map/all_to_all | solution.py:223
  802.7 323.8 %all-to-all-start.2 = ((bf16[32,1,256,128]{3,2,1,0:T(8,128)(2,1)}), bf16[32,1,256,128]{3,2,1,0:T(8,128)(2,1)S(1)}, u32[]{:S(2)}, u32[]{:S(2)}) async-start(bf16[32,1,256,128]{3,2,1,0:T(8,128)(2,1)} %bitcast.184), calls=%async_computation.2 | async-start | bytes 4194304 | tf_op jit(solution)/shard_map/all_to_all | solution.py:222
  808.2 312.2 %all-reduce.4.cloned.1.call-start = ((), (), s32[]{:S(2)}) async-start(), calls=%async_computation.5 | async-start | bytes 3538944 | tf_op jit(solution)/shard_map/psum | solution.py:196
  860.6 267.4 %copy-start.1 = (f32[256,256]{1,0:T(8,128)S(1)}, f32[256,256]{1,0:T(8,128)}, u32[]{:S(2)}) copy-start(f32[256,256]{1,0:T(8,128)} %param.19) | copy-start | bytes 786436
  (77 other events, 488.2 us)
Sparse Core Ops, SparseCore 0:
  860.7 259.6 all-reduce.3
where the time goes:
time: 1150 us; the launch traced here: 1140 us
  waiting for transfers between devices  404 us (35%)
  local copies, waits for them, and re-layouts  315 us (27%)
  blocking collectives  192 us (17%)
  other arithmetic  120 us (10%)
  starting transfers between devices  48.6 us (4%)
  matrix products  36.1 us (3%)
  between operations  18.9 us (2%)
    psum x1, waiting for transfers between devices, local(): weight_total = lax.psum(local_grads, ('wide', 'narrow'))  257 us
    psum x1, blocking collectives, local(): lax.psum((first_sums, squares, jnp.sum(occupied).reshape(1)), ('wide', 'n...  119 us
    gather x54, local copies, waits for them, and re-layouts, pick_rows(): picked = source[jnp.clip(local_index, 0, source.shape[0] - 1)]  74.8 us
    unnamed x363, local copies, waits for them, and re-layouts  73.9 us
    psum x1, blocking collectives, local(): lax.psum((first_grad, second_grad), ('wide', 'narrow'))  72.7 us
    ppermute x4, waiting for transfers between devices, passed_along(): return lax.ppermute(block, axis, route)  62.6 us
    ppermute x2, waiting for transfers between devices, padded_2(): lax.ppermute(tail, axis, [(i, (i + 1) % count) for i in range(ends)])  43.7 us
    slice x14, local copies, waits for them, and re-layouts, neighbourhood(): low_part = pick_rows(rim_cells[:, :1], lower_ids, first_live)  39.8 us
  transfers between devices with their start and end apart: 14, of which 8 were waited for; matrix products, arithmetic and copies ran while one was open for 29% of the time, Pallas kernels for 0%

commit v1 on v0

v1 whole, which is shorter than its diff:
```python
import functools

import jax
import jax.numpy as jnp
from jax import lax
from jax.experimental import pallas as pl
from jax.experimental.pallas import tpu as pltpu
from jax.sharding import PartitionSpec as P

G = 32
norm_eps = 1e-05
step_eps = 1e-06
MIB = 1 << 20
f32 = jnp.float32
bf16 = jnp.bfloat16

SMEM = pl.BlockSpec(memory_space=pltpu.SMEM)
VMEM = pl.BlockSpec(memory_space=pltpu.VMEM)


def params(limit, semantics=None):
    return pltpu.CompilerParams(vmem_limit_bytes=limit * MIB, dimension_semantics=semantics)


def cost(flops, size):
    return pl.CostEstimate(flops=flops, bytes_accessed=size, transcendentals=0)


def film_terms(timestep, film_weight):
    half_width = film_weight.shape[0] // 2
    channels = film_weight.shape[1] // 2
    frequencies = jnp.exp(
        -jnp.log(10000.0) * jnp.arange(half_width).astype(jnp.float32) / half_width
    )
    angles = timestep.astype(jnp.float32)[0] * frequencies
    embedding = jax.nn.silu(jnp.concatenate([jnp.cos(angles), jnp.sin(angles)]))
    film_out = jnp.dot(embedding[None, :], film_weight, precision=lax.Precision.HIGHEST)[0]
    return (film_out[:channels], film_out[channels:])


def plane_mask(occ_ref, slot, z, edge, channels):
    bit = lax.broadcasted_iota(jnp.int32, (edge, channels), 0)
    rows = [
        jnp.bitwise_and(jnp.right_shift(jnp.full((edge, channels), occ_ref[slot, z, y], jnp.int32), bit), 1)
        for y in range(edge)
    ]
    return jnp.concatenate(rows, axis=0) != 0


def planes_mask(occ_ref, slot, z, count, edge, channels):
    return jnp.concatenate([plane_mask(occ_ref, slot, z + i, edge, channels) for i in range(count)], axis=0)


def x_row(rows, edge, channels):
    return lax.rem(lax.broadcasted_iota(jnp.int32, (rows, channels), 0), edge)


def pieces(value, count):
    found = []
    for _ in range(count):
        part = value.astype(bf16).astype(f32)
        found.append(part)
        value = value - part
    return found


def surface_kernel(edge, with_stats, fill, occ_ref, v_ref, out_ref, plane_s, edge_s, stat_s):
    channels = v_ref.shape[-1]
    last = edge - 1
    slot = pl.program_id(0)

    @pl.when(slot == 0)
    def _():
        stat_s[...] = jnp.zeros_like(stat_s)
        edge_s[...] = jnp.zeros_like(edge_s)

    def coded(z):
        mask = plane_mask(occ_ref, slot, z, edge, channels)
        values = v_ref[0, z].astype(f32)
        return (mask, values, jnp.where(mask, values, fill))

    def step(z, carry):
        mask, values, shown = coded(z)
        plane_s[...] = shown
        for side in range(2):
            row = side * last
            out_ref[z, 4 + 2 * slot + side] = shown[row * edge : (row + 1) * edge].astype(bf16)
            out_ref[z, 8 + 2 * slot + side] = plane_s[pl.ds(row, edge, stride=edge), :].astype(bf16)
        if not with_stats:
            return carry
        total, squares, count = carry
        masked = jnp.where(mask, values, 0.0)
        total = total + jnp.sum(masked, axis=0, keepdims=True)
        squares = squares + jnp.sum(masked * values, axis=0, keepdims=True)
        count = count + jnp.sum(mask.astype(f32), axis=0, keepdims=True)
        return (total, squares, count)

    zero = jnp.zeros((1, channels), f32)
    found = lax.fori_loop(0, edge, step, (zero, zero, zero) if with_stats else 0)
    if with_stats:
        for index in range(3):
            stat_s[index : index + 1, :] = stat_s[index : index + 1, :] + found[index]
    for z_side in range(2):
        _, _, shown = coded(z_side * last)
        for hub in range(edge):
            out_ref[hub, 2 * slot + z_side] = shown[hub * edge : (hub + 1) * edge].astype(bf16)
        for y_side in range(2):
            for hub in range(edge):
                first = y_side * last * edge + hub
                for place in range(2):

                    @pl.when(slot == place)
                    def _():
                        row = 4 * place + 2 * z_side + y_side
                        edge_s[hub, row : row + 1, :] = shown[first : first + 1]

    @pl.when(slot == 1)
    def _():
        if with_stats:
            parts = pieces(stat_s[0:1, :], 3) + pieces(stat_s[1:2, :], 3) + pieces(stat_s[2:3, :], 2)
            for hub in range(edge):
                for row, part in enumerate(parts):
                    edge_s[hub, 8 + row : 9 + row, :] = part
        for hub in range(edge):
            for tile in range(16 // edge):
                out_ref[hub, 12 + tile] = edge_s[hub, tile * edge : (tile + 1) * edge].astype(bf16)


def surface(occupancy, values, fill, with_stats):
    edge, cells, channels = values.shape[1:]
    tiles = 12 + 16 // edge
    return pl.pallas_call(
        functools.partial(surface_kernel, edge, with_stats, fill),
        grid=(2,),
        out_shape=jax.ShapeDtypeStruct((edge, tiles, edge, channels), bf16),
        in_specs=[SMEM, pl.BlockSpec((1, edge, cells, channels), lambda s: (s, 0, 0, 0))],
        out_specs=pl.BlockSpec((edge, tiles, edge, channels), lambda s: (0, 0, 0, 0)),
        scratch_shapes=[
            pltpu.VMEM((cells, channels), f32),
            pltpu.VMEM((edge, 16, channels), f32),
            pltpu.VMEM((8, channels), f32),
        ],
        compiler_params=params(24, ("arbitrary",)),
        cost_estimate=cost(0, 3 * MIB),
        name="surface",
    )(occupancy, values)


def trade_kernel(edge, live_ref, got_ref, left_ref, right_ref, stat_ref, ends_s):
    live_count = live_ref.shape[1]
    for k in range(live_count):
        slot = live_ref[0, k]
        owner, local = slot // 2, lax.rem(slot, 2)
        for side, out in ((0, left_ref), (1, right_ref)):
            out[k] = got_ref[owner, 8 + 2 * local + side]
            for z_side in range(2):
                tile = got_ref[owner, 2 * local + z_side].astype(f32)
                row = 2 * k + z_side
                x = side * (edge - 1)
                ends_s[side, row : row + 1, :] = tile[x : x + 1]
    for side, out in ((0, left_ref), (1, right_ref)):
        for tile in range(2 * live_count // edge):
            out[live_count + tile] = ends_s[side, tile * edge : (tile + 1) * edge].astype(bf16)
    rows = []
    for tile in range(8 // edge if edge < 16 else 0, 16 // edge):
        total = got_ref[0, 12 + tile].astype(f32)
        for source in range(1, edge):
            total = total + got_ref[source, 12 + tile].astype(f32)
        rows.append(total)
    rows = jnp.concatenate(rows, axis=0)
    if edge == 16:
        rows = rows[8:]
    stat_ref[...] = jnp.zeros_like(stat_ref)
    stat_ref[0:1, :] = rows[0:1] + rows[1:2] + rows[2:3]
    stat_ref[1:2, :] = rows[3:4] + rows[4:5] + rows[5:6]
    stat_ref[2:3, :] = rows[6:7] + rows[7:8]


def trade(live_slots, got):
    edge, channels = got.shape[2], got.shape[-1]
    live_count = live_slots.shape[1]
    tiles = live_count + 2 * live_count // edge
    payload = jax.ShapeDtypeStruct((tiles, edge, channels), bf16)
    return pl.pallas_call(
        functools.partial(trade_kernel, edge),
        out_shape=(payload, payload, jax.ShapeDtypeStruct((8, channels), f32)),
        in_specs=[SMEM, VMEM],
        out_specs=(VMEM, VMEM, VMEM),
        scratch_shapes=[pltpu.VMEM((2, 2 * live_count, channels), f32)],
        compiler_params=params(16),
        cost_estimate=cost(0, 2 * MIB),
        name="trade",
    )(live_slots, got)


def hub_kernel(edge, fill, place_ref, live_ref, near_ref, got_ref, lower_ref, upper_ref, out_ref, wide_s, rows_s):
    live_count = live_ref.shape[1]
    last = edge - 1
    hub, group = place_ref[0], place_ref[1]
    x_refs = (lower_ref, upper_ref)
    for side in range(2):
        wide_s[side] = x_refs[side][...].astype(f32)

    def entry(k, dz, dy, dx):
        number = near_ref[k, 9 * (dz + 1) + 3 * (dy + 1) + (dx + 1)]
        index = jnp.clip(number - (group + dx) * live_count, 0, live_count - 1)
        return (number >= 0, index)

    def own(k, dz, dy):
        there, index = entry(k, dz, dy, 0)
        slot = live_ref[0, index]
        return (there, slot // 2, lax.rem(slot, 2))

    def step(k, carry):
        slot = live_ref[0, k]
        owner, local = slot // 2, lax.rem(slot, 2)

        def put(tile, there, values):
            out_ref[owner, local, tile] = jnp.where(there, values, fill).astype(bf16)

        def put_row(row, there, values):
            rows_s[row : row + 1, :] = jnp.where(there, values, fill)

        for side in range(2):
            step_to = 2 * side - 1
            there, source, place = own(k, step_to, 0)
            put(side, there, got_ref[source, 2 * place + 1 - side].astype(f32))
            there, source, place = own(k, 0, step_to)
            put(2 + side, there, got_ref[source, 4 + 2 * place + 1 - side].astype(f32))
            there, index = entry(k, 0, 0, step_to)
            put(4 + side, there, wide_s[side, index])
        dz_corner = jnp.where(hub == last, -1, 1)
        for a in range(2):
            for b in range(2):
                there, source, place = own(k, 2 * a - 1, 2 * b - 1)
                row = 4 * place + 2 * (1 - a) + (1 - b)
                tile = got_ref[source, 12 + row // edge].astype(f32)
                picked = lax.broadcasted_iota(jnp.int32, tile.shape, 0) == lax.rem(row, edge)
                put_row(2 * a + b, there, jnp.sum(jnp.where(picked, tile, 0.0), axis=0, keepdims=True))
                there, index = entry(k, 2 * a - 1, 0, 2 * b - 1)
                row = 2 * index + (1 - a)
                tile = wide_s[b, live_count + row // edge]
                picked = lax.broadcasted_iota(jnp.int32, tile.shape, 0) == lax.rem(row, edge)
                put_row(4 + 2 * a + b, there, jnp.sum(jnp.where(picked, tile, 0.0), axis=0, keepdims=True))
                row = last if a == 0 else 0
                there, index = entry(k, 0, 2 * a - 1, 2 * b - 1)
                put_row(8 + 2 * a + b, there, wide_s[b, index, row : row + 1, :])
                there, index = entry(k, dz_corner, 2 * a - 1, 2 * b - 1)
                put_row(12 + 2 * a + b, there, wide_s[b, index, row : row + 1, :])
        for tile in range(16 // edge):
            out_ref[owner, local, 6 + tile] = rows_s[tile * edge : (tile + 1) * edge].astype(bf16)
        return carry

    lax.fori_loop(0, live_count, step, 0)


def hub_rows(place, live_slots, neighbours, got, lower, upper, fill):
    edge, channels = got.shape[2], got.shape[-1]
    return pl.pallas_call(
        functools.partial(hub_kernel, edge, fill),
        out_shape=jax.ShapeDtypeStruct((edge, 2, 6 + 16 // edge, edge, channels), bf16),
        in_specs=[SMEM, SMEM, SMEM, VMEM, VMEM, VMEM],
        out_specs=VMEM,
        scratch_shapes=[
            pltpu.VMEM((2,) + lower.shape, f32),
            pltpu.VMEM((16, channels), f32),
        ],
        compiler_params=params(16),
        cost_estimate=cost(0, 8 * MIB),
        name="hub_rows",
    )(place, live_slots, neighbours, got, lower, upper)


def exchange(values, axis):
    return lax.all_to_all(values, axis, split_axis=0, concat_axis=0, tiled=True)


def hub_stage(place, live_slots, neighbours, got, fill):
    to_left, to_right, stats = trade(live_slots, got)
    count = lax.axis_size("wide")
    lower = lax.ppermute(to_right, "wide", [(i, i + 1) for i in range(count - 1)])
    upper = lax.ppermute(to_left, "wide", [(i + 1, i) for i in range(count - 1)])
    return (hub_rows(place, live_slots, neighbours, got, lower, upper, fill), stats)


def coefficients(coef_ref):
    return [coef_ref[i : i + 1, :] for i in range(5)]


def set_halo(edge, rim_ref, pad_ref, pad_lead, shift_ref, shift_lead, xh_s, edge_s, change):
    last = edge - 1
    for hub in range(edge):
        tiles = [change(rim_ref[hub, 0, tile].astype(f32)) for tile in range(6 + 16 // edge)]
        for side in range(2):
            pad_ref[pad_lead + (side * (edge + 1), hub + 1)] = tiles[side].astype(bf16)
            pad_ref[pad_lead + (hub + 1, side * (edge + 1))] = tiles[2 + side].astype(bf16)
            xh_s[side, hub + 1, 8 : 8 + edge, :] = tiles[4 + side]

        def row(index):
            tile = tiles[6 + index // edge]
            return tile[index % edge : index % edge + 1]

        for a in range(2):
            for b in range(2):
                edge_s[2 * a + b, hub : hub + 1, :] = row(2 * a + b)
                xh_s[b, a * (edge + 1), 8 + hub : 9 + hub, :] = row(4 + 2 * a + b)
                y = 8 + edge if a else 7
                xh_s[b, hub + 1, y : y + 1, :] = row(8 + 2 * a + b)
                if hub == last:
                    xh_s[b, 0, y : y + 1, :] = row(12 + 2 * a + b)
                if hub == 0:
                    xh_s[b, edge + 1, y : y + 1, :] = row(12 + 2 * a + b)
    for a in range(2):
        for b in range(2):
            pad_ref[pad_lead + (a * (edge + 1), b * (edge + 1))] = edge_s[2 * a + b].astype(bf16)
    for side in range(2):
        for z in range(edge + 2):
            for y in range(3):
                shift_ref[shift_lead + (side, y, z)] = xh_s[side, z, 7 + y : 7 + y + edge, :].astype(bf16)


def hidden_plane(feats, mask, coef):
    mean, rstd, scale, shift = coef[:4]
    pre = (feats - mean) * rstd * scale + shift
    return jnp.where(mask, pre * jax.nn.sigmoid(pre), 0.0)


def weight_kernel(edge, occ_ref, live_ref, f_ref, g_ref, rim_ref, coef_ref, grad_ref, pad_ref, shift_ref,
                  hid_ref, acc_s, even_s, odd_s, xh_s, edge_s, plane_s, face_s):
    channels = f_ref.shape[-1]
    cells = edge * edge
    slot = pl.program_id(0)
    coef = coefficients(coef_ref)
    depth = min(4, edge // 2)
    chunks = edge // depth

    @pl.when(slot == 0)
    def _():
        acc_s[...] = jnp.zeros_like(acc_s)

    @pl.when(live_ref[slot] != 0)
    def _():
        set_halo(edge, rim_ref, pad_ref, (0,), shift_ref, (0,), xh_s, edge_s, lambda v: v)
        lane_x = lax.rem(lax.broadcasted_iota(jnp.int32, (channels, cells), 1), edge)

        def fill(z, carry):
            mask = plane_mask(occ_ref, slot, z, edge, channels)
            ups = jnp.where(mask, g_ref[0, z].astype(f32), 0.0).astype(bf16)
            pad_ref[0, z + 1, 1 : edge + 1] = ups.reshape(edge, edge, channels)
            return carry

        lax.fori_loop(0, edge, fill, 0)

        def prepare(chunk, flip_s):
            for part in range(depth):
                z = chunk * depth + part
                mask = plane_mask(occ_ref, slot, z, edge, channels)
                hidden = hidden_plane(f_ref[0, z].astype(f32), mask, coef).astype(bf16)
                hid_ref[0, z] = hidden
                hidden = hidden.astype(f32)
                plane_s[part] = hidden
                for side in range(2):
                    face_s[side, pl.ds(z * edge, edge), :] = plane_s[
                        part, pl.ds(side * (edge - 1), edge, stride=edge), :
                    ]
                flat = hidden.T
                before = jnp.where(lane_x == edge - 1, 0.0, pltpu.roll(flat, cells - 1, 1))
                after = jnp.where(lane_x == 0, 0.0, pltpu.roll(flat, 1, 1))
                columns = slice(part * cells, (part + 1) * cells)
                flip_s[0:channels, columns] = before.astype(bf16)
                flip_s[channels : 2 * channels, columns] = flat.astype(bf16)
                flip_s[2 * channels : 3 * channels, columns] = after.astype(bf16)

        def add(tap, px, values):
            pz, py = tap // 3, tap % 3
            offset = 9 * (2 - pz) + 3 * (2 - py) + (2 - px)
            acc_s[offset] = acc_s[offset] + values

        pairs = [(0, 1), (2, 3), (4, 5), (6, 7), (8,)]

        def multiply(chunk, flip_s):
            z0 = chunk * depth
            left = flip_s[...]
            for pair in pairs:
                right = [
                    pad_ref[0, pl.ds(z0 + tap // 3, depth), tap % 3 : tap % 3 + edge].reshape(
                        depth * cells, channels
                    )
                    for tap in pair
                ]
                right = right[0] if len(right) == 1 else jnp.concatenate(right, axis=1)
                found = jnp.dot(left, right, preferred_element_type=f32)
                for place, tap in enumerate(pair):
                    for px in range(3):
                        add(
                            tap,
                            px,
                            found[
                                px * channels : (px + 1) * channels,
                                place * channels : (place + 1) * channels,
                            ],
                        )

        prepare(0, even_s)

        def two(i, carry):
            prepare(2 * i + 1, odd_s)
            multiply(2 * i, even_s)
            prepare(jnp.minimum(2 * i + 2, chunks - 1), even_s)
            multiply(2 * i + 1, odd_s)
            return carry

        lax.fori_loop(0, chunks // 2, two, 0)
        for side in range(2):
            left = face_s[side].T.astype(bf16)
            for tap in range(9):
                right = shift_ref[0, side, tap % 3, tap // 3 : tap // 3 + edge].reshape(cells, channels)
                add(tap, 2 * side, jnp.dot(left, right, preferred_element_type=f32))

    @pl.when(slot == 1)
    def _():
        grad_ref[...] = acc_s[...]


def weight_grad(occupancy, live, features, cotangent, rim, coef):
    edge, channels = features.shape[1], features.shape[-1]
    cells = edge * edge
    wide = edge + 2
    whole = pl.BlockSpec((1, edge, cells, channels), lambda s: (s, 0, 0, 0))
    return pl.pallas_call(
        functools.partial(weight_kernel, edge),
        grid=(2,),
        out_shape=(
            jax.ShapeDtypeStruct((27, channels, channels), f32),
            jax.ShapeDtypeStruct((2, wide, wide, edge, channels), bf16),
            jax.ShapeDtypeStruct((2, 2, 3, wide, edge, channels), bf16),
            jax.ShapeDtypeStruct(features.shape, bf16),
        ),
        in_specs=[
            SMEM,
            SMEM,
            whole,
            whole,
            pl.BlockSpec((edge, 1) + rim.shape[2:], lambda s: (0, s, 0, 0, 0)),
            pl.BlockSpec((8, channels), lambda s: (0, 0)),
        ],
        out_specs=(
            pl.BlockSpec((27, channels, channels), lambda s: (0, 0, 0)),
            pl.BlockSpec((1, wide, wide, edge, channels), lambda s: (s, 0, 0, 0, 0)),
            pl.BlockSpec((1, 2, 3, wide, edge, channels), lambda s: (s, 0, 0, 0, 0, 0)),
            whole,
        ),
        scratch_shapes=[
            pltpu.VMEM((27, channels, channels), f32),
            pltpu.VMEM((3 * channels, min(4, edge // 2) * cells), bf16),
            pltpu.VMEM((3 * channels, min(4, edge // 2) * cells), bf16),
            pltpu.VMEM((2, wide, 8 * ((edge + 16) // 8), channels), f32),
            pltpu.VMEM((4, edge, channels), f32),
            pltpu.VMEM((min(4, edge // 2), cells, channels), f32),
            pltpu.VMEM((2, cells, channels), f32),
        ],
        compiler_params=params(48, ("arbitrary",)),
        cost_estimate=cost(20 * 10**9, 8 * MIB),
        name="weight_grad",
    )(occupancy, live, features, cotangent, rim, coef)


def side_rows(edge, shift_ref, shift_lead, w_ref, side_s):
    cells = edge * edge
    channels = w_ref.shape[0] // 9
    for side in range(2):
        rows = jnp.concatenate(
            [
                shift_ref[shift_lead + (side, tap % 3, slice(tap // 3, tap // 3 + edge))].reshape(cells, channels)
                for tap in range(9)
            ],
            axis=1,
        )
        first = 2 * side * channels
        side_s[side] = jnp.dot(rows, w_ref[:, first : first + channels], preferred_element_type=f32)


DEPTH = 2


def conv_planes(edge, z, pad_ref, pad_lead, w_ref, side_s, x_at):
    cells = edge * edge
    rows = DEPTH * cells
    channels = w_ref.shape[0] // 9
    found = jnp.dot(
        jnp.concatenate(
            [
                pad_ref[pad_lead + (pl.ds(z + tap // 3, DEPTH), slice(tap % 3, tap % 3 + edge))].reshape(
                    rows, channels
                )
                for tap in range(9)
            ],
            axis=1,
        ),
        w_ref[...],
        preferred_element_type=f32,
    )

    def beside(side):
        line = side_s[side, pl.ds(pl.multiple_of(z * edge, edge), DEPTH * edge), :]
        return jnp.broadcast_to(line[:, None, :], (DEPTH * edge, edge, channels)).reshape(rows, channels)

    before = jnp.where(x_at == 0, beside(0), pltpu.roll(found[:, :channels], 1, 0))
    after = jnp.where(x_at == edge - 1, beside(1), pltpu.roll(found[:, 2 * channels :], rows - 1, 0))
    return found[:, channels : 2 * channels] + before + after


def back_kernel(edge, occ_ref, live_ref, f_ref, pad_ref, shift_ref, w_ref, coef_ref, hat_ref, sum_ref, side_s):
    channels = f_ref.shape[-1]
    slot = pl.program_id(0)
    coef = coefficients(coef_ref)
    mean, rstd, scale, shift = coef[:4]

    @pl.when(slot == 0)
    def _():
        sum_ref[...] = jnp.zeros_like(sum_ref)

    @pl.when(live_ref[slot] != 0)
    def _():
        side_rows(edge, shift_ref, (0,), w_ref, side_s)
        rows = DEPTH * edge * edge
        x_at = x_row(rows, edge, channels)

        def planes(z, first, second):
            back = conv_planes(edge, z, pad_ref, (0,), w_ref, side_s, x_at)
            mask = planes_mask(occ_ref, slot, z, DEPTH, edge, channels)
            feats = f_ref[0, pl.ds(z, DEPTH)].reshape(rows, channels).astype(f32)
            normed = (feats - mean) * rstd
            pre = normed * scale + shift
            gate = jax.nn.sigmoid(pre)
            hat = jnp.where(mask, back * (gate * (1.0 + pre * (1.0 - gate))) * scale, 0.0)
            hat_ref[0, pl.ds(z, DEPTH)] = hat.reshape(DEPTH, edge * edge, channels)
            first = first + jnp.sum(hat, axis=0, keepdims=True)
            second = second + jnp.sum(hat * normed, axis=0, keepdims=True)
            return (first, second)

        def step(i, carry):
            for part in range(2):
                carry = planes((2 * i + part) * DEPTH, *carry)
            return carry

        zero = jnp.zeros((1, channels), f32)
        first, second = lax.fori_loop(0, edge // (2 * DEPTH), step, (zero, zero))
        sum_ref[0:1, :] = sum_ref[0:1, :] + first
        sum_ref[1:2, :] = sum_ref[1:2, :] + second


def back_conv(occupancy, live, features, padded, shifted, weight, coef):
    edge, channels = features.shape[1], features.shape[-1]
    cells = edge * edge
    whole = pl.BlockSpec((1, edge, cells, channels), lambda s: (s, 0, 0, 0))
    return pl.pallas_call(
        functools.partial(back_kernel, edge),
        grid=(2,),
        out_shape=(
            jax.ShapeDtypeStruct((2, edge, cells, channels), f32),
            jax.ShapeDtypeStruct((8, channels), f32),
        ),
        in_specs=[
            SMEM,
            SMEM,
            whole,
            pl.BlockSpec((1,) + padded.shape[1:], lambda s: (s, 0, 0, 0, 0)),
            pl.BlockSpec((1,) + shifted.shape[1:], lambda s: (s, 0, 0, 0, 0, 0)),
            pl.BlockSpec(weight.shape, lambda s: (0, 0)),
            pl.BlockSpec((8, channels), lambda s: (0, 0)),
        ],
        out_specs=(whole, pl.BlockSpec((8, channels), lambda s: (0, 0))),
        scratch_shapes=[pltpu.VMEM((2, cells, channels), f32)],
        compiler_params=params(48, ("arbitrary",)),
        cost_estimate=cost(20 * 10**9, 8 * MIB),
        name="back_conv",
    )(occupancy, live, features, padded, shifted, weight, coef)


def forward_kernel(edge, slot, occ_ref, live_ref, f_ref, hid_ref, rim_ref, w_ref, coef_ref, bias_ref, *refs):
    out_ref, pad_s, shift_s, xh_s, edge_s, side_s = refs[-6:]
    channels = f_ref.shape[-1]
    coef = coefficients(coef_ref)

    @pl.when(live_ref[slot] == 0)
    def _():
        out_ref[...] = f_ref[...]

    @pl.when(live_ref[slot] != 0)
    def _():
        def activate(coded):
            return hidden_plane(coded, coded < jnp.inf, coef)

        set_halo(edge, rim_ref, pad_s, (), shift_s, (), xh_s, edge_s, activate)
        for z in range(edge):
            pad_s[z + 1, 1 : edge + 1] = hid_ref[0, z].reshape(edge, edge, channels)
        side_rows(edge, shift_s, (), w_ref, side_s)
        rows = DEPTH * edge * edge
        x_at = x_row(rows, edge, channels)

        def step(i, carry):
            for part in range(2):
                z = (2 * i + part) * DEPTH
                conv = conv_planes(edge, z, pad_s, (), w_ref, side_s, x_at)
                mask = planes_mask(occ_ref, slot, z, DEPTH, edge, channels)
                feats = f_ref[0, pl.ds(z, DEPTH)].reshape(rows, channels).astype(f32)
                mixed = (feats + jnp.where(mask, conv + bias_ref[...], 0.0)).astype(bf16)
                out_ref[0, pl.ds(z, DEPTH)] = mixed.reshape(DEPTH, edge * edge, channels)
            return carry

        lax.fori_loop(0, edge // (2 * DEPTH), step, 0)


def forward_conv(slot, occupancy, live, features, hidden, rim, weight, coef, bias, base=None):
    edge, channels = features.shape[1], features.shape[-1]
    cells = edge * edge
    wide = edge + 2
    whole = pl.BlockSpec((1, edge, cells, channels), lambda s: (slot, 0, 0, 0))
    extra = [] if base is None else [base]
    return pl.pallas_call(
        functools.partial(forward_kernel, edge, slot),
        grid=(1,),
        out_shape=jax.ShapeDtypeStruct(features.shape, bf16),
        in_specs=[
            SMEM,
            SMEM,
            whole,
            whole,
            pl.BlockSpec((edge, 1) + rim.shape[2:], lambda s: (0, slot, 0, 0, 0)),
            pl.BlockSpec(weight.shape, lambda s: (0, 0)),
            pl.BlockSpec((8, channels), lambda s: (0, 0)),
            pl.BlockSpec((1, channels), lambda s: (0, 0)),
        ]
        + [pl.BlockSpec(memory_space=pl.ANY)] * len(extra),
        out_specs=whole,
        scratch_shapes=[
            pltpu.VMEM((wide, wide, edge, channels), bf16),
            pltpu.VMEM((2, 3, wide, edge, channels), bf16),
            pltpu.VMEM((2, wide, 8 * ((edge + 16) // 8), channels), f32),
            pltpu.VMEM((4, edge, channels), f32),
            pltpu.VMEM((2, cells, channels), f32),
        ],
        input_output_aliases={8: 0} if extra else {},
        compiler_params=params(48, ("arbitrary",)),
        cost_estimate=cost(10 * 10**9, 4 * MIB),
        name="forward_conv",
    )(occupancy, live, features, hidden, rim, weight, coef, bias, *extra)


def finish_kernel(edge, occ_ref, live_ref, f_ref, g_ref, hat_ref, coef_ref, out_ref):
    channels = f_ref.shape[-1]
    slot = pl.program_id(0)
    mean, rstd = coef_ref[0:1, :], coef_ref[1:2, :]
    first, second = coef_ref[2:3, :], coef_ref[3:4, :]

    @pl.when(live_ref[slot] == 0)
    def _():
        out_ref[...] = g_ref[...]

    @pl.when(live_ref[slot] != 0)
    def _():
        def plane(z, carry):
            mask = plane_mask(occ_ref, slot, z, edge, channels)
            normed = (f_ref[0, z].astype(f32) - mean) * rstd
            change = rstd * (hat_ref[0, z] - first - normed * second)
            out_ref[0, z] = (g_ref[0, z].astype(f32) + jnp.where(mask, change, 0.0)).astype(bf16)
            return carry

        lax.fori_loop(0, edge, plane, 0)


def finish(occupancy, live, features, cotangent, hat, coef):
    edge, channels = features.shape[1], features.shape[-1]
    whole = pl.BlockSpec((1, edge, edge * edge, channels), lambda s: (s, 0, 0, 0))
    return pl.pallas_call(
        functools.partial(finish_kernel, edge),
        grid=(2,),
        out_shape=jax.ShapeDtypeStruct(features.shape, bf16),
        in_specs=[SMEM, SMEM, whole, whole, whole, pl.BlockSpec((8, channels), lambda s: (0, 0))],
        out_specs=whole,
        compiler_params=params(32, ("arbitrary",)),
        cost_estimate=cost(0, 12 * MIB),
        name="finish",
    )(occupancy, live, features, cotangent, hat, coef)


def wide_sum(values):
    count = lax.axis_size("wide")
    step = 1
    while step < count:
        values = values + lax.ppermute(values, "wide", [(i, i ^ step) for i in range(count)])
        step *= 2
    return values


def group_sums(rows, channels):
    width = channels // G
    which = jnp.arange(channels) // width
    same = (which[:, None] == which[None, :]).astype(f32)
    return jnp.dot(rows, same, precision=lax.Precision.HIGHEST)


def scale_kernel(parts_ref, out_ref):
    total = jnp.zeros((1, parts_ref.shape[-1]), f32)
    for part in range(parts_ref.shape[0]):
        values = parts_ref[part].astype(f32)
        total = total + jnp.sum(values * values, axis=0, keepdims=True)
    mean = jnp.sum(total, axis=1, keepdims=True) / out_ref.size
    factor = lax.rsqrt(mean + step_eps)
    for part in range(parts_ref.shape[0]):
        out_ref[part] = parts_ref[part].astype(f32) * factor


def reduce_weights(grads, sums, tie):
    shape = grads.shape
    wide, narrow = lax.axis_size("wide"), lax.axis_size("narrow")
    rows = shape[0] * shape[1] // wide
    mine = jnp.sum(exchange(grads.reshape(wide, rows, shape[2]), "wide"), axis=0)
    deep = -(-rows // (8 * narrow)) * 8
    mine = jnp.pad(mine, ((0, deep * narrow - rows), (0, 0))).reshape(narrow, deep, shape[2])
    sums = jnp.broadcast_to(sums[None], (narrow,) + sums.shape)
    mine = jnp.sum(exchange(jnp.concatenate([mine, sums], axis=1), "narrow"), axis=0)
    mine, sums = mine[:deep], mine[deep:]
    mine, sums, tie = lax.optimization_barrier((mine, sums, tie))
    mine = exchange(jnp.broadcast_to(mine.astype(bf16)[None], (narrow, deep, shape[2])), "narrow")
    mine = mine.reshape(narrow * deep, shape[2])[:rows]
    parts = exchange(jnp.broadcast_to(mine[None], (wide,) + mine.shape), "wide")
    step = pl.pallas_call(
        scale_kernel,
        out_shape=jax.ShapeDtypeStruct(parts.shape, f32),
        in_specs=[VMEM],
        out_specs=VMEM,
        compiler_params=params(16),
        cost_estimate=cost(0, 3 * MIB),
        name="scale",
    )(parts)
    return (step.reshape(shape), sums, tie)


def local(
    features,
    out_cotangent,
    occupancy,
    live_slots,
    neighbours,
    timestep,
    norm_gain,
    norm_bias,
    film_weight,
    conv_weight,
    conv_bias,
):
    channels = features.shape[-1]
    group_width = channels // G
    hub = lax.axis_index("narrow").astype(jnp.int32)
    place = jnp.stack([hub, lax.axis_index("wide").astype(jnp.int32)])
    mine = 2 * hub + jnp.arange(2, dtype=jnp.int32)
    live = jnp.any(live_slots[0][None, :] == mine[:, None], axis=1).astype(jnp.int32)

    taps = conv_weight.reshape(9, 3, channels, channels)
    forward_weight = taps.transpose(0, 2, 1, 3).reshape(9 * channels, 3 * channels)
    flipped = conv_weight[::-1].reshape(9, 3, channels, channels)
    back_weight = flipped.transpose(0, 3, 1, 2).reshape(9 * channels, 3 * channels)
    film_scale, film_shift = film_terms(timestep, film_weight)
    scale = norm_gain * (1.0 + film_scale)
    shift = norm_bias * (1.0 + film_scale) + film_shift

    up_got = exchange(surface(occupancy, out_cotangent, 0.0, False), "narrow")
    feat_message = surface(occupancy, features, float("inf"), True)
    feat_message, up_got, forward_weight, back_weight, scale, shift = lax.optimization_barrier(
        (feat_message, up_got, forward_weight, back_weight, scale, shift)
    )
    feat_got = exchange(feat_message, "narrow")
    up_rows, _ = hub_stage(place, live_slots, neighbours, up_got, 0.0)
    up_rows, feat_got = lax.optimization_barrier((up_rows, feat_got))
    up_rim = exchange(up_rows, "narrow")
    feat_rows, stats = hub_stage(place, live_slots, neighbours, feat_got, float("inf"))
    stats = wide_sum(stats)
    feat_rows, up_rim = lax.optimization_barrier((feat_rows, up_rim))
    feat_rim = exchange(feat_rows, "narrow")

    voxel_count = stats[2, 0] * group_width
    sums = group_sums(stats[:2], channels)
    mean = sums[0] / voxel_count
    rstd = lax.rsqrt(sums[1] / voxel_count - mean * mean + norm_eps)
    blank = jnp.zeros((channels,), f32)
    coef = jnp.stack([mean, rstd, scale, shift, blank, blank, blank, blank])

    grads, padded, shifted, hidden = weight_grad(occupancy, live, features, out_cotangent, up_rim, coef)
    grads, feat_rim = lax.optimization_barrier((grads, feat_rim))
    hat, grad_sums = back_conv(occupancy, live, features, padded, shifted, back_weight, coef)
    forward = (occupancy, live, features, hidden, feat_rim, forward_weight, coef, conv_bias[None, :])
    mixed = forward_conv(0, *forward)
    weight_step, grad_sums, mixed = reduce_weights(grads, grad_sums, mixed)
    grad_sums, mixed = lax.optimization_barrier((wide_sum(grad_sums), mixed))
    grad_sums = group_sums(grad_sums[:2], channels) / voxel_count
    mixed = forward_conv(1, *forward, base=mixed)
    grad_coef = jnp.stack([mean, rstd, grad_sums[0], grad_sums[1], blank, blank, blank, blank])
    feature_grad = finish(occupancy, live, features, out_cotangent, hat, grad_coef)
    return (mixed, feature_grad, weight_step)


def solution(mesh):
    return jax.shard_map(
        local,
        mesh=mesh,
        in_specs=(
            P(("wide", "narrow"), None, None, None),
            P(("wide", "narrow"), None, None, None),
            P(("wide", "narrow"), None, None),
            P("wide", None),
            P("wide", None),
            P(),
            P(),
            P(),
            P(),
            P(),
            P(),
        ),
        out_specs=(
            P(("wide", "narrow"), None, None, None),
            P(("wide", "narrow"), None, None, None),
            P(),
        ),
        check_vma=False,
    )
```

time: 1150 us -> 239 us (0.21); the launches traced: 1140 us -> 238 us
  waiting for transfers between devices: 404 us -> 53.4 us
  local copies, waits for them, and re-layouts: 315 us -> 30.6 us
  blocking collectives: 192 us -> 0 us
  other arithmetic: 120 us -> 2.72 us
  Pallas kernels: 0 us -> 75.7 us
  matrix products: 36.1 us -> 0.58 us
  starting transfers between devices: 48.6 us -> 72.3 us
  between operations: 18.9 us -> 2.33 us
    psum x1 -> x0, waiting for transfers between devices: 257 us -> none  [local(): weight_total = lax.psum(local_grads, ('wide', 'narrow'))]
    psum x2 -> x0, blocking collectives: 192 us -> none  [the longest x1 119 us: local(): lax.psum((first_sums, squares, jnp.sum(occupied).reshape(1)), ('wide', 'n...]
    ppermute x8 -> x12, waiting for transfers between devices: 112 us -> 19.2 us  [the longest x8 12.4 us: wide_sum(): lax.ppermute(values, 'wide', [(i, i ^ step) for i in range(count)])]
    gather x57 -> x0, local copies, waits for them, and re-layouts: 80 us -> none  [the longest x54 74.8 us: pick_rows(): picked = source[jnp.clip(local_index, 0, source.shape[0] - 1)]]
    pallas_call x0 -> x12, Pallas kernels: none -> 75.7 us  [the longest x1 17.7 us: back_conv(): pl.pallas_call(functools.partial(back_kernel, edge), grid=(2,), out_shape...]
    slice x32 -> x4, local copies, waits for them, and re-layouts: 73.3 us -> 0.52 us  [the longest x1 0.51 us: local(): voxel_count = stats[2, 0] * group_width]
    unnamed x363 -> x58, local copies, waits for them, and re-layouts: 73.9 us -> 21.3 us
    concatenate x27 -> x1, other arithmetic: 49.9 us -> 0.69 us  [reduce_weights(): jnp.concatenate([mine, sums], axis=1)]
  transfers between devices with their start and end apart: 14 -> 20, of which waited for: 8 -> 14; matrix products, arithmetic and copies ran while one was open for 29% -> 4% of each run, Pallas kernels for 0% -> 30%
where the time goes in v1:
time: 239 us; the launch traced here: 238 us
  Pallas kernels  75.7 us (32%)
  starting transfers between devices  72.3 us (30%)
  waiting for transfers between devices  53.4 us (22%)
  local copies, waits for them, and re-layouts  30.6 us (13%)
  other arithmetic  2.72 us (1%)
    all_to_all x8, starting transfers between devices, exchange(): return lax.all_to_all(values, axis, split_axis=0, concat_axis=0, tiled=True)  54.1 us
    all_to_all x8, waiting for transfers between devices, exchange(): return lax.all_to_all(values, axis, split_axis=0, concat_axis=0, tiled=True)  34.2 us
    unnamed x58, local copies, waits for them, and re-layouts  21.3 us
    pallas_call x1, Pallas kernels, back_conv(): pl.pallas_call(functools.partial(back_kernel, edge), grid=(2,), out_shape...  17.7 us
    pallas_call x2, Pallas kernels, forward_conv(): pl.pallas_call(functools.partial(forward_kernel, edge, slot), grid=(1,),...  17.6 us
    pallas_call x1, Pallas kernels, weight_grad(): pl.pallas_call(functools.partial(weight_kernel, edge), grid=(2,), out_sha...  15.5 us
    ppermute x8, waiting for transfers between devices, wide_sum(): lax.ppermute(values, 'wide', [(i, i ^ step) for i in range(count)])  12.4 us
    ppermute x8, starting transfers between devices, wide_sum(): lax.ppermute(values, 'wide', [(i, i ^ step) for i in range(count)])  9.16 us
  transfers between devices with their start and end apart: 20, of which 14 were waited for; matrix products, arithmetic and copies ran while one was open for 4% of the time, Pallas kernels for 30%

profile of v1, /device:TPU:1, one launch (start us, length us, event | category | flops | bytes accessed | tf_op | source)
XLA Modules:
  0.0 237.7 jit_solution(15410181504172054772)
XLA Ops:
  0.7 1.6 copy-done.1
  2.3 0.7 copy-done.16
  3.0 3.0 %surface.3 = bf16[16,13,16,128]{3,2,1,0:T(8,128)(2,1)S(1)} custom-call(s32[2,16,16]{2,1,0:T(8,128)S(1)} %copy-done.16, bf16[2,16,256,128]{3,2,1,0:T(8,128)(2,1)S(1)} %copy-done.1), custom_call_target="tpu_custom_call" | custom-call | bytes 3145728 | tf_op jit(solution)/shard_map/surface/pallas_call | solution.py:132
  6.0 0.9 copy-done.9
  6.9 10.0 %all-to-all-start = ((bf16[16,13,16,128]{3,2,1,0:T(8,128)(2,1)}), bf16[16,13,16,128]{3,2,1,0:T(8,128)(2,1)S(1)}, u32[]{:S(2)}, u32[]{:S(2)}) async-start(bf16[16,13,16,128]{3,2,1,0:T(8,128)(2,1)} %copy-done.9), calls=%async_computation | async-start | bytes 1703936 | tf_op jit(solution)/shard_map/all_to_all | solution.py:275
  16.9 5.6 %surface.2 = bf16[16,13,16,128]{3,2,1,0:T(8,128)(2,1)} custom-call(s32[2,16,16]{2,1,0:T(8,128)S(1)} %copy-done.17, bf16[2,16,256,128]{3,2,1,0:T(8,128)(2,1)S(1)} %copy-done.3), custom_call_target="tpu_custom_call" | custom-call | bytes 3145728 | tf_op jit(solution)/shard_map/surface/pallas_call | solution.py:132
  22.5 2.3 rev.3
  24.8 2.5 %copy.20 = bf16[9,3,128,128]{2,1,3,0:T(4,128)(2,1)S(1)} copy(bf16[9,3,128,128]{3,2,1,0:T(8,128)(2,1)} %bitcast.35) | data formatting | bytes 1769472 | tf_op jit(solution)/shard_map/reshape | solution.py:763
  27.3 0.8 copy.19
  29.0 1.6 copy_bitcast_fusion
  30.7 10.2 %all-to-all-done.got_ref = bf16[16,13,16,128]{3,2,1,0:T(8,128)(2,1)S(1)} async-done(((bf16[16,13,16,128]{3,2,1,0:T(8,128)(2,1)}), bf16[16,13,16,128]{3,2,1,0:T(8,128)(2,1)S(1)}, u32[]{:S(2)}, u32[]{:S(2)}) %all-to-all-start) | async-done | bytes 852000 | tf_op jit(solution)/shard_map/all_to_all | solution.py:275
  40.9 3.5 %all-to-all-start.1 = ((bf16[16,13,16,128]{3,2,1,0:T(8,128)(2,1)}), bf16[16,13,16,128]{3,2,1,0:T(8,128)(2,1)S(1)}, u32[]{:S(2)}, u32[]{:S(2)}) async-start(bf16[16,13,16,128]{3,2,1,0:T(8,128)(2,1)} %surface.2), calls=%async_computation.1 | async-start | bytes 1703936 | tf_op jit(solution)/shard_map/all_to_all | solution.py:275
  44.4 1.2 trade.2
  45.7 3.2 %collective-permute-start = (bf16[18,16,128]{2,1,0:T(8,128)(2,1)S(1)}, bf16[18,16,128]{2,1,0:T(8,128)(2,1)S(1)}, u32[]{:S(2)}, u32[]{:S(2)}) collective-permute-start(bf16[18,16,128]{2,1,0:T(8,128)(2,1)S(1)} %get-tuple-element.32), channel_id=1, source_target_pairs={{0,16},{16,32},{32,48},{48,64},{64,80},{80,96},{96,112},{112,128},... | collective-permute-start | bytes 221192 | tf_op jit(solution)/shard_map/ppermute | solution.py:281
  48.9 1.3 collective-permute-start.1
  50.6 3.9 %collective-permute-done.1.upper_ref = bf16[18,16,128]{2,1,0:T(8,128)(2,1)S(1)} collective-permute-done((bf16[18,16,128]{2,1,0:T(8,128)(2,1)S(1)}, bf16[18,16,128]{2,1,0:T(8,128)(2,1)S(1)}, u32[]{:S(2)}, u32[]{:S(2)}) %collective-permute-start.1) | collective-permute-done | bytes 73760 | tf_op jit(solution)/shard_map/ppermute | solution.py:282
  54.5 4.4 %hub_rows.2 = bf16[16,2,7,16,128]{4,3,2,1,0:T(8,128)(2,1)} custom-call(s32[2]{0:T(128)S(1)} %pad_add_fusion.place_ref, s32[1,16]{1,0:T(1,128)S(1)} %copy-done.19, s32[16,27]{1,0:T(8,128)S(1)} %copy-done.18, bf16[16,13,16,128]{3,2,1,0:T(8,128)(2,1)S(1)} %all-to-all-done.got_ref, bf16[18,16,128]{2,1,0:T(8,128)(2,1)S(1)} %collective-permute-done.lower_ref, ...), custom_call_target="tpu_custom_call" | custom-call | bytes 8388608 | tf_op jit(solution)/shard_map/hub_rows/pallas_call | solution.py:259
  58.9 9.2 %all-to-all-done.1.got_ref = bf16[16,13,16,128]{3,2,1,0:T(8,128)(2,1)S(1)} async-done(((bf16[16,13,16,128]{3,2,1,0:T(8,128)(2,1)}), bf16[16,13,16,128]{3,2,1,0:T(8,128)(2,1)S(1)}, u32[]{:S(2)}, u32[]{:S(2)}) %all-to-all-start.1) | async-done | bytes 852000 | tf_op jit(solution)/shard_map/all_to_all | solution.py:275
  68.1 3.5 %all-to-all-start.2 = ((bf16[16,2,7,16,128]{4,3,2,1,0:T(8,128)(2,1)}), bf16[16,2,7,16,128]{4,3,2,1,0:T(8,128)(2,1)S(1)}, u32[]{:S(2)}, u32[]{:S(2)}) async-start(bf16[16,2,7,16,128]{4,3,2,1,0:T(8,128)(2,1)} %hub_rows.2), calls=%async_computation.2 | async-start | bytes 1835008 | tf_op jit(solution)/shard_map/all_to_all | solution.py:275
  71.7 0.6 trade.3
  72.3 1.4 collective-permute-start.4
  73.7 1.2 collective-permute-done.4
  74.9 2.9 %collective-permute-start.5 = (f32[8,128]{1,0:T(8,128)S(1)}, f32[8,128]{1,0:T(8,128)S(1)}, u32[]{:S(2)}, u32[]{:S(2)}) collective-permute-start(f32[8,128]{1,0:T(8,128)S(1)} %add.69), channel_id=1, source_target_pairs={{0,32},{16,48},{32,0},{48,16},{64,96},{80,112},{96,64},{112,80},{1... | collective-permute-start | bytes 12296 | tf_op jit(solution)/shard_map/ppermute | solution.py:692
  77.8 1.3 collective-permute-done.5
  79.1 1.2 collective-permute-start.6
  80.5 1.4 collective-permute-done.6
  81.8 2.7 %collective-permute-start.7 = (f32[8,128]{1,0:T(8,128)S(1)}, f32[8,128]{1,0:T(8,128)S(1)}, u32[]{:S(2)}, u32[]{:S(2)}) collective-permute-start(f32[8,128]{1,0:T(8,128)S(1)} %add.71), channel_id=1, source_target_pairs={{0,128},{16,144},{32,160},{48,176},{64,192},{80,208},{96,224},{112... | collective-permute-start | bytes 12296 | tf_op jit(solution)/shard_map/ppermute | solution.py:692
  84.6 3.3 %collective-permute-start.2 = (bf16[18,16,128]{2,1,0:T(8,128)(2,1)S(1)}, bf16[18,16,128]{2,1,0:T(8,128)(2,1)S(1)}, u32[]{:S(2)}, u32[]{:S(2)}) collective-permute-start(bf16[18,16,128]{2,1,0:T(8,128)(2,1)S(1)} %get-tuple-element.36), channel_id=1, source_target_pairs={{0,16},{16,32},{32,48},{48,64},{64,80},{80,96},{96,112},{112,128},... | collective-permute-start | bytes 221192 | tf_op jit(solution)/shard_map/ppermute | solution.py:281
  87.8 1.3 collective-permute-start.3
  90.6 2.6 %collective-permute-done.3.upper_ref = bf16[18,16,128]{2,1,0:T(8,128)(2,1)S(1)} collective-permute-done((bf16[18,16,128]{2,1,0:T(8,128)(2,1)S(1)}, bf16[18,16,128]{2,1,0:T(8,128)(2,1)S(1)}, u32[]{:S(2)}, u32[]{:S(2)}) %collective-permute-start.3) | collective-permute-done | bytes 73760 | tf_op jit(solution)/shard_map/ppermute | solution.py:282
  93.2 4.4 %hub_rows.3 = bf16[16,2,7,16,128]{4,3,2,1,0:T(8,128)(2,1)} custom-call(s32[2]{0:T(128)S(1)} %pad_add_fusion.place_ref, s32[1,16]{1,0:T(1,128)S(1)} %copy-done.19, s32[16,27]{1,0:T(8,128)S(1)} %copy-done.18, bf16[16,13,16,128]{3,2,1,0:T(8,128)(2,1)S(1)} %all-to-all-done.1.got_ref, bf16[18,16,128]{2,1,0:T(8,128)(2,1)S(1)} %collective-permute-done.2.lower_ref, ...), custom_call_target="tpu_custom_call" | custom-call | bytes 8388608 | tf_op jit(solution)/shard_map/hub_rows/pallas_call | solution.py:259
  97.7 11.2 %all-to-all-start.3 = ((bf16[16,2,7,16,128]{4,3,2,1,0:T(8,128)(2,1)}), bf16[16,2,7,16,128]{4,3,2,1,0:T(8,128)(2,1)S(1)}, u32[]{:S(2)}, u32[]{:S(2)}) async-start(bf16[16,2,7,16,128]{4,3,2,1,0:T(8,128)(2,1)} %hub_rows.3), calls=%async_computation.3 | async-start | bytes 1835008 | tf_op jit(solution)/shard_map/all_to_all | solution.py:275
  108.9 15.5 %weight_grad.1 = (f32[27,128,128]{2,1,0:T(8,128)S(1)}, bf16[2,18,18,16,128]{4,3,2,1,0:T(8,128)(2,1)}, bf16[2,2,3,18,16,128]{5,4,3,2,1,0:T(8,128)(2,1)S(1)}, bf16[2,16,256,128]{3,2,1,0:T(8,128)(2,1)S(1)}) custom-call(s32[2,16,16]{2,1,0:T(8,128)S(1)} %copy-done.17, s32[2]{0:T(128)S(1)} %convert_element_type.16.live_ref, bf16[2,16,256,128]{3,2,1,0:T(8,128)(2,1)} %f_ref.9, ...), custom_call_target="tpu_custom_call" | custom-call | flops 20000000000 | bytes 8388608 | tf_op jit(solution)/shard_map/weight_grad/pallas_call | solution.py:430
  124.4 1.2 copy-done.10
  125.6 1.4 copy-done.21
  127.0 1.0 copy-done.24
  128.0 6.2 %all-to-all-done.3.rim_ref = bf16[16,2,7,16,128]{4,3,2,1,0:T(8,128)(2,1)S(1)} async-done(((bf16[16,2,7,16,128]{4,3,2,1,0:T(8,128)(2,1)}), bf16[16,2,7,16,128]{4,3,2,1,0:T(8,128)(2,1)S(1)}, u32[]{:S(2)}, u32[]{:S(2)}) %all-to-all-start.3) | async-done | bytes 917536 | tf_op jit(solution)/shard_map/all_to_all | solution.py:275
  134.2 6.4 %all-to-all-start.4 = ((f32[16,216,128]{2,1,0:T(8,128)}), f32[16,216,128]{2,1,0:T(8,128)}, u32[]{:S(2)}, u32[]{:S(2)}) async-start(f32[16,216,128]{2,1,0:T(8,128)} %bitcast.28), calls=%async_computation.4 | async-start | bytes 3538944 | tf_op jit(solution)/shard_map/all_to_all | solution.py:275
  140.6 1.2 copy-done.15
  141.8 1.2 copy-done.25
  143.0 17.7 %back_conv.1 = (f32[2,16,256,128]{3,2,1,0:T(8,128)}, f32[8,128]{1,0:T(8,128)S(1)}) custom-call(s32[2,16,16]{2,1,0:T(8,128)S(1)} %copy-done.17, s32[2]{0:T(128)S(1)} %convert_element_type.16.live_ref, bf16[2,16,256,128]{3,2,1,0:T(8,128)(2,1)S(1)} %copy-done.4, bf16[2,18,18,16,128]{4,3,2,1,0:T(8,128)(2,1)} %get-tuple-element.49.pad_ref, ...), custom_call_target="tpu_custom_call" | custom-call | flops 20000000000 | bytes 8388608 | tf_op jit(solution)/shard_map/back_conv/pallas_call | solution.py:557
  160.7 6.2 %all-to-all-done.4 = f32[16,216,128]{2,1,0:T(8,128)} async-done(((f32[16,216,128]{2,1,0:T(8,128)}), f32[16,216,128]{2,1,0:T(8,128)}, u32[]{:S(2)}, u32[]{:S(2)}) %all-to-all-start.4) | async-done | bytes 1769504 | tf_op jit(solution)/shard_map/all_to_all | solution.py:275
  166.9 1.6 reduce_sum.18
  168.5 0.7 pad_maximum_fusion
  169.2 4.2 %all-to-all-start.5 = ((f32[16,24,128]{2,1,0:T(8,128)}), f32[16,24,128]{2,1,0:T(8,128)S(1)}, u32[]{:S(2)}, u32[]{:S(2)}) async-start(f32[16,24,128]{2,1,0:T(8,128)} %pad_maximum_fusion), calls=%async_computation.5 | async-start | bytes 393216 | tf_op jit(solution)/shard_map/all_to_all | solution.py:275
  173.4 1.6 copy-done.5
  175.0 1.2 copy-done.13
  176.1 1.6 copy-done.22
  177.7 8.8 %forward_conv.2.refs_0_ = bf16[2,16,256,128]{3,2,1,0:T(8,128)(2,1)} custom-call(s32[2,16,16]{2,1,0:T(8,128)S(1)} %copy-done.17, s32[2]{0:T(128)S(1)} %convert_element_type.16.live_ref, bf16[2,16,256,128]{3,2,1,0:T(8,128)(2,1)S(1)} %copy-done.5, bf16[2,16,256,128]{3,2,1,0:T(8,128)(2,1)S(1)} %copy-done.22, ...), custom_call_target="tpu_custom_call" | custom-call | flops 10000000000 | bytes 4194304 | tf_op jit(solution)/shard_map/forward_conv/pallas_call | solution.py:621
  186.9 2.2 collective-permute-done.8
  189.1 4.0 %collective-permute-done.9 = f32[8,128]{1,0:T(8,128)S(1)} collective-permute-done((f32[8,128]{1,0:T(8,128)S(1)}, f32[8,128]{1,0:T(8,128)S(1)}, u32[]{:S(2)}, u32[]{:S(2)}) %collective-permute-start.9) | collective-permute-done | bytes 4128 | tf_op jit(solution)/shard_map/ppermute | solution.py:692
  193.1 2.5 %collective-permute-done.10 = f32[8,128]{1,0:T(8,128)S(1)} collective-permute-done((f32[8,128]{1,0:T(8,128)S(1)}, f32[8,128]{1,0:T(8,128)S(1)}, u32[]{:S(2)}, u32[]{:S(2)}) %collective-permute-start.10) | collective-permute-done | bytes 4128 | tf_op jit(solution)/shard_map/ppermute | solution.py:692
  196.7 9.4 %all-to-all-start.6 = ((bf16[16,16,128]{2,1,0:T(8,128)(2,1)}), bf16[16,16,128]{2,1,0:T(8,128)(2,1)S(1)}, u32[]{:S(2)}, u32[]{:S(2)}) async-start(bf16[16,16,128]{2,1,0:T(8,128)(2,1)} %broadcast_in_dim.10), calls=%async_computation.6 | async-start | bytes 131072 | tf_op jit(solution)/shard_map/all_to_all | solution.py:275
  206.4 1.6 copy-done.6
  208.0 2.2 copy-done.8
  210.2 4.0 %finish.1 = bf16[2,16,256,128]{3,2,1,0:T(8,128)(2,1)} custom-call(s32[2,16,16]{2,1,0:T(8,128)S(1)} %copy-done.17, s32[2]{0:T(128)S(1)} %convert_element_type.16.live_ref, bf16[2,16,256,128]{3,2,1,0:T(8,128)(2,1)S(1)} %copy-done.6, bf16[2,16,256,128]{3,2,1,0:T(8,128)(2,1)S(1)} %copy-done.2, f32[2,16,256,128]{3,2,1,0:T(8,128)S(1)} %copy-done.8, ...), custom_call_target="tpu_custom_call" | custom-call | bytes 12582912 | tf_op jit(solution)/shard_map/finish/pallas_call | solution.py:676
  214.1 1.0 broadcast_in_dim.11
  215.2 5.9 %all-to-all-start.7 = ((bf16[16,216,128]{2,1,0:T(8,128)(2,1)}), bf16[16,216,128]{2,1,0:T(8,128)(2,1)S(1)}, u32[]{:S(2)}, u32[]{:S(2)}) async-start(bf16[16,216,128]{2,1,0:T(8,128)(2,1)} %broadcast_in_dim.11), calls=%async_computation.7 | async-start | bytes 1769472 | tf_op jit(solution)/shard_map/all_to_all | solution.py:275
  221.1 1.2 copy-done.12
  222.3 1.2 copy-done.14
  223.4 1.6 copy-done.23
  225.0 8.8 %forward_conv.3 = bf16[2,16,256,128]{3,2,1,0:T(8,128)(2,1)} custom-call(s32[2,16,16]{2,1,0:T(8,128)S(1)} %copy-done.17, s32[2]{0:T(128)S(1)} %convert_element_type.16.live_ref, bf16[2,16,256,128]{3,2,1,0:T(8,128)(2,1)S(1)} %copy-done.7, bf16[2,16,256,128]{3,2,1,0:T(8,128)(2,1)S(1)} %copy-done.23, ...), custom_call_target="tpu_custom_call", output_to_operand_aliasing={{}: (8, {})} | custom-call | flops 10000000000 | bytes 4194304 | tf_op jit(solution)/shard_map/forward_conv/pallas_call | solution.py:621
  233.8 2.3 all-to-all-done.7.parts_ref
  236.1 1.6 scale.1
  (84 shorter events, 3.7 us)
Async XLA Ops:
  0.6 28.1 %copy-start = (f32[256,256]{1,0:T(8,128)S(1)}, f32[256,256]{1,0:T(8,128)}, u32[]{:S(2)}) copy-start(f32[256,256]{1,0:T(8,128)} %param.19) | copy-start | bytes 786436
  0.6 1.6 copy-start.1
  2.3 0.7 copy-start.16
  3.0 13.9 %copy-start.3 = (bf16[2,16,256,128]{3,2,1,0:T(8,128)(2,1)S(1)}, bf16[2,16,256,128]{3,2,1,0:T(8,128)(2,1)}, u32[]{:S(2)}) copy-start(bf16[2,16,256,128]{3,2,1,0:T(8,128)(2,1)} %f_ref.9) | copy-start | bytes 6291460
  3.0 13.9 %copy-start.17 = (s32[2,16,16]{2,1,0:T(8,128)S(1)}, s32[2,16,16]{2,1,0:T(8,128)}, u32[]{:S(2)}) copy-start(s32[2,16,16]{2,1,0:T(8,128)} %occ_ref.13) | copy-start | bytes 6148
  6.0 0.9 copy-start.9
  6.9 34.0 %all-to-all-start = ((bf16[16,13,16,128]{3,2,1,0:T(8,128)(2,1)}), bf16[16,13,16,128]{3,2,1,0:T(8,128)(2,1)S(1)}, u32[]{:S(2)}, u32[]{:S(2)}) async-start(bf16[16,13,16,128]{3,2,1,0:T(8,128)(2,1)} %copy-done.9), calls=%async_computation | async-start | bytes 1703936 | tf_op jit(solution)/shard_map/all_to_all | solution.py:275
  22.5 4.7 %copy-start.26 = (bf16[27,128,128]{2,1,0:T(8,128)(2,1)S(1)}, bf16[27,128,128]{2,1,0:T(8,128)(2,1)}, u32[]{:S(2)}) copy-start(bf16[27,128,128]{2,1,0:T(8,128)(2,1)} %param.20) | copy-start | bytes 2654212
  24.8 4.2 %copy-start.27 = (f32[128]{0:T(128)S(1)}, f32[128]{0:T(128)}, u32[]{:S(2)}) copy-start(f32[128]{0:T(128)} %param.18) | copy-start | bytes 1540
  24.8 4.2 %copy-start.28 = (f32[128]{0:T(128)S(1)}, f32[128]{0:T(128)}, u32[]{:S(2)}) copy-start(f32[128]{0:T(128)} %param.17) | copy-start | bytes 1540
  29.0 15.4 %copy-start.19 = (s32[1,16]{1,0:T(1,128)S(1)}, s32[1,16]{1,0:T(1,128)}, u32[]{:S(2)}) copy-start(s32[1,16]{1,0:T(1,128)} %live_ref.7) | copy-start | bytes 196
  30.7 23.8 %copy-start.18 = (s32[16,27]{1,0:T(8,128)S(1)}, s32[16,27]{1,0:T(8,128)}, u32[]{:S(2)}) copy-start(s32[16,27]{1,0:T(8,128)} %near_ref.3) | copy-start | bytes 5188
  40.9 27.2 %all-to-all-start.1 = ((bf16[16,13,16,128]{3,2,1,0:T(8,128)(2,1)}), bf16[16,13,16,128]{3,2,1,0:T(8,128)(2,1)S(1)}, u32[]{:S(2)}, u32[]{:S(2)}) async-start(bf16[16,13,16,128]{3,2,1,0:T(8,128)(2,1)} %surface.2), calls=%async_computation.1 | async-start | bytes 1703936 | tf_op jit(solution)/shard_map/all_to_all | solution.py:275
  45.7 5.0 %collective-permute-start = (bf16[18,16,128]{2,1,0:T(8,128)(2,1)S(1)}, bf16[18,16,128]{2,1,0:T(8,128)(2,1)S(1)}, u32[]{:S(2)}, u32[]{:S(2)}) collective-permute-start(bf16[18,16,128]{2,1,0:T(8,128)(2,1)S(1)} %get-tuple-element.32), channel_id=1, source_target_pairs={{0,16},{16,32},{32,48},{48,64},{64,80},{80,96},{96,112},{112,128},... | collective-permute-start | bytes 221192 | tf_op jit(solution)/shard_map/ppermute | solution.py:281
  48.9 5.6 %collective-permute-start.1 = (bf16[18,16,128]{2,1,0:T(8,128)(2,1)S(1)}, bf16[18,16,128]{2,1,0:T(8,128)(2,1)S(1)}, u32[]{:S(2)}, u32[]{:S(2)}) collective-permute-start(bf16[18,16,128]{2,1,0:T(8,128)(2,1)S(1)} %get-tuple-element.33), channel_id=1, source_target_pairs={{16,0},{32,16},{48,32},{64,48},{80,64},{96,80},{112,96},{128,112},... | collective-permute-start | bytes 221192 | tf_op jit(solution)/shard_map/ppermute | solution.py:282
  68.1 29.5 %all-to-all-start.2 = ((bf16[16,2,7,16,128]{4,3,2,1,0:T(8,128)(2,1)}), bf16[16,2,7,16,128]{4,3,2,1,0:T(8,128)(2,1)S(1)}, u32[]{:S(2)}, u32[]{:S(2)}) async-start(bf16[16,2,7,16,128]{4,3,2,1,0:T(8,128)(2,1)} %hub_rows.2), calls=%async_computation.2 | async-start | bytes 1835008 | tf_op jit(solution)/shard_map/all_to_all | solution.py:275
  72.3 2.5 %collective-permute-start.4 = (f32[8,128]{1,0:T(8,128)S(1)}, f32[8,128]{1,0:T(8,128)S(1)}, u32[]{:S(2)}, u32[]{:S(2)}) collective-permute-start(f32[8,128]{1,0:T(8,128)S(1)} %get-tuple-element.40), channel_id=1, source_target_pairs={{0,16},{16,0},{32,48},{48,32},{64,80},{80,64},{96,112},{112,96},{1... | collective-permute-start | bytes 12296 | tf_op jit(solution)/shard_map/ppermute | solution.py:692
  74.9 4.2 %collective-permute-start.5 = (f32[8,128]{1,0:T(8,128)S(1)}, f32[8,128]{1,0:T(8,128)S(1)}, u32[]{:S(2)}, u32[]{:S(2)}) collective-permute-start(f32[8,128]{1,0:T(8,128)S(1)} %add.69), channel_id=1, source_target_pairs={{0,32},{16,48},{32,0},{48,16},{64,96},{80,112},{96,64},{112,80},{1... | collective-permute-start | bytes 12296 | tf_op jit(solution)/shard_map/ppermute | solution.py:692
  79.1 2.8 %collective-permute-start.6 = (f32[8,128]{1,0:T(8,128)S(1)}, f32[8,128]{1,0:T(8,128)S(1)}, u32[]{:S(2)}, u32[]{:S(2)}) collective-permute-start(f32[8,128]{1,0:T(8,128)S(1)} %add.70), channel_id=1, source_target_pairs={{0,64},{16,80},{32,96},{48,112},{64,0},{80,16},{96,32},{112,48},{1... | collective-permute-start | bytes 12296 | tf_op jit(solution)/shard_map/ppermute | solution.py:692
  81.8 7.3 %collective-permute-start.7 = (f32[8,128]{1,0:T(8,128)S(1)}, f32[8,128]{1,0:T(8,128)S(1)}, u32[]{:S(2)}, u32[]{:S(2)}) collective-permute-start(f32[8,128]{1,0:T(8,128)S(1)} %add.71), channel_id=1, source_target_pairs={{0,128},{16,144},{32,160},{48,176},{64,192},{80,208},{96,224},{112... | collective-permute-start | bytes 12296 | tf_op jit(solution)/shard_map/ppermute | solution.py:692
  84.6 6.0 %collective-permute-start.2 = (bf16[18,16,128]{2,1,0:T(8,128)(2,1)S(1)}, bf16[18,16,128]{2,1,0:T(8,128)(2,1)S(1)}, u32[]{:S(2)}, u32[]{:S(2)}) collective-permute-start(bf16[18,16,128]{2,1,0:T(8,128)(2,1)S(1)} %get-tuple-element.36), channel_id=1, source_target_pairs={{0,16},{16,32},{32,48},{48,64},{64,80},{80,96},{96,112},{112,128},... | collective-permute-start | bytes 221192 | tf_op jit(solution)/shard_map/ppermute | solution.py:281
  87.8 5.4 %collective-permute-start.3 = (bf16[18,16,128]{2,1,0:T(8,128)(2,1)S(1)}, bf16[18,16,128]{2,1,0:T(8,128)(2,1)S(1)}, u32[]{:S(2)}, u32[]{:S(2)}) collective-permute-start(bf16[18,16,128]{2,1,0:T(8,128)(2,1)S(1)} %get-tuple-element.37), channel_id=1, source_target_pairs={{16,0},{32,16},{48,32},{64,48},{80,64},{96,80},{112,96},{128,112},... | collective-permute-start | bytes 221192 | tf_op jit(solution)/shard_map/ppermute | solution.py:282
  97.7 36.5 %all-to-all-start.3 = ((bf16[16,2,7,16,128]{4,3,2,1,0:T(8,128)(2,1)}), bf16[16,2,7,16,128]{4,3,2,1,0:T(8,128)(2,1)S(1)}, u32[]{:S(2)}, u32[]{:S(2)}) async-start(bf16[16,2,7,16,128]{4,3,2,1,0:T(8,128)(2,1)} %hub_rows.3), calls=%async_computation.3 | async-start | bytes 1835008 | tf_op jit(solution)/shard_map/all_to_all | solution.py:275
  124.4 1.2 copy-start.10
  125.6 1.4 copy-start.21
  127.0 1.0 copy-start.24
  128.0 12.7 %copy-start.4 = (bf16[2,16,256,128]{3,2,1,0:T(8,128)(2,1)S(1)}, bf16[2,16,256,128]{3,2,1,0:T(8,128)(2,1)}, u32[]{:S(2)}) copy-start(bf16[2,16,256,128]{3,2,1,0:T(8,128)(2,1)} %f_ref.9) | copy-start | bytes 6291460
  134.2 39.2 %copy-start.11 = (bf16[16,2,7,16,128]{4,3,2,1,0:T(8,128)(2,1)}, bf16[16,2,7,16,128]{4,3,2,1,0:T(8,128)(2,1)S(1)}, u32[]{:S(2)}) copy-start(bf16[16,2,7,16,128]{4,3,2,1,0:T(8,128)(2,1)S(1)} %all-to-all-done.3.rim_ref) | copy-start | bytes 2752516
  134.2 32.7 %all-to-all-start.4 = ((f32[16,216,128]{2,1,0:T(8,128)}), f32[16,216,128]{2,1,0:T(8,128)}, u32[]{:S(2)}, u32[]{:S(2)}) async-start(f32[16,216,128]{2,1,0:T(8,128)} %bitcast.28), calls=%async_computation.4 | async-start | bytes 3538944 | tf_op jit(solution)/shard_map/all_to_all | solution.py:275
  140.6 1.2 copy-start.15
  141.8 1.2 copy-start.25
  160.6 12.7 %copy-start.20 = (f32[128]{0:T(128)S(1)}, f32[128]{0:T(128)}, u32[]{:S(2)}) copy-start(f32[128]{0:T(128)} %param.21) | copy-start | bytes 1540
  169.2 17.3 %all-to-all-start.5 = ((f32[16,24,128]{2,1,0:T(8,128)}), f32[16,24,128]{2,1,0:T(8,128)S(1)}, u32[]{:S(2)}, u32[]{:S(2)}) async-start(f32[16,24,128]{2,1,0:T(8,128)} %pad_maximum_fusion), calls=%async_computation.5 | async-start | bytes 393216 | tf_op jit(solution)/shard_map/all_to_all | solution.py:275
  173.4 1.6 copy-start.5
  175.0 1.2 copy-start.13
  176.1 1.6 copy-start.22
  177.7 28.6 %copy-start.2 = (bf16[2,16,256,128]{3,2,1,0:T(8,128)(2,1)S(1)}, bf16[2,16,256,128]{3,2,1,0:T(8,128)(2,1)}, u32[]{:S(2)}) copy-start(bf16[2,16,256,128]{3,2,1,0:T(8,128)(2,1)} %g_ref.3) | copy-start | bytes 6291460
  186.6 2.5 %collective-permute-start.8 = (f32[8,128]{1,0:T(8,128)S(1)}, f32[8,128]{1,0:T(8,128)S(1)}, u32[]{:S(2)}, u32[]{:S(2)}) collective-permute-start(f32[8,128]{1,0:T(8,128)S(1)} %slice.45), channel_id=1, source_target_pairs={{0,16},{16,0},{32,48},{48,32},{64,80},{80,64},{96,112},{112,96},{1... | collective-permute-start | bytes 12296 | tf_op jit(solution)/shard_map/ppermute | solution.py:692
  189.1 4.0 %collective-permute-start.9 = (f32[8,128]{1,0:T(8,128)S(1)}, f32[8,128]{1,0:T(8,128)S(1)}, u32[]{:S(2)}, u32[]{:S(2)}) collective-permute-start(f32[8,128]{1,0:T(8,128)S(1)} %add.75), channel_id=1, source_target_pairs={{0,32},{16,48},{32,0},{48,16},{64,96},{80,112},{96,64},{112,80},{1... | collective-permute-start | bytes 12296 | tf_op jit(solution)/shard_map/ppermute | solution.py:692
  193.1 2.5 %collective-permute-start.10 = (f32[8,128]{1,0:T(8,128)S(1)}, f32[8,128]{1,0:T(8,128)S(1)}, u32[]{:S(2)}, u32[]{:S(2)}) collective-permute-start(f32[8,128]{1,0:T(8,128)S(1)} %add.76), channel_id=1, source_target_pairs={{0,64},{16,80},{32,96},{48,112},{64,0},{80,16},{96,32},{112,48},{1... | collective-permute-start | bytes 12296 | tf_op jit(solution)/shard_map/ppermute | solution.py:692
  195.6 10.6 %collective-permute-start.11 = (f32[8,128]{1,0:T(8,128)S(1)}, f32[8,128]{1,0:T(8,128)S(1)}, u32[]{:S(2)}, u32[]{:S(2)}) collective-permute-start(f32[8,128]{1,0:T(8,128)S(1)} %add.77), channel_id=1, source_target_pairs={{0,128},{16,144},{32,160},{48,176},{64,192},{80,208},{96,224},{112... | collective-permute-start | bytes 12296 | tf_op jit(solution)/shard_map/ppermute | solution.py:692
  196.7 17.4 %all-to-all-start.6 = ((bf16[16,16,128]{2,1,0:T(8,128)(2,1)}), bf16[16,16,128]{2,1,0:T(8,128)(2,1)S(1)}, u32[]{:S(2)}, u32[]{:S(2)}) async-start(bf16[16,16,128]{2,1,0:T(8,128)(2,1)} %broadcast_in_dim.10), calls=%async_computation.6 | async-start | bytes 131072 | tf_op jit(solution)/shard_map/all_to_all | solution.py:275
  206.4 1.6 copy-start.6
  208.0 2.2 copy-start.8
  214.1 7.0 %copy-start.7 = (bf16[2,16,256,128]{3,2,1,0:T(8,128)(2,1)S(1)}, bf16[2,16,256,128]{3,2,1,0:T(8,128)(2,1)}, u32[]{:S(2)}) copy-start(bf16[2,16,256,128]{3,2,1,0:T(8,128)(2,1)} %f_ref.9) | copy-start | bytes 6291460
  215.2 20.9 %all-to-all-start.7 = ((bf16[16,216,128]{2,1,0:T(8,128)(2,1)}), bf16[16,216,128]{2,1,0:T(8,128)(2,1)S(1)}, u32[]{:S(2)}, u32[]{:S(2)}) async-start(bf16[16,216,128]{2,1,0:T(8,128)(2,1)} %broadcast_in_dim.11), calls=%async_computation.7 | async-start | bytes 1769472 | tf_op jit(solution)/shard_map/all_to_all | solution.py:275
  221.1 1.2 copy-start.12
  222.3 1.2 copy-start.14
  223.4 1.6 copy-start.23

commit v2 on v1

--- a/solution.py
+++ b/solution.py
@@ -45,10 +45,6 @@
         for y in range(edge)
     ]
     return jnp.concatenate(rows, axis=0) != 0
-
-
-def planes_mask(occ_ref, slot, z, count, edge, channels):
-    return jnp.concatenate([plane_mask(occ_ref, slot, z + i, edge, channels) for i in range(count)], axis=0)
 
 
 def x_row(rows, edge, channels):
@@ -140,7 +136,7 @@
             pltpu.VMEM((edge, 16, channels), f32),
             pltpu.VMEM((8, channels), f32),
         ],
-        compiler_params=params(24, ("arbitrary",)),
+        compiler_params=params(60, ("arbitrary",)),
         cost_estimate=cost(0, 3 * MIB),
         name="surface",
     )(occupancy, values)
@@ -275,11 +271,14 @@
     return lax.all_to_all(values, axis, split_axis=0, concat_axis=0, tiled=True)
 
 
-def hub_stage(place, live_slots, neighbours, got, fill):
+def hub_stage(place, live_slots, neighbours, got, fill, with_stats=False):
     to_left, to_right, stats = trade(live_slots, got)
     count = lax.axis_size("wide")
     lower = lax.ppermute(to_right, "wide", [(i, i + 1) for i in range(count - 1)])
     upper = lax.ppermute(to_left, "wide", [(i + 1, i) for i in range(count - 1)])
+    if with_stats:
+        stats, lower, upper = lax.optimization_barrier((stats, lower, upper))
+        stats = wide_round(stats, 1)
     return (hub_rows(place, live_slots, neighbours, got, lower, upper, fill), stats)
 
 
@@ -351,8 +350,8 @@
 
         lax.fori_loop(0, edge, fill, 0)
 
-        def prepare(chunk, flip_s):
-            for part in range(depth):
+        def prepare(chunk, flip_s, part):
+            if part < depth:
                 z = chunk * depth + part
                 mask = plane_mask(occ_ref, slot, z, edge, channels)
                 hidden = hidden_plane(f_ref[0, z].astype(f32), mask, coef).astype(bf16)
@@ -378,10 +377,10 @@
 
         pairs = [(0, 1), (2, 3), (4, 5), (6, 7), (8,)]
 
-        def multiply(chunk, flip_s):
+        def multiply(chunk, flip_s, beside):
             z0 = chunk * depth
             left = flip_s[...]
-            for pair in pairs:
+            for turn, pair in enumerate(pairs):
                 right = [
                     pad_ref[0, pl.ds(z0 + tap // 3, depth), tap % 3 : tap % 3 + edge].reshape(
                         depth * cells, channels
@@ -400,17 +399,18 @@
                                 place * channels : (place + 1) * channels,
                             ],
                         )
-
-        prepare(0, even_s)
+                beside(turn)
 
         def two(i, carry):
-            prepare(2 * i + 1, odd_s)
-            multiply(2 * i, even_s)
-            prepare(jnp.minimum(2 * i + 2, chunks - 1), even_s)
-            multiply(2 * i + 1, odd_s)
+            multiply(2 * i, even_s, functools.partial(prepare, 2 * i + 1, odd_s))
+            multiply(2 * i + 1, odd_s, functools.partial(prepare, 2 * i + 2, even_s))
             return carry
 
-        lax.fori_loop(0, chunks // 2, two, 0)
+        for part in range(depth):
+            prepare(0, even_s, part)
+        lax.fori_loop(0, chunks // 2 - 1, two, 0)
+        multiply(chunks - 2, even_s, functools.partial(prepare, chunks - 1, odd_s))
+        multiply(chunks - 1, odd_s, lambda turn: None)
         for side in range(2):
             left = face_s[side].T.astype(bf16)
             for tap in range(9):
@@ -459,7 +459,7 @@
             pltpu.VMEM((min(4, edge // 2), cells, channels), f32),
             pltpu.VMEM((2, cells, channels), f32),
         ],
-        compiler_params=params(48, ("arbitrary",)),
+        compiler_params=params(60, ("arbitrary",)),
         cost_estimate=cost(20 * 10**9, 8 * MIB),
         name="weight_grad",
     )(occupancy, live, features, cotangent, rim, coef)
@@ -483,12 +483,17 @@
 DEPTH = 2
 
 
-def conv_planes(edge, z, pad_ref, pad_lead, w_ref, side_s, x_at):
+def conv_pipeline(edge, pad_ref, pad_lead, w_ref, side_s, found_s, finish_plane, carry):
     cells = edge * edge
     rows = DEPTH * cells
     channels = w_ref.shape[0] // 9
-    found = jnp.dot(
-        jnp.concatenate(
+    groups = edge // DEPTH
+    x_at = x_row(cells, edge, channels)
+    spans = [slice(0, 2 * channels), slice(2 * channels, 3 * channels)]
+
+    def multiply(group, buffer, span):
+        z = group * DEPTH
+        lines = jnp.concatenate(
             [
                 pad_ref[pad_lead + (pl.ds(z + tap // 3, DEPTH), slice(tap % 3, tap % 3 + edge))].reshape(
                     rows, channels
@@ -496,21 +501,40 @@
                 for tap in range(9)
             ],
             axis=1,
-        ),
-        w_ref[...],
-        preferred_element_type=f32,
-    )
-
-    def beside(side):
-        line = side_s[side, pl.ds(pl.multiple_of(z * edge, edge), DEPTH * edge), :]
-        return jnp.broadcast_to(line[:, None, :], (DEPTH * edge, edge, channels)).reshape(rows, channels)
-
-    before = jnp.where(x_at == 0, beside(0), pltpu.roll(found[:, :channels], 1, 0))
-    after = jnp.where(x_at == edge - 1, beside(1), pltpu.roll(found[:, 2 * channels :], rows - 1, 0))
-    return found[:, channels : 2 * channels] + before + after
-
-
-def back_kernel(edge, occ_ref, live_ref, f_ref, pad_ref, shift_ref, w_ref, coef_ref, hat_ref, sum_ref, side_s):
+        )
+        found_s[buffer, :, span] = jnp.dot(lines, w_ref[:, span], preferred_element_type=f32)
+
+    def combine(group, buffer, part, carry):
+        z = group * DEPTH + part
+        found = found_s[buffer, part * cells : (part + 1) * cells]
+
+        def beside(side):
+            line = side_s[side, pl.ds(pl.multiple_of(z * edge, edge), edge), :]
+            return jnp.broadcast_to(line[:, None, :], (edge, edge, channels)).reshape(cells, channels)
+
+        before = jnp.where(x_at == 0, beside(0), pltpu.roll(found[:, :channels], 1, 0))
+        after = jnp.where(x_at == edge - 1, beside(1), pltpu.roll(found[:, 2 * channels :], cells - 1, 0))
+        return finish_plane(z, found[:, channels : 2 * channels] + before + after, carry)
+
+    def advance(group, buffer, carry):
+        for part in range(DEPTH):
+            multiply(group + 1, 1 - buffer, spans[part])
+            carry = combine(group, buffer, part, carry)
+        return carry
+
+    def step(i, carry):
+        return advance(2 * i + 1, 1, advance(2 * i, 0, carry))
+
+    for span in spans:
+        multiply(0, 0, span)
+    carry = lax.fori_loop(0, groups // 2 - 1, step, carry)
+    carry = advance(groups - 2, 0, carry)
+    for part in range(DEPTH):
+        carry = combine(groups - 1, 1, part, carry)
+    return carry
+
+
+def back_kernel(edge, occ_ref, live_ref, f_ref, pad_ref, shift_ref, w_ref, coef_ref, hat_ref, sum_ref, side_s, found_s):
     channels = f_ref.shape[-1]
     slot = pl.program_id(0)
     coef = coefficients(coef_ref)
@@ -523,29 +547,21 @@
     @pl.when(live_ref[slot] != 0)
     def _():
         side_rows(edge, shift_ref, (0,), w_ref, side_s)
-        rows = DEPTH * edge * edge
-        x_at = x_row(rows, edge, channels)
-
-        def planes(z, first, second):
-            back = conv_planes(edge, z, pad_ref, (0,), w_ref, side_s, x_at)
-            mask = planes_mask(occ_ref, slot, z, DEPTH, edge, channels)
-            feats = f_ref[0, pl.ds(z, DEPTH)].reshape(rows, channels).astype(f32)
-            normed = (feats - mean) * rstd
+
+        def plane(z, back, carry):
+            first, second = carry
+            mask = plane_mask(occ_ref, slot, z, edge, channels)
+            normed = (f_ref[0, z].astype(f32) - mean) * rstd
             pre = normed * scale + shift
             gate = jax.nn.sigmoid(pre)
             hat = jnp.where(mask, back * (gate * (1.0 + pre * (1.0 - gate))) * scale, 0.0)
-            hat_ref[0, pl.ds(z, DEPTH)] = hat.reshape(DEPTH, edge * edge, channels)
+            hat_ref[0, z] = hat
             first = first + jnp.sum(hat, axis=0, keepdims=True)
             second = second + jnp.sum(hat * normed, axis=0, keepdims=True)
             return (first, second)
 
-        def step(i, carry):
-            for part in range(2):
-                carry = planes((2 * i + part) * DEPTH, *carry)
-            return carry
-
         zero = jnp.zeros((1, channels), f32)
-        first, second = lax.fori_loop(0, edge // (2 * DEPTH), step, (zero, zero))
+        first, second = conv_pipeline(edge, pad_ref, (0,), w_ref, side_s, found_s, plane, (zero, zero))
         sum_ref[0:1, :] = sum_ref[0:1, :] + first
         sum_ref[1:2, :] = sum_ref[1:2, :] + second
 
@@ -571,15 +587,18 @@
             pl.BlockSpec((8, channels), lambda s: (0, 0)),
         ],
         out_specs=(whole, pl.BlockSpec((8, channels), lambda s: (0, 0))),
-        scratch_shapes=[pltpu.VMEM((2, cells, channels), f32)],
-        compiler_params=params(48, ("arbitrary",)),
+        scratch_shapes=[
+            pltpu.VMEM((2, cells, channels), f32),
+            pltpu.VMEM((2, DEPTH * cells, 3 * channels), f32),
+        ],
+        compiler_params=params(60, ("arbitrary",)),
         cost_estimate=cost(20 * 10**9, 8 * MIB),
         name="back_conv",
     )(occupancy, live, features, padded, shifted, weight, coef)
 
 
 def forward_kernel(edge, slot, occ_ref, live_ref, f_ref, hid_ref, rim_ref, w_ref, coef_ref, bias_ref, *refs):
-    out_ref, pad_s, shift_s, xh_s, edge_s, side_s = refs[-6:]
+    out_ref, pad_s, shift_s, xh_s, edge_s, side_s, found_s = refs[-7:]
     channels = f_ref.shape[-1]
     coef = coefficients(coef_ref)
 
@@ -596,20 +615,14 @@
         for z in range(edge):
             pad_s[z + 1, 1 : edge + 1] = hid_ref[0, z].reshape(edge, edge, channels)
         side_rows(edge, shift_s, (), w_ref, side_s)
-        rows = DEPTH * edge * edge
-        x_at = x_row(rows, edge, channels)
-
-        def step(i, carry):
-            for part in range(2):
-                z = (2 * i + part) * DEPTH
-                conv = conv_planes(edge, z, pad_s, (), w_ref, side_s, x_at)
-                mask = planes_mask(occ_ref, slot, z, DEPTH, edge, channels)
-                feats = f_ref[0, pl.ds(z, DEPTH)].reshape(rows, channels).astype(f32)
-                mixed = (feats + jnp.where(mask, conv + bias_ref[...], 0.0)).astype(bf16)
-                out_ref[0, pl.ds(z, DEPTH)] = mixed.reshape(DEPTH, edge * edge, channels)
+
+        def plane(z, conv, carry):
+            mask = plane_mask(occ_ref, slot, z, edge, channels)
+            feats = f_ref[0, z].astype(f32)
+            out_ref[0, z] = (feats + jnp.where(mask, conv + bias_ref[...], 0.0)).astype(bf16)
             return carry
 
-        lax.fori_loop(0, edge // (2 * DEPTH), step, 0)
+        conv_pipeline(edge, pad_s, (), w_ref, side_s, found_s, plane, 0)
 
 
 def forward_conv(slot, occupancy, live, features, hidden, rim, weight, coef, bias, base=None):
@@ -640,19 +653,21 @@
             pltpu.VMEM((2, wide, 8 * ((edge + 16) // 8), channels), f32),
             pltpu.VMEM((4, edge, channels), f32),
             pltpu.VMEM((2, cells, channels), f32),
+            pltpu.VMEM((2, DEPTH * cells, 3 * channels), f32),
         ],
         input_output_aliases={8: 0} if extra else {},
-        compiler_params=params(48, ("arbitrary",)),
+        compiler_params=params(60, ("arbitrary",)),
         cost_estimate=cost(10 * 10**9, 4 * MIB),
         name="forward_conv",
     )(occupancy, live, features, hidden, rim, weight, coef, bias, *extra)
 
 
-def finish_kernel(edge, occ_ref, live_ref, f_ref, g_ref, hat_ref, coef_ref, out_ref):
+def finish_kernel(edge, occ_ref, live_ref, f_ref, g_ref, hat_ref, coef_ref, sums_ref, out_ref):
     channels = f_ref.shape[-1]
     slot = pl.program_id(0)
+    first_plane = pl.program_id(1) * f_ref.shape[1]
     mean, rstd = coef_ref[0:1, :], coef_ref[1:2, :]
-    first, second = coef_ref[2:3, :], coef_ref[3:4, :]
+    first, second = sums_ref[0:1, :], sums_ref[1:2, :]
 
     @pl.when(live_ref[slot] == 0)
     def _():
@@ -660,38 +675,35 @@
 
     @pl.when(live_ref[slot] != 0)
     def _():
-        def plane(z, carry):
-            mask = plane_mask(occ_ref, slot, z, edge, channels)
+        for z in range(f_ref.shape[1]):
+            mask = plane_mask(occ_ref, slot, first_plane + z, edge, channels)
             normed = (f_ref[0, z].astype(f32) - mean) * rstd
             change = rstd * (hat_ref[0, z] - first - normed * second)
             out_ref[0, z] = (g_ref[0, z].astype(f32) + jnp.where(mask, change, 0.0)).astype(bf16)
-            return carry
-
-        lax.fori_loop(0, edge, plane, 0)
-
-
-def finish(occupancy, live, features, cotangent, hat, coef):
+
+
+def finish(occupancy, live, features, cotangent, hat, coef, sums):
     edge, channels = features.shape[1], features.shape[-1]
-    whole = pl.BlockSpec((1, edge, edge * edge, channels), lambda s: (s, 0, 0, 0))
+    few = pl.BlockSpec((1, edge // 4, edge * edge, channels), lambda s, z: (s, z, 0, 0))
     return pl.pallas_call(
         functools.partial(finish_kernel, edge),
-        grid=(2,),
+        grid=(2, 4),
         out_shape=jax.ShapeDtypeStruct(features.shape, bf16),
-        in_specs=[SMEM, SMEM, whole, whole, whole, pl.BlockSpec((8, channels), lambda s: (0, 0))],
-        out_specs=whole,
-        compiler_params=params(32, ("arbitrary",)),
+        in_specs=[SMEM, SMEM, few, few, few] + [pl.BlockSpec((8, channels), lambda s, z: (0, 0))] * 2,
+        out_specs=few,
+        compiler_params=params(60, ("arbitrary", "arbitrary")),
         cost_estimate=cost(0, 12 * MIB),
         name="finish",
-    )(occupancy, live, features, cotangent, hat, coef)
-
-
-def wide_sum(values):
+    )(occupancy, live, features, cotangent, hat, coef, sums)
+
+
+def wide_round(values, step):
     count = lax.axis_size("wide")
-    step = 1
-    while step < count:
-        values = values + lax.ppermute(values, "wide", [(i, i ^ step) for i in range(count)])
-        step *= 2
-    return values
+    terms = [values]
+    for turn in range(1, 4):
+        route = [(i, i ^ (turn * step)) for i in range(count)]
+        terms.append(lax.ppermute(values, "wide", route))
+    return (terms[0] + terms[1]) + (terms[2] + terms[3])
 
 
 def group_sums(rows, channels):
@@ -701,40 +713,61 @@
     return jnp.dot(rows, same, precision=lax.Precision.HIGHEST)
 
 
-def scale_kernel(parts_ref, out_ref):
-    total = jnp.zeros((1, parts_ref.shape[-1]), f32)
+def scale_kernel(rows, parts_ref, coef_ref, out_ref, sums_ref):
+    channels = parts_ref.shape[-1]
+    tail = jnp.zeros((parts_ref.shape[1] - rows, channels), f32)
+    total = jnp.zeros((1, channels), f32)
     for part in range(parts_ref.shape[0]):
-        values = parts_ref[part].astype(f32)
+        values = parts_ref[part, 0:rows].astype(f32)
         total = total + jnp.sum(values * values, axis=0, keepdims=True)
+        tail = tail + parts_ref[part, rows:].astype(f32)
     mean = jnp.sum(total, axis=1, keepdims=True) / out_ref.size
     factor = lax.rsqrt(mean + step_eps)
     for part in range(parts_ref.shape[0]):
-        out_ref[part] = parts_ref[part].astype(f32) * factor
-
-
-def reduce_weights(grads, sums, tie):
+        out_ref[part] = parts_ref[part, 0:rows].astype(f32) * factor
+    first = tail[0:1] + tail[1:2] + tail[2:3]
+    second = tail[3:4] + tail[4:5] + tail[5:6]
+    both = jnp.concatenate([first, second] + [jnp.zeros_like(first)] * 6, axis=0)
+    row = lax.broadcasted_iota(jnp.int32, (channels, channels), 0) // (channels // G)
+    column = lax.broadcasted_iota(jnp.int32, (channels, channels), 1) // (channels // G)
+    same = (row == column).astype(f32)
+    grouped = jnp.dot(both, same, precision=lax.Precision.HIGHEST, preferred_element_type=f32)
+    sums_ref[...] = grouped / coef_ref[4:5, :]
+
+
+def reduce_weights(grads, sums, coef, tie):
     shape = grads.shape
+    channels = shape[2]
     wide, narrow = lax.axis_size("wide"), lax.axis_size("narrow")
     rows = shape[0] * shape[1] // wide
-    mine = jnp.sum(exchange(grads.reshape(wide, rows, shape[2]), "wide"), axis=0)
+    mine = jnp.sum(exchange(grads.reshape(wide, rows, channels), "wide"), axis=0)
     deep = -(-rows // (8 * narrow)) * 8
-    mine = jnp.pad(mine, ((0, deep * narrow - rows), (0, 0))).reshape(narrow, deep, shape[2])
+    mine = jnp.pad(mine, ((0, deep * narrow - rows), (0, 0))).reshape(narrow, deep, channels)
     sums = jnp.broadcast_to(sums[None], (narrow,) + sums.shape)
+    mine, tie = lax.optimization_barrier((mine, tie))
     mine = jnp.sum(exchange(jnp.concatenate([mine, sums], axis=1), "narrow"), axis=0)
-    mine, sums = mine[:deep], mine[deep:]
-    mine, sums, tie = lax.optimization_barrier((mine, sums, tie))
-    mine = exchange(jnp.broadcast_to(mine.astype(bf16)[None], (narrow, deep, shape[2])), "narrow")
-    mine = mine.reshape(narrow * deep, shape[2])[:rows]
+    mine, sums = mine[:deep], mine[deep : deep + 2]
+    mine = exchange(jnp.broadcast_to(mine.astype(bf16)[None], (narrow, deep, channels)), "narrow")
+    high = lax.reduce_precision(sums, 8, 7)
+    middle = lax.reduce_precision(sums - high, 8, 7)
+    low = (sums - high) - middle
+    tail = jnp.stack([high, middle, low], axis=1).reshape(6, channels).astype(bf16)
+    mine = mine.reshape(narrow * deep, channels)[:rows]
+    mine, tie = lax.optimization_barrier((mine, tie))
+    mine = jnp.concatenate([mine, tail, jnp.zeros((2, channels), bf16)], axis=0)
     parts = exchange(jnp.broadcast_to(mine[None], (wide,) + mine.shape), "wide")
-    step = pl.pallas_call(
-        scale_kernel,
-        out_shape=jax.ShapeDtypeStruct(parts.shape, f32),
-        in_specs=[VMEM],
-        out_specs=VMEM,
+    step, sums = pl.pallas_call(
+        functools.partial(scale_kernel, rows),
+        out_shape=(
+            jax.ShapeDtypeStruct((wide, rows, channels), f32),
+            jax.ShapeDtypeStruct((8, channels), f32),
+        ),
+        in_specs=[VMEM, VMEM],
+        out_specs=(VMEM, VMEM),
         compiler_params=params(16),
         cost_estimate=cost(0, 3 * MIB),
         name="scale",
-    )(parts)
+    )(parts, coef)
     return (step.reshape(shape), sums, tie)
 
 
@@ -775,9 +808,12 @@
     up_rows, _ = hub_stage(place, live_slots, neighbours, up_got, 0.0)
     up_rows, feat_got = lax.optimization_barrier((up_rows, feat_got))
     up_rim = exchange(up_rows, "narrow")
-    feat_rows, stats = hub_stage(place, live_slots, neighbours, feat_got, float("inf"))
-    stats = wide_sum(stats)
-    feat_rows, up_rim = lax.optimization_barrier((feat_rows, up_rim))
+    feat_rows, stats = hub_stage(place, live_slots, neighbours, feat_got, float("inf"), True)
+    feat_rows, up_rim, stats = lax.optimization_barrier((feat_rows, up_rim, stats))
+    step = 4
+    while step < lax.axis_size("wide"):
+        stats = wide_round(stats, step)
+        step *= 4
     feat_rim = exchange(feat_rows, "narrow")
 
     voxel_count = stats[2, 0] * group_width
@@ -785,19 +821,16 @@
     mean = sums[0] / voxel_count
     rstd = lax.rsqrt(sums[1] / voxel_count - mean * mean + norm_eps)
     blank = jnp.zeros((channels,), f32)
-    coef = jnp.stack([mean, rstd, scale, shift, blank, blank, blank, blank])
+    coef = jnp.stack([mean, rstd, scale, shift, blank + voxel_count, blank, blank, blank])
 
     grads, padded, shifted, hidden = weight_grad(occupancy, live, features, out_cotangent, up_rim, coef)
     grads, feat_rim = lax.optimization_barrier((grads, feat_rim))
     hat, grad_sums = back_conv(occupancy, live, features, padded, shifted, back_weight, coef)
     forward = (occupancy, live, features, hidden, feat_rim, forward_weight, coef, conv_bias[None, :])
     mixed = forward_conv(0, *forward)
-    weight_step, grad_sums, mixed = reduce_weights(grads, grad_sums, mixed)
-    grad_sums, mixed = lax.optimization_barrier((wide_sum(grad_sums), mixed))
-    grad_sums = group_sums(grad_sums[:2], channels) / voxel_count
+    weight_step, grad_sums, mixed = reduce_weights(grads, grad_sums, coef, mixed)
     mixed = forward_conv(1, *forward, base=mixed)
-    grad_coef = jnp.stack([mean, rstd, grad_sums[0], grad_sums[1], blank, blank, blank, blank])
-    feature_grad = finish(occupancy, live, features, out_cotangent, hat, grad_coef)
+    feature_grad = finish(occupancy, live, features, out_cotangent, hat, coef, grad_sums)
     return (mixed, feature_grad, weight_step)
 
 

time: 239 us -> 223 us (0.933)
  waiting for transfers between devices: 53.4 us -> 100 us
  Pallas kernels: 75.7 us -> 45 us
  local copies, waits for them, and re-layouts: 30.6 us -> 9.47 us
  starting transfers between devices: 72.3 us -> 61.6 us
    all_to_all x8, waiting for transfers between devices: 34.2 us -> 91.5 us  [exchange(): return lax.all_to_all(values, axis, split_axis=0, concat_axis=0, tiled=True)]
    unnamed x58 -> x22, local copies, waits for them, and re-layouts: 21.3 us -> 0.67 us
    pallas_call x1, Pallas kernels: 17.7 us -> 4.44 us  [back_conv(): pl.pallas_call(functools.partial(back_kernel, edge), grid=(2,), out_shape...]
    ppermute x8 -> x6, waiting for transfers between devices: 12.4 us -> 0.02 us  [wide_round(): terms.append(lax.ppermute(values, 'wide', route))]
    pallas_call x2, Pallas kernels: 17.6 us -> 6.01 us  [forward_conv(): pl.pallas_call(functools.partial(forward_kernel, edge, slot), grid=(1,),...]
    pallas_call x1, Pallas kernels: 15.5 us -> 4.82 us  [weight_grad(): pl.pallas_call(functools.partial(weight_kernel, edge), grid=(2,), out_sha...]
    all_to_all x8, starting transfers between devices: 54.1 us -> 44.1 us  [exchange(): return lax.all_to_all(values, axis, split_axis=0, concat_axis=0, tiled=True)]
    pallas_call x2, Pallas kernels: 5.56 us -> 8.57 us  [the longest x1 6.93 us: finish(): pl.pallas_call(functools.partial(finish_kernel, edge), grid=(2, 4), out_s...]
  transfers between devices with their start and end apart: 20 -> 18, of which waited for: 14 -> 12; matrix products, arithmetic and copies ran while one was open for 4% -> 4% of each run, Pallas kernels for 30% -> 15%
where the time goes in v2:
time: 223 us; the launch traced here: 221 us
  waiting for transfers between devices  100 us (45%)
  starting transfers between devices  61.6 us (28%)
  Pallas kernels  45 us (20%)
  local copies, waits for them, and re-layouts  9.47 us (4%)
  between operations  2.3 us (1%)
    all_to_all x8, waiting for transfers between devices, exchange(): return lax.all_to_all(values, axis, split_axis=0, concat_axis=0, tiled=True)  91.5 us
    all_to_all x8, starting transfers between devices, exchange(): return lax.all_to_all(values, axis, split_axis=0, concat_axis=0, tiled=True)  44.1 us
    pallas_call x2, Pallas kernels, surface(): pl.pallas_call(functools.partial(surface_kernel, edge, with_stats, fill),...  10.4 us
    pallas_call x2, Pallas kernels, hub_rows(): pl.pallas_call(functools.partial(hub_kernel, edge, fill), out_shape=jax.S...  8.89 us
    ppermute x6, starting transfers between devices, wide_round(): terms.append(lax.ppermute(values, 'wide', route))  8.6 us
    ppermute x2, waiting for transfers between devices, hub_stage(): lax.ppermute(to_left, 'wide', [(i + 1, i) for i in range(count - 1)])  7.81 us
    pallas_call x1, Pallas kernels, finish(): pl.pallas_call(functools.partial(finish_kernel, edge), grid=(2, 4), out_s...  6.93 us
    ppermute x2, starting transfers between devices, hub_stage(): lax.ppermute(to_right, 'wide', [(i, i + 1) for i in range(count - 1)])  6.4 us
  transfers between devices with their start and end apart: 18, of which 12 were waited for; matrix products, arithmetic and copies ran while one was open for 4% of the time, Pallas kernels for 15%

profile of v2, /device:TPU:1, one launch (start us, length us, event | category | flops | bytes accessed | tf_op | source)
XLA Modules:
  0.0 220.8 jit_solution(15840022872670788855)
XLA Ops:
  0.6 0.0 copy-start
  0.6 4.4 %surface.3 = bf16[16,13,16,128]{3,2,1,0:T(8,128)(2,1)} custom-call(s32[2,16,16]{2,1,0:T(8,128)} %occ_ref.13, bf16[2,16,256,128]{3,2,1,0:T(8,128)(2,1)} %g_ref.3), custom_call_target="tpu_custom_call" | custom-call | bytes 3145728 | tf_op jit(solution)/shard_map/surface/pallas_call | solution.py:128
  5.0 10.1 %all-to-all-start = ((bf16[16,13,16,128]{3,2,1,0:T(8,128)(2,1)}), bf16[16,13,16,128]{3,2,1,0:T(8,128)(2,1)S(1)}, u32[]{:S(2)}, u32[]{:S(2)}) async-start(bf16[16,13,16,128]{3,2,1,0:T(8,128)(2,1)} %surface.3), calls=%async_computation | async-start | bytes 1703936 | tf_op jit(solution)/shard_map/all_to_all | solution.py:271
  15.2 6.0 %surface.2 = bf16[16,13,16,128]{3,2,1,0:T(8,128)(2,1)} custom-call(s32[2,16,16]{2,1,0:T(8,128)} %occ_ref.13, bf16[2,16,256,128]{3,2,1,0:T(8,128)(2,1)} %f_ref.9), custom_call_target="tpu_custom_call" | custom-call | bytes 3145728 | tf_op jit(solution)/shard_map/surface/pallas_call | solution.py:128
  21.2 1.0 rev.3
  22.1 2.4 %copy.23 = bf16[9,3,128,128]{2,1,3,0:T(4,128)(2,1)S(1)} copy(bf16[9,3,128,128]{3,2,1,0:T(8,128)(2,1)} %bitcast.38) | data formatting | bytes 1769472 | tf_op jit(solution)/shard_map/reshape | solution.py:796
  24.6 0.8 copy.22
  26.1 0.2 fusion.12
  26.3 0.0 copy-done.10
  26.3 0.0 copy-start.3
  26.3 1.7 copy_bitcast_fusion
  28.0 11.1 %all-to-all-done.got_ref = bf16[16,13,16,128]{3,2,1,0:T(8,128)(2,1)S(1)} async-done(((bf16[16,13,16,128]{3,2,1,0:T(8,128)(2,1)}), bf16[16,13,16,128]{3,2,1,0:T(8,128)(2,1)S(1)}, u32[]{:S(2)}, u32[]{:S(2)}) %all-to-all-start) | async-done | bytes 852000 | tf_op jit(solution)/shard_map/all_to_all | solution.py:271
  39.1 3.5 %all-to-all-start.1 = ((bf16[16,13,16,128]{3,2,1,0:T(8,128)(2,1)}), bf16[16,13,16,128]{3,2,1,0:T(8,128)(2,1)S(1)}, u32[]{:S(2)}, u32[]{:S(2)}) async-start(bf16[16,13,16,128]{3,2,1,0:T(8,128)(2,1)} %surface.2), calls=%async_computation.1 | async-start | bytes 1703936 | tf_op jit(solution)/shard_map/all_to_all | solution.py:271
  42.7 1.2 trade.2
  43.9 3.2 %collective-permute-start = (bf16[18,16,128]{2,1,0:T(8,128)(2,1)S(1)}, bf16[18,16,128]{2,1,0:T(8,128)(2,1)S(1)}, u32[]{:S(2)}, u32[]{:S(2)}) collective-permute-start(bf16[18,16,128]{2,1,0:T(8,128)(2,1)S(1)} %get-tuple-element.37), channel_id=1, source_target_pairs={{0,16},{16,32},{32,48},{48,64},{64,80},{80,96},{96,112},{112,128},... | collective-permute-start | bytes 221192 | tf_op jit(solution)/shard_map/ppermute | solution.py:277
  47.1 1.3 collective-permute-start.1
  48.4 0.1 pad_add_fusion.place_ref
  48.5 0.4 collective-permute-done.lower_ref
  48.9 3.9 %collective-permute-done.1.upper_ref = bf16[18,16,128]{2,1,0:T(8,128)(2,1)S(1)} collective-permute-done((bf16[18,16,128]{2,1,0:T(8,128)(2,1)S(1)}, bf16[18,16,128]{2,1,0:T(8,128)(2,1)S(1)}, u32[]{:S(2)}, u32[]{:S(2)}) %collective-permute-start.1) | collective-permute-done | bytes 73760 | tf_op jit(solution)/shard_map/ppermute | solution.py:278
  52.7 4.4 %hub_rows.2 = bf16[16,2,7,16,128]{4,3,2,1,0:T(8,128)(2,1)} custom-call(s32[2]{0:T(128)S(1)} %pad_add_fusion.place_ref, s32[1,16]{1,0:T(1,128)S(1)} %copy-done.3, s32[16,27]{1,0:T(8,128)S(1)} %copy-done.2, bf16[16,13,16,128]{3,2,1,0:T(8,128)(2,1)S(1)} %all-to-all-done.got_ref, bf16[18,16,128]{2,1,0:T(8,128)(2,1)S(1)} %collective-permute-done.lower_ref, ...), custom_call_target="tpu_custom_call" | custom-call | bytes 8388608 | tf_op jit(solution)/shard_map/hub_rows/pallas_call | solution.py:255
  57.2 9.2 %all-to-all-done.1.got_ref = bf16[16,13,16,128]{3,2,1,0:T(8,128)(2,1)S(1)} async-done(((bf16[16,13,16,128]{3,2,1,0:T(8,128)(2,1)}), bf16[16,13,16,128]{3,2,1,0:T(8,128)(2,1)S(1)}, u32[]{:S(2)}, u32[]{:S(2)}) %all-to-all-start.1) | async-done | bytes 852000 | tf_op jit(solution)/shard_map/all_to_all | solution.py:271
  66.4 3.5 %all-to-all-start.2 = ((bf16[16,2,7,16,128]{4,3,2,1,0:T(8,128)(2,1)}), bf16[16,2,7,16,128]{4,3,2,1,0:T(8,128)(2,1)S(1)}, u32[]{:S(2)}, u32[]{:S(2)}) async-start(bf16[16,2,7,16,128]{4,3,2,1,0:T(8,128)(2,1)} %hub_rows.2), calls=%async_computation.2 | async-start | bytes 1835008 | tf_op jit(solution)/shard_map/all_to_all | solution.py:271
  69.9 0.6 trade.3
  70.6 3.2 %collective-permute-start.2 = (bf16[18,16,128]{2,1,0:T(8,128)(2,1)S(1)}, bf16[18,16,128]{2,1,0:T(8,128)(2,1)S(1)}, u32[]{:S(2)}, u32[]{:S(2)}) collective-permute-start(bf16[18,16,128]{2,1,0:T(8,128)(2,1)S(1)} %get-tuple-element.42), channel_id=1, source_target_pairs={{0,16},{16,32},{32,48},{48,64},{64,80},{80,96},{96,112},{112,128},... | collective-permute-start | bytes 221192 | tf_op jit(solution)/shard_map/ppermute | solution.py:277
  73.8 1.3 collective-permute-start.3
  75.1 0.5 collective-permute-done.2.lower_ref
  75.6 3.9 %collective-permute-done.3.upper_ref = bf16[18,16,128]{2,1,0:T(8,128)(2,1)S(1)} collective-permute-done((bf16[18,16,128]{2,1,0:T(8,128)(2,1)S(1)}, bf16[18,16,128]{2,1,0:T(8,128)(2,1)S(1)}, u32[]{:S(2)}, u32[]{:S(2)}) %collective-permute-start.3) | collective-permute-done | bytes 73760 | tf_op jit(solution)/shard_map/ppermute | solution.py:278
  79.5 2.6 %collective-permute-start.5 = (f32[8,128]{1,0:T(8,128)S(1)}, f32[8,128]{1,0:T(8,128)S(1)}, u32[]{:S(2)}, u32[]{:S(2)}) collective-permute-start(f32[8,128]{1,0:T(8,128)S(1)} %get-tuple-element.47), channel_id=1, source_target_pairs={{0,32},{16,48},{32,0},{48,16},{64,96},{80,112},{96,64},{112,80},{1... | collective-permute-start | bytes 12296 | tf_op jit(solution)/shard_map/ppermute | solution.py:705
  82.1 1.8 collective-permute-start.6
  83.9 0.6 collective-permute-start.4
  84.5 0.2 compare_reduce_fusion
  84.7 4.4 %hub_rows.3 = bf16[16,2,7,16,128]{4,3,2,1,0:T(8,128)(2,1)} custom-call(s32[2]{0:T(128)S(1)} %pad_add_fusion.place_ref, s32[1,16]{1,0:T(1,128)S(1)} %copy-done.3, s32[16,27]{1,0:T(8,128)S(1)} %copy-done.2, bf16[16,13,16,128]{3,2,1,0:T(8,128)(2,1)S(1)} %all-to-all-done.1.got_ref, bf16[18,16,128]{2,1,0:T(8,128)(2,1)S(1)} %collective-permute-done.2.lower_ref, ...), custom_call_target="tpu_custom_call" | custom-call | bytes 8388608 | tf_op jit(solution)/shard_map/hub_rows/pallas_call | solution.py:255
  89.2 5.8 %all-to-all-done.2.rim_ref = bf16[16,2,7,16,128]{4,3,2,1,0:T(8,128)(2,1)S(1)} async-done(((bf16[16,2,7,16,128]{4,3,2,1,0:T(8,128)(2,1)}), bf16[16,2,7,16,128]{4,3,2,1,0:T(8,128)(2,1)S(1)}, u32[]{:S(2)}, u32[]{:S(2)}) %all-to-all-start.2) | async-done | bytes 917536 | tf_op jit(solution)/shard_map/all_to_all | solution.py:271
  94.9 2.7 %collective-permute-start.8 = (f32[8,128]{1,0:T(8,128)S(1)}, f32[8,128]{1,0:T(8,128)S(1)}, u32[]{:S(2)}, u32[]{:S(2)}) collective-permute-start(f32[8,128]{1,0:T(8,128)S(1)} %add_add_fusion.1), channel_id=1, source_target_pairs={{0,128},{16,144},{32,160},{48,176},{64,192},{80,208},{96,224},{112... | collective-permute-start | bytes 12296 | tf_op jit(solution)/shard_map/ppermute | solution.py:705
  97.7 0.9 collective-permute-start.9
  98.6 0.5 convert_element_type.17.live_ref
  99.1 3.9 %all-to-all-start.3 = ((bf16[16,2,7,16,128]{4,3,2,1,0:T(8,128)(2,1)}), bf16[16,2,7,16,128]{4,3,2,1,0:T(8,128)(2,1)S(1)}, u32[]{:S(2)}, u32[]{:S(2)}) async-start(bf16[16,2,7,16,128]{4,3,2,1,0:T(8,128)(2,1)} %hub_rows.3), calls=%async_computation.3 | async-start | bytes 1835008 | tf_op jit(solution)/shard_map/all_to_all | solution.py:271
  103.0 0.0 collective-permute-done.8
  103.0 0.0 collective-permute-done.7
  103.1 0.5 slice.33
  103.6 0.2 fusion
  104.5 0.6 stack.46.coef_ref
  105.1 4.8 %weight_grad.1 = (f32[27,128,128]{2,1,0:T(8,128)}, bf16[2,18,18,16,128]{4,3,2,1,0:T(8,128)(2,1)}, bf16[2,2,3,18,16,128]{5,4,3,2,1,0:T(8,128)(2,1)}, bf16[2,16,256,128]{3,2,1,0:T(8,128)(2,1)}) custom-call(s32[2,16,16]{2,1,0:T(8,128)} %occ_ref.13, s32[2]{0:T(128)} %convert_element_type.17.live_ref, bf16[2,16,256,128]{3,2,1,0:T(8,128)(2,1)} %f_ref.9, ...), custom_call_target="tpu_custom_call" | custom-call | flops 20000000000 | bytes 8388608 | tf_op jit(solution)/shard_map/weight_grad/pallas_call | solution.py:430
  109.9 18.4 %all-to-all-done.3.rim_ref = bf16[16,2,7,16,128]{4,3,2,1,0:T(8,128)(2,1)S(1)} async-done(((bf16[16,2,7,16,128]{4,3,2,1,0:T(8,128)(2,1)}), bf16[16,2,7,16,128]{4,3,2,1,0:T(8,128)(2,1)S(1)}, u32[]{:S(2)}, u32[]{:S(2)}) %all-to-all-start.3) | async-done | bytes 917536 | tf_op jit(solution)/shard_map/all_to_all | solution.py:271
  128.3 7.3 %all-to-all-start.4 = ((f32[16,216,128]{2,1,0:T(8,128)}), f32[16,216,128]{2,1,0:T(8,128)S(1)}, u32[]{:S(2)}, u32[]{:S(2)}) async-start(f32[16,216,128]{2,1,0:T(8,128)} %bitcast.39), calls=%async_computation.4 | async-start | bytes 3538944 | tf_op jit(solution)/shard_map/all_to_all | solution.py:271
  135.6 4.4 %back_conv.1 = (f32[2,16,256,128]{3,2,1,0:T(8,128)}, f32[8,128]{1,0:T(8,128)}) custom-call(s32[2,16,16]{2,1,0:T(8,128)} %occ_ref.13, s32[2]{0:T(128)} %convert_element_type.17.live_ref, bf16[2,16,256,128]{3,2,1,0:T(8,128)(2,1)} %f_ref.9, bf16[2,18,18,16,128]{4,3,2,1,0:T(8,128)(2,1)} %get-tuple-element.59.pad_ref, ...), custom_call_target="tpu_custom_call" | custom-call | flops 20000000000 | bytes 8388608 | tf_op jit(solution)/shard_map/back_conv/pallas_call | solution.py:573
  140.0 3.0 %forward_conv.2.refs_0_ = bf16[2,16,256,128]{3,2,1,0:T(8,128)(2,1)} custom-call(s32[2,16,16]{2,1,0:T(8,128)} %occ_ref.13, s32[2]{0:T(128)} %convert_element_type.17.live_ref, bf16[2,16,256,128]{3,2,1,0:T(8,128)(2,1)} %f_ref.9, bf16[2,16,256,128]{3,2,1,0:T(8,128)(2,1)} %get-tuple-element.52.hid_ref, bf16[16,2,7,16,128]{4,3,2,1,0:T(8,128)(2,1)} %copy-done.6, ...), custom_call_target="tpu_custom_call" | custom-call | flops 10000000000 | bytes 4194304 | tf_op jit(solution)/shard_map/forward_conv/pallas_call | solution.py:634
  143.1 18.8 %all-to-all-done.4 = f32[16,216,128]{2,1,0:T(8,128)S(1)} async-done(((f32[16,216,128]{2,1,0:T(8,128)}), f32[16,216,128]{2,1,0:T(8,128)S(1)}, u32[]{:S(2)}, u32[]{:S(2)}) %all-to-all-start.4) | async-done | bytes 1769504 | tf_op jit(solution)/shard_map/all_to_all | solution.py:271
  161.8 0.1 reduce_sum.18
  162.0 0.7 pad_maximum_fusion
  162.7 5.6 %all-to-all-start.5 = ((f32[16,24,128]{2,1,0:T(8,128)}), f32[16,24,128]{2,1,0:T(8,128)S(1)}, u32[]{:S(2)}, u32[]{:S(2)}) async-start(f32[16,24,128]{2,1,0:T(8,128)} %pad_maximum_fusion), calls=%async_computation.5 | async-start | bytes 393216 | tf_op jit(solution)/shard_map/all_to_all | solution.py:271
  168.2 0.1 pad.7.clone
  168.3 10.2 %all-to-all-done.5 = f32[16,24,128]{2,1,0:T(8,128)S(1)} async-done(((f32[16,24,128]{2,1,0:T(8,128)}), f32[16,24,128]{2,1,0:T(8,128)S(1)}, u32[]{:S(2)}, u32[]{:S(2)}) %all-to-all-start.5) | async-done | bytes 196640 | tf_op jit(solution)/shard_map/all_to_all | solution.py:271
  178.6 0.6 broadcast_in_dim.12
  179.2 3.4 %all-to-all-start.6 = ((bf16[16,16,128]{2,1,0:T(8,128)(2,1)}), bf16[16,16,128]{2,1,0:T(8,128)(2,1)S(1)}, u32[]{:S(2)}, u32[]{:S(2)}) async-start(bf16[16,16,128]{2,1,0:T(8,128)(2,1)} %broadcast_in_dim.12), calls=%async_computation.6 | async-start | bytes 131072 | tf_op jit(solution)/shard_map/all_to_all | solution.py:271
  182.7 7.3 %all-to-all-done.6 = bf16[16,16,128]{2,1,0:T(8,128)(2,1)S(1)} async-done(((bf16[16,16,128]{2,1,0:T(8,128)(2,1)}), bf16[16,16,128]{2,1,0:T(8,128)(2,1)S(1)}, u32[]{:S(2)}, u32[]{:S(2)}) %all-to-all-start.6) | async-done | bytes 65568 | tf_op jit(solution)/shard_map/all_to_all | solution.py:271
  190.0 0.1 maximum_maximum_fusion
  190.1 1.0 broadcast_in_dim.14
  191.1 6.7 %all-to-all-start.7 = ((bf16[16,224,128]{2,1,0:T(8,128)(2,1)}), bf16[16,224,128]{2,1,0:T(8,128)(2,1)S(1)}, u32[]{:S(2)}, u32[]{:S(2)}) async-start(bf16[16,224,128]{2,1,0:T(8,128)(2,1)} %broadcast_in_dim.14), calls=%async_computation.7 | async-start | bytes 1835008 | tf_op jit(solution)/shard_map/all_to_all | solution.py:271
  197.9 3.0 %forward_conv.3 = bf16[2,16,256,128]{3,2,1,0:T(8,128)(2,1)} custom-call(s32[2,16,16]{2,1,0:T(8,128)} %occ_ref.13, s32[2]{0:T(128)} %convert_element_type.17.live_ref, bf16[2,16,256,128]{3,2,1,0:T(8,128)(2,1)} %f_ref.9, bf16[2,16,256,128]{3,2,1,0:T(8,128)(2,1)} %get-tuple-element.52.hid_ref, ...), custom_call_target="tpu_custom_call", output_to_operand_aliasing={{}: (8, {})} | custom-call | flops 10000000000 | bytes 4194304 | tf_op jit(solution)/shard_map/forward_conv/pallas_call | solution.py:634
  200.9 10.8 %all-to-all-done.7.parts_ref = bf16[16,224,128]{2,1,0:T(8,128)(2,1)S(1)} async-done(((bf16[16,224,128]{2,1,0:T(8,128)(2,1)}), bf16[16,224,128]{2,1,0:T(8,128)(2,1)S(1)}, u32[]{:S(2)}, u32[]{:S(2)}) %all-to-all-start.7) | async-done | bytes 917536 | tf_op jit(solution)/shard_map/all_to_all | solution.py:271
  211.6 1.6 scale.1
  213.3 0.6 copy-done.4
  213.9 6.9 %finish.1 = bf16[2,16,256,128]{3,2,1,0:T(8,128)(2,1)} custom-call(s32[2,16,16]{2,1,0:T(8,128)} %occ_ref.13, s32[2]{0:T(128)} %convert_element_type.17.live_ref, bf16[2,16,256,128]{3,2,1,0:T(8,128)(2,1)} %f_ref.9, bf16[2,16,256,128]{3,2,1,0:T(8,128)(2,1)} %g_ref.3, f32[2,16,256,128]{3,2,1,0:T(8,128)} %get-tuple-element.65.hat_ref, f32[8,128]{1,0:T(8,128)} %stack.46.coef_ref, ...), custom_call_target="tpu_custom_call" | custom-call | bytes 12582912 | tf_op jit(solution)/shard_map/finish/pallas_call | solution.py:688
  (44 shorter events, 0.2 us)
Async XLA Ops:
  0.6 25.4 %copy-start = (f32[256,256]{1,0:T(8,128)S(1)}, f32[256,256]{1,0:T(8,128)}, u32[]{:S(2)}) copy-start(f32[256,256]{1,0:T(8,128)} %param.19) | copy-start | bytes 786436
  5.0 16.1 %copy-start.5 = (bf16[27,128,128]{2,1,0:T(8,128)(2,1)S(1)}, bf16[27,128,128]{2,1,0:T(8,128)(2,1)}, u32[]{:S(2)}) copy-start(bf16[27,128,128]{2,1,0:T(8,128)(2,1)} %param.20) | copy-start | bytes 2654212
  5.0 34.1 %all-to-all-start = ((bf16[16,13,16,128]{3,2,1,0:T(8,128)(2,1)}), bf16[16,13,16,128]{3,2,1,0:T(8,128)(2,1)S(1)}, u32[]{:S(2)}, u32[]{:S(2)}) async-start(bf16[16,13,16,128]{3,2,1,0:T(8,128)(2,1)} %surface.3), calls=%async_computation | async-start | bytes 1703936 | tf_op jit(solution)/shard_map/all_to_all | solution.py:271
  22.1 4.1 %copy-start.9 = (f32[128]{0:T(128)S(1)}, f32[128]{0:T(128)}, u32[]{:S(2)}) copy-start(f32[128]{0:T(128)} %param.18) | copy-start | bytes 1540
  22.1 4.2 %copy-start.10 = (f32[128]{0:T(128)S(1)}, f32[128]{0:T(128)}, u32[]{:S(2)}) copy-start(f32[128]{0:T(128)} %param.17) | copy-start | bytes 1540
  26.3 16.3 %copy-start.3 = (s32[1,16]{1,0:T(1,128)S(1)}, s32[1,16]{1,0:T(1,128)}, u32[]{:S(2)}) copy-start(s32[1,16]{1,0:T(1,128)} %live_ref.7) | copy-start | bytes 196
  28.0 24.7 %copy-start.2 = (s32[16,27]{1,0:T(8,128)S(1)}, s32[16,27]{1,0:T(8,128)}, u32[]{:S(2)}) copy-start(s32[16,27]{1,0:T(8,128)} %near_ref.3) | copy-start | bytes 5188
  39.1 27.2 %all-to-all-start.1 = ((bf16[16,13,16,128]{3,2,1,0:T(8,128)(2,1)}), bf16[16,13,16,128]{3,2,1,0:T(8,128)(2,1)S(1)}, u32[]{:S(2)}, u32[]{:S(2)}) async-start(bf16[16,13,16,128]{3,2,1,0:T(8,128)(2,1)} %surface.2), calls=%async_computation.1 | async-start | bytes 1703936 | tf_op jit(solution)/shard_map/all_to_all | solution.py:271
  43.9 5.0 %collective-permute-start = (bf16[18,16,128]{2,1,0:T(8,128)(2,1)S(1)}, bf16[18,16,128]{2,1,0:T(8,128)(2,1)S(1)}, u32[]{:S(2)}, u32[]{:S(2)}) collective-permute-start(bf16[18,16,128]{2,1,0:T(8,128)(2,1)S(1)} %get-tuple-element.37), channel_id=1, source_target_pairs={{0,16},{16,32},{32,48},{48,64},{64,80},{80,96},{96,112},{112,128},... | collective-permute-start | bytes 221192 | tf_op jit(solution)/shard_map/ppermute | solution.py:277
  47.1 5.6 %collective-permute-start.1 = (bf16[18,16,128]{2,1,0:T(8,128)(2,1)S(1)}, bf16[18,16,128]{2,1,0:T(8,128)(2,1)S(1)}, u32[]{:S(2)}, u32[]{:S(2)}) collective-permute-start(bf16[18,16,128]{2,1,0:T(8,128)(2,1)S(1)} %get-tuple-element.38), channel_id=1, source_target_pairs={{16,0},{32,16},{48,32},{64,48},{80,64},{96,80},{112,96},{128,112},... | collective-permute-start | bytes 221192 | tf_op jit(solution)/shard_map/ppermute | solution.py:278
  66.4 28.6 %all-to-all-start.2 = ((bf16[16,2,7,16,128]{4,3,2,1,0:T(8,128)(2,1)}), bf16[16,2,7,16,128]{4,3,2,1,0:T(8,128)(2,1)S(1)}, u32[]{:S(2)}, u32[]{:S(2)}) async-start(bf16[16,2,7,16,128]{4,3,2,1,0:T(8,128)(2,1)} %hub_rows.2), calls=%async_computation.2 | async-start | bytes 1835008 | tf_op jit(solution)/shard_map/all_to_all | solution.py:271
  70.6 5.0 %collective-permute-start.2 = (bf16[18,16,128]{2,1,0:T(8,128)(2,1)S(1)}, bf16[18,16,128]{2,1,0:T(8,128)(2,1)S(1)}, u32[]{:S(2)}, u32[]{:S(2)}) collective-permute-start(bf16[18,16,128]{2,1,0:T(8,128)(2,1)S(1)} %get-tuple-element.42), channel_id=1, source_target_pairs={{0,16},{16,32},{32,48},{48,64},{64,80},{80,96},{96,112},{112,128},... | collective-permute-start | bytes 221192 | tf_op jit(solution)/shard_map/ppermute | solution.py:277
  73.8 5.7 %collective-permute-start.3 = (bf16[18,16,128]{2,1,0:T(8,128)(2,1)S(1)}, bf16[18,16,128]{2,1,0:T(8,128)(2,1)S(1)}, u32[]{:S(2)}, u32[]{:S(2)}) collective-permute-start(bf16[18,16,128]{2,1,0:T(8,128)(2,1)S(1)} %get-tuple-element.43), channel_id=1, source_target_pairs={{16,0},{32,16},{48,32},{64,48},{80,64},{96,80},{112,96},{128,112},... | collective-permute-start | bytes 221192 | tf_op jit(solution)/shard_map/ppermute | solution.py:278
  79.5 9.6 %collective-permute-start.5 = (f32[8,128]{1,0:T(8,128)S(1)}, f32[8,128]{1,0:T(8,128)S(1)}, u32[]{:S(2)}, u32[]{:S(2)}) collective-permute-start(f32[8,128]{1,0:T(8,128)S(1)} %get-tuple-element.47), channel_id=1, source_target_pairs={{0,32},{16,48},{32,0},{48,16},{64,96},{80,112},{96,64},{112,80},{1... | collective-permute-start | bytes 12296 | tf_op jit(solution)/shard_map/ppermute | solution.py:705
  82.1 7.0 %collective-permute-start.6 = (f32[8,128]{1,0:T(8,128)S(1)}, f32[8,128]{1,0:T(8,128)S(1)}, u32[]{:S(2)}, u32[]{:S(2)}) collective-permute-start(f32[8,128]{1,0:T(8,128)S(1)} %get-tuple-element.47), channel_id=1, source_target_pairs={{0,48},{16,32},{32,16},{48,0},{64,112},{80,96},{96,80},{112,64},{1... | collective-permute-start | bytes 12296 | tf_op jit(solution)/shard_map/ppermute | solution.py:705
  83.9 5.2 %collective-permute-start.4 = (f32[8,128]{1,0:T(8,128)S(1)}, f32[8,128]{1,0:T(8,128)S(1)}, u32[]{:S(2)}, u32[]{:S(2)}) collective-permute-start(f32[8,128]{1,0:T(8,128)S(1)} %get-tuple-element.47), channel_id=1, source_target_pairs={{0,16},{16,0},{32,48},{48,32},{64,80},{80,64},{96,112},{112,96},{1... | collective-permute-start | bytes 12296 | tf_op jit(solution)/shard_map/ppermute | solution.py:705
  94.9 4.2 %copy-start.7 = (bf16[16,2,7,16,128]{4,3,2,1,0:T(8,128)(2,1)}, bf16[16,2,7,16,128]{4,3,2,1,0:T(8,128)(2,1)S(1)}, u32[]{:S(2)}) copy-start(bf16[16,2,7,16,128]{4,3,2,1,0:T(8,128)(2,1)S(1)} %all-to-all-done.2.rim_ref) | copy-start | bytes 2752516
  94.9 8.1 %collective-permute-start.8 = (f32[8,128]{1,0:T(8,128)S(1)}, f32[8,128]{1,0:T(8,128)S(1)}, u32[]{:S(2)}, u32[]{:S(2)}) collective-permute-start(f32[8,128]{1,0:T(8,128)S(1)} %add_add_fusion.1), channel_id=1, source_target_pairs={{0,128},{16,144},{32,160},{48,176},{64,192},{80,208},{96,224},{112... | collective-permute-start | bytes 12296 | tf_op jit(solution)/shard_map/ppermute | solution.py:705
  97.7 5.3 %collective-permute-start.9 = (f32[8,128]{1,0:T(8,128)S(1)}, f32[8,128]{1,0:T(8,128)S(1)}, u32[]{:S(2)}, u32[]{:S(2)}) collective-permute-start(f32[8,128]{1,0:T(8,128)S(1)} %add_add_fusion.1), channel_id=1, source_target_pairs={{0,192},{16,208},{32,224},{48,240},{64,128},{80,144},{96,160},{112... | collective-permute-start | bytes 12296 | tf_op jit(solution)/shard_map/ppermute | solution.py:705
  98.6 4.5 %collective-permute-start.7 = (f32[8,128]{1,0:T(8,128)S(1)}, f32[8,128]{1,0:T(8,128)S(1)}, u32[]{:S(2)}, u32[]{:S(2)}) collective-permute-start(f32[8,128]{1,0:T(8,128)S(1)} %add_add_fusion.1), channel_id=1, source_target_pairs={{0,64},{16,80},{32,96},{48,112},{64,0},{80,16},{96,32},{112,48},{1... | collective-permute-start | bytes 12296 | tf_op jit(solution)/shard_map/ppermute | solution.py:705
  99.1 29.2 %all-to-all-start.3 = ((bf16[16,2,7,16,128]{4,3,2,1,0:T(8,128)(2,1)}), bf16[16,2,7,16,128]{4,3,2,1,0:T(8,128)(2,1)S(1)}, u32[]{:S(2)}, u32[]{:S(2)}) async-start(bf16[16,2,7,16,128]{4,3,2,1,0:T(8,128)(2,1)} %hub_rows.3), calls=%async_computation.3 | async-start | bytes 1835008 | tf_op jit(solution)/shard_map/all_to_all | solution.py:271
  128.3 11.7 %copy-start.6 = (bf16[16,2,7,16,128]{4,3,2,1,0:T(8,128)(2,1)}, bf16[16,2,7,16,128]{4,3,2,1,0:T(8,128)(2,1)S(1)}, u32[]{:S(2)}) copy-start(bf16[16,2,7,16,128]{4,3,2,1,0:T(8,128)(2,1)S(1)} %all-to-all-done.3.rim_ref) | copy-start | bytes 2752516
  128.3 33.5 %all-to-all-start.4 = ((f32[16,216,128]{2,1,0:T(8,128)}), f32[16,216,128]{2,1,0:T(8,128)S(1)}, u32[]{:S(2)}, u32[]{:S(2)}) async-start(f32[16,216,128]{2,1,0:T(8,128)} %bitcast.39), calls=%async_computation.4 | async-start | bytes 3538944 | tf_op jit(solution)/shard_map/all_to_all | solution.py:271
  143.1 18.9 %copy-start.8 = (f32[8,128]{1,0:T(8,128)S(1)}, f32[8,128]{1,0:T(8,128)}, u32[]{:S(2)}) copy-start(f32[8,128]{1,0:T(8,128)} %get-tuple-element.62) | copy-start | bytes 12292
  162.7 15.9 %all-to-all-start.5 = ((f32[16,24,128]{2,1,0:T(8,128)}), f32[16,24,128]{2,1,0:T(8,128)S(1)}, u32[]{:S(2)}, u32[]{:S(2)}) async-start(f32[16,24,128]{2,1,0:T(8,128)} %pad_maximum_fusion), calls=%async_computation.5 | async-start | bytes 393216 | tf_op jit(solution)/shard_map/all_to_all | solution.py:271
  179.2 10.7 %all-to-all-start.6 = ((bf16[16,16,128]{2,1,0:T(8,128)(2,1)}), bf16[16,16,128]{2,1,0:T(8,128)(2,1)S(1)}, u32[]{:S(2)}, u32[]{:S(2)}) async-start(bf16[16,16,128]{2,1,0:T(8,128)(2,1)} %broadcast_in_dim.12), calls=%async_computation.6 | async-start | bytes 131072 | tf_op jit(solution)/shard_map/all_to_all | solution.py:271
  191.1 20.5 %all-to-all-start.7 = ((bf16[16,224,128]{2,1,0:T(8,128)(2,1)}), bf16[16,224,128]{2,1,0:T(8,128)(2,1)S(1)}, u32[]{:S(2)}, u32[]{:S(2)}) async-start(bf16[16,224,128]{2,1,0:T(8,128)(2,1)} %broadcast_in_dim.14), calls=%async_computation.7 | async-start | bytes 1835008 | tf_op jit(solution)/shard_map/all_to_all | solution.py:271
  197.8 13.8 %copy-start.1 = (f32[8,128]{1,0:T(8,128)S(1)}, f32[8,128]{1,0:T(8,128)}, u32[]{:S(2)}) copy-start(f32[8,128]{1,0:T(8,128)} %stack.46.coef_ref) | copy-start | bytes 12292
  213.3 0.6 copy-start.4

commit v3 on v2

--- a/solution.py
+++ b/solution.py
@@ -277,8 +277,8 @@
     lower = lax.ppermute(to_right, "wide", [(i, i + 1) for i in range(count - 1)])
     upper = lax.ppermute(to_left, "wide", [(i + 1, i) for i in range(count - 1)])
     if with_stats:
-        stats, lower, upper = lax.optimization_barrier((stats, lower, upper))
-        stats = wide_round(stats, 1)
+        stats, lower, upper = lax.optimization_barrier((wide_round(stats, 1), lower, upper))
+        stats = wide_round(stats, 4)
     return (hub_rows(place, live_slots, neighbours, got, lower, upper, fill), stats)
 
 
@@ -480,7 +480,7 @@
         side_s[side] = jnp.dot(rows, w_ref[:, first : first + channels], preferred_element_type=f32)
 
 
-DEPTH = 2
+DEPTH = 4
 
 
 def conv_pipeline(edge, pad_ref, pad_lead, w_ref, side_s, found_s, finish_plane, carry):
@@ -518,7 +518,8 @@
 
     def advance(group, buffer, carry):
         for part in range(DEPTH):
-            multiply(group + 1, 1 - buffer, spans[part])
+            if part % (DEPTH // 2) == 0:
+                multiply(group + 1, 1 - buffer, spans[2 * part // DEPTH])
             carry = combine(group, buffer, part, carry)
         return carry
 
@@ -534,103 +535,171 @@
     return carry
 
 
-def back_kernel(edge, occ_ref, live_ref, f_ref, pad_ref, shift_ref, w_ref, coef_ref, hat_ref, sum_ref, side_s, found_s):
+def forward_block(edge, slot, occ_ref, f_ref, hid_ref, rim_ref, w_ref, coef, bias_ref, out_ref,
+                  pad_s, shift_s, xh_s, edge_s, side_s, found_s):
     channels = f_ref.shape[-1]
-    slot = pl.program_id(0)
+
+    def activate(coded):
+        return hidden_plane(coded, coded < jnp.inf, coef)
+
+    set_halo(edge, rim_ref, pad_s, (), shift_s, (), xh_s, edge_s, activate)
+    for z in range(edge):
+        pad_s[z + 1, 1 : edge + 1] = hid_ref[0, z].reshape(edge, edge, channels)
+    side_rows(edge, shift_s, (), w_ref, side_s)
+
+    def plane(z, conv, carry):
+        mask = plane_mask(occ_ref, slot, z, edge, channels)
+        feats = f_ref[0, z].astype(f32)
+        out_ref[0, z] = (feats + jnp.where(mask, conv + bias_ref[...], 0.0)).astype(bf16)
+        return carry
+
+    conv_pipeline(edge, pad_s, (), w_ref, side_s, found_s, plane, 0)
+
+
+def convs_kernel(edge, occ_ref, live_ref, f_ref, pad_ref, shift_ref, back_ref, coef_ref, bias_ref,
+                 hid_hbm, rim_hbm, forward_hbm, hat_hbm, sum_ref, out_ref,
+                 side_s, found_s, hat_s, hid_s, rim_s, forward_s, pad_s, shift_s, xh_s, edge_s, sems):
+    channels = f_ref.shape[-1]
+    turn = pl.program_id(0)
     coef = coefficients(coef_ref)
     mean, rstd, scale, shift = coef[:4]
-
-    @pl.when(slot == 0)
-    def _():
+    fetches = [
+        pltpu.make_async_copy(hid_hbm.at[pl.ds(0, 1)], hid_s, sems.at[0]),
+        pltpu.make_async_copy(rim_hbm.at[:, pl.ds(0, 1)], rim_s, sems.at[1]),
+        pltpu.make_async_copy(forward_hbm, forward_s, sems.at[2]),
+    ]
+    stores = [pltpu.make_async_copy(hat_s.at[slot], hat_hbm.at[slot], sems.at[3 + slot]) for slot in range(2)]
+
+    @pl.when(turn == 0)
+    def _():
+        for fetch in fetches:
+            fetch.start()
         sum_ref[...] = jnp.zeros_like(sum_ref)
 
-    @pl.when(live_ref[slot] != 0)
-    def _():
-        side_rows(edge, shift_ref, (0,), w_ref, side_s)
+    @pl.when(jnp.logical_and(turn < 2, live_ref[jnp.minimum(turn, 1)] != 0))
+    def _():
+        side_rows(edge, shift_ref, (0,), back_ref, side_s)
 
         def plane(z, back, carry):
             first, second = carry
-            mask = plane_mask(occ_ref, slot, z, edge, channels)
+            mask = plane_mask(occ_ref, turn, z, edge, channels)
             normed = (f_ref[0, z].astype(f32) - mean) * rstd
             pre = normed * scale + shift
             gate = jax.nn.sigmoid(pre)
             hat = jnp.where(mask, back * (gate * (1.0 + pre * (1.0 - gate))) * scale, 0.0)
-            hat_ref[0, z] = hat
+            hat_s[turn, z] = hat
             first = first + jnp.sum(hat, axis=0, keepdims=True)
             second = second + jnp.sum(hat * normed, axis=0, keepdims=True)
             return (first, second)
 
         zero = jnp.zeros((1, channels), f32)
-        first, second = conv_pipeline(edge, pad_ref, (0,), w_ref, side_s, found_s, plane, (zero, zero))
+        first, second = conv_pipeline(edge, pad_ref, (0,), back_ref, side_s, found_s, plane, (zero, zero))
         sum_ref[0:1, :] = sum_ref[0:1, :] + first
         sum_ref[1:2, :] = sum_ref[1:2, :] + second
 
-
-def back_conv(occupancy, live, features, padded, shifted, weight, coef):
+    for slot in range(2):
+
+        @pl.when(turn == slot)
+        def _():
+            stores[slot].start()
+
+    @pl.when(turn == 2)
+    def _():
+        for fetch in fetches:
+            fetch.wait()
+
+        @pl.when(live_ref[0] == 0)
+        def _():
+            out_ref[...] = f_ref[...]
+
+        @pl.when(live_ref[0] != 0)
+        def _():
+            forward_block(edge, 0, occ_ref, f_ref, hid_s, rim_s, forward_s, coef, bias_ref, out_ref,
+                          pad_s, shift_s, xh_s, edge_s, side_s, found_s)
+
+        for store in stores:
+            store.wait()
+
+
+def forward_scratch(edge, channels):
+    wide, cells = edge + 2, edge * edge
+    return [
+        pltpu.VMEM((wide, wide, edge, channels), bf16),
+        pltpu.VMEM((2, 3, wide, edge, channels), bf16),
+        pltpu.VMEM((2, wide, 8 * ((edge + 16) // 8), channels), f32),
+        pltpu.VMEM((4, edge, channels), f32),
+    ]
+
+
+def conv_scratch(edge, channels):
+    cells = edge * edge
+    return [
+        pltpu.VMEM((2, cells, channels), f32),
+        pltpu.VMEM((2, DEPTH * cells, 3 * channels), f32),
+    ]
+
+
+def convs(occupancy, live, features, padded, shifted, back_weight, coef, bias, hidden, rim, forward_weight):
     edge, channels = features.shape[1], features.shape[-1]
     cells = edge * edge
-    whole = pl.BlockSpec((1, edge, cells, channels), lambda s: (s, 0, 0, 0))
+    block = (1, edge, cells, channels)
+    any_space = pl.BlockSpec(memory_space=pl.ANY)
+
+    def small(rows):
+        return pl.BlockSpec((rows, channels), lambda t: (0, 0))
+
     return pl.pallas_call(
-        functools.partial(back_kernel, edge),
-        grid=(2,),
+        functools.partial(convs_kernel, edge),
+        grid=(3,),
         out_shape=(
             jax.ShapeDtypeStruct((2, edge, cells, channels), f32),
             jax.ShapeDtypeStruct((8, channels), f32),
+            jax.ShapeDtypeStruct(features.shape, bf16),
         ),
         in_specs=[
             SMEM,
             SMEM,
-            whole,
-            pl.BlockSpec((1,) + padded.shape[1:], lambda s: (s, 0, 0, 0, 0)),
-            pl.BlockSpec((1,) + shifted.shape[1:], lambda s: (s, 0, 0, 0, 0, 0)),
-            pl.BlockSpec(weight.shape, lambda s: (0, 0)),
-            pl.BlockSpec((8, channels), lambda s: (0, 0)),
+            pl.BlockSpec(block, lambda t: (t % 2, 0, 0, 0)),
+            pl.BlockSpec((1,) + padded.shape[1:], lambda t: (jnp.minimum(t, 1), 0, 0, 0, 0)),
+            pl.BlockSpec((1,) + shifted.shape[1:], lambda t: (jnp.minimum(t, 1), 0, 0, 0, 0, 0)),
+            pl.BlockSpec(back_weight.shape, lambda t: (0, 0)),
+            small(8),
+            small(1),
+            any_space,
+            any_space,
+            any_space,
         ],
-        out_specs=(whole, pl.BlockSpec((8, channels), lambda s: (0, 0))),
-        scratch_shapes=[
-            pltpu.VMEM((2, cells, channels), f32),
-            pltpu.VMEM((2, DEPTH * cells, 3 * channels), f32),
-        ],
+        out_specs=(any_space, small(8), pl.BlockSpec(block, lambda t: (0, 0, 0, 0))),
+        scratch_shapes=conv_scratch(edge, channels)
+        + [
+            pltpu.VMEM((2, edge, cells, channels), f32),
+            pltpu.VMEM(block, bf16),
+            pltpu.VMEM((edge, 1) + rim.shape[2:], bf16),
+            pltpu.VMEM(forward_weight.shape, bf16),
+        ]
+        + forward_scratch(edge, channels)
+        + [pltpu.SemaphoreType.DMA((5,))],
         compiler_params=params(60, ("arbitrary",)),
-        cost_estimate=cost(20 * 10**9, 8 * MIB),
-        name="back_conv",
-    )(occupancy, live, features, padded, shifted, weight, coef)
-
-
-def forward_kernel(edge, slot, occ_ref, live_ref, f_ref, hid_ref, rim_ref, w_ref, coef_ref, bias_ref, *refs):
-    out_ref, pad_s, shift_s, xh_s, edge_s, side_s, found_s = refs[-7:]
-    channels = f_ref.shape[-1]
-    coef = coefficients(coef_ref)
-
+        cost_estimate=cost(30 * 10**9, 16 * MIB),
+        name="convs",
+    )(occupancy, live, features, padded, shifted, back_weight, coef, bias, hidden, rim, forward_weight)
+
+
+def forward_kernel(edge, slot, occ_ref, live_ref, f_ref, hid_ref, rim_ref, w_ref, coef_ref, bias_ref, base_ref,
+                   out_ref, side_s, found_s, *scratch):
     @pl.when(live_ref[slot] == 0)
     def _():
         out_ref[...] = f_ref[...]
 
     @pl.when(live_ref[slot] != 0)
     def _():
-        def activate(coded):
-            return hidden_plane(coded, coded < jnp.inf, coef)
-
-        set_halo(edge, rim_ref, pad_s, (), shift_s, (), xh_s, edge_s, activate)
-        for z in range(edge):
-            pad_s[z + 1, 1 : edge + 1] = hid_ref[0, z].reshape(edge, edge, channels)
-        side_rows(edge, shift_s, (), w_ref, side_s)
-
-        def plane(z, conv, carry):
-            mask = plane_mask(occ_ref, slot, z, edge, channels)
-            feats = f_ref[0, z].astype(f32)
-            out_ref[0, z] = (feats + jnp.where(mask, conv + bias_ref[...], 0.0)).astype(bf16)
-            return carry
-
-        conv_pipeline(edge, pad_s, (), w_ref, side_s, found_s, plane, 0)
-
-
-def forward_conv(slot, occupancy, live, features, hidden, rim, weight, coef, bias, base=None):
+        forward_block(edge, slot, occ_ref, f_ref, hid_ref, rim_ref, w_ref, coefficients(coef_ref), bias_ref,
+                      out_ref, *scratch, side_s, found_s)
+
+
+def forward_conv(slot, occupancy, live, features, hidden, rim, weight, coef, bias, base):
     edge, channels = features.shape[1], features.shape[-1]
-    cells = edge * edge
-    wide = edge + 2
-    whole = pl.BlockSpec((1, edge, cells, channels), lambda s: (slot, 0, 0, 0))
-    extra = [] if base is None else [base]
+    whole = pl.BlockSpec((1, edge, edge * edge, channels), lambda s: (slot, 0, 0, 0))
     return pl.pallas_call(
         functools.partial(forward_kernel, edge, slot),
         grid=(1,),
@@ -644,28 +713,20 @@
             pl.BlockSpec(weight.shape, lambda s: (0, 0)),
             pl.BlockSpec((8, channels), lambda s: (0, 0)),
             pl.BlockSpec((1, channels), lambda s: (0, 0)),
-        ]
-        + [pl.BlockSpec(memory_space=pl.ANY)] * len(extra),
+            pl.BlockSpec(memory_space=pl.ANY),
+        ],
         out_specs=whole,
-        scratch_shapes=[
-            pltpu.VMEM((wide, wide, edge, channels), bf16),
-            pltpu.VMEM((2, 3, wide, edge, channels), bf16),
-            pltpu.VMEM((2, wide, 8 * ((edge + 16) // 8), channels), f32),
-            pltpu.VMEM((4, edge, channels), f32),
-            pltpu.VMEM((2, cells, channels), f32),
-            pltpu.VMEM((2, DEPTH * cells, 3 * channels), f32),
-        ],
-        input_output_aliases={8: 0} if extra else {},
+        scratch_shapes=conv_scratch(edge, channels) + forward_scratch(edge, channels),
+        input_output_aliases={8: 0},
         compiler_params=params(60, ("arbitrary",)),
         cost_estimate=cost(10 * 10**9, 4 * MIB),
         name="forward_conv",
-    )(occupancy, live, features, hidden, rim, weight, coef, bias, *extra)
+    )(occupancy, live, features, hidden, rim, weight, coef, bias, base)
 
 
 def finish_kernel(edge, occ_ref, live_ref, f_ref, g_ref, hat_ref, coef_ref, sums_ref, out_ref):
     channels = f_ref.shape[-1]
     slot = pl.program_id(0)
-    first_plane = pl.program_id(1) * f_ref.shape[1]
     mean, rstd = coef_ref[0:1, :], coef_ref[1:2, :]
     first, second = sums_ref[0:1, :], sums_ref[1:2, :]
 
@@ -675,23 +736,26 @@
 
     @pl.when(live_ref[slot] != 0)
     def _():
-        for z in range(f_ref.shape[1]):
-            mask = plane_mask(occ_ref, slot, first_plane + z, edge, channels)
+        def plane(z, carry):
+            mask = plane_mask(occ_ref, slot, z, edge, channels)
             normed = (f_ref[0, z].astype(f32) - mean) * rstd
             change = rstd * (hat_ref[0, z] - first - normed * second)
             out_ref[0, z] = (g_ref[0, z].astype(f32) + jnp.where(mask, change, 0.0)).astype(bf16)
+            return carry
+
+        lax.fori_loop(0, edge, plane, 0)
 
 
 def finish(occupancy, live, features, cotangent, hat, coef, sums):
     edge, channels = features.shape[1], features.shape[-1]
-    few = pl.BlockSpec((1, edge // 4, edge * edge, channels), lambda s, z: (s, z, 0, 0))
+    few = pl.BlockSpec((1, edge, edge * edge, channels), lambda s: (s, 0, 0, 0))
     return pl.pallas_call(
         functools.partial(finish_kernel, edge),
-        grid=(2, 4),
+        grid=(2,),
         out_shape=jax.ShapeDtypeStruct(features.shape, bf16),
-        in_specs=[SMEM, SMEM, few, few, few] + [pl.BlockSpec((8, channels), lambda s, z: (0, 0))] * 2,
+        in_specs=[SMEM, SMEM, few, few, few] + [pl.BlockSpec((8, channels), lambda s: (0, 0))] * 2,
         out_specs=few,
-        compiler_params=params(60, ("arbitrary", "arbitrary")),
+        compiler_params=params(60, ("arbitrary",)),
         cost_estimate=cost(0, 12 * MIB),
         name="finish",
     )(occupancy, live, features, cotangent, hat, coef, sums)
@@ -740,7 +804,7 @@
     channels = shape[2]
     wide, narrow = lax.axis_size("wide"), lax.axis_size("narrow")
     rows = shape[0] * shape[1] // wide
-    mine = jnp.sum(exchange(grads.reshape(wide, rows, channels), "wide"), axis=0)
+    mine = lax.psum_scatter(grads.reshape(wide * rows, channels), "wide", scatter_dimension=0, tiled=True)
     deep = -(-rows // (8 * narrow)) * 8
     mine = jnp.pad(mine, ((0, deep * narrow - rows), (0, 0))).reshape(narrow, deep, channels)
     sums = jnp.broadcast_to(sums[None], (narrow,) + sums.shape)
@@ -755,7 +819,7 @@
     mine = mine.reshape(narrow * deep, channels)[:rows]
     mine, tie = lax.optimization_barrier((mine, tie))
     mine = jnp.concatenate([mine, tail, jnp.zeros((2, channels), bf16)], axis=0)
-    parts = exchange(jnp.broadcast_to(mine[None], (wide,) + mine.shape), "wide")
+    parts = lax.all_gather(mine, "wide")
     step, sums = pl.pallas_call(
         functools.partial(scale_kernel, rows),
         out_shape=(
@@ -809,11 +873,7 @@
     up_rows, feat_got = lax.optimization_barrier((up_rows, feat_got))
     up_rim = exchange(up_rows, "narrow")
     feat_rows, stats = hub_stage(place, live_slots, neighbours, feat_got, float("inf"), True)
-    feat_rows, up_rim, stats = lax.optimization_barrier((feat_rows, up_rim, stats))
-    step = 4
-    while step < lax.axis_size("wide"):
-        stats = wide_round(stats, step)
-        step *= 4
+    feat_rows, up_rim = lax.optimization_barrier((feat_rows, up_rim))
     feat_rim = exchange(feat_rows, "narrow")
 
     voxel_count = stats[2, 0] * group_width
@@ -824,12 +884,12 @@
     coef = jnp.stack([mean, rstd, scale, shift, blank + voxel_count, blank, blank, blank])
 
     grads, padded, shifted, hidden = weight_grad(occupancy, live, features, out_cotangent, up_rim, coef)
-    grads, feat_rim = lax.optimization_barrier((grads, feat_rim))
-    hat, grad_sums = back_conv(occupancy, live, features, padded, shifted, back_weight, coef)
-    forward = (occupancy, live, features, hidden, feat_rim, forward_weight, coef, conv_bias[None, :])
-    mixed = forward_conv(0, *forward)
+    bias = conv_bias[None, :]
+    hat, grad_sums, mixed = convs(
+        occupancy, live, features, padded, shifted, back_weight, coef, bias, hidden, feat_rim, forward_weight
+    )
     weight_step, grad_sums, mixed = reduce_weights(grads, grad_sums, coef, mixed)
-    mixed = forward_conv(1, *forward, base=mixed)
+    mixed = forward_conv(1, occupancy, live, features, hidden, feat_rim, forward_weight, coef, bias, mixed)
     feature_grad = finish(occupancy, live, features, out_cotangent, hat, coef, grad_sums)
     return (mixed, feature_grad, weight_step)
 

time: 223 us -> 284 us (1.27)
  blocking collectives: 0 us -> 19.5 us
  waiting for transfers between devices: 100 us -> 119 us
  Pallas kernels: 45 us -> 59.3 us
  between operations: 2.3 us -> 15.6 us
  starting transfers between devices: 61.6 us -> 53.5 us
    unnamed x0 -> x2, waiting for transfers between devices: none -> 57.9 us
    all_to_all x8 -> x6, waiting for transfers between devices: 91.5 us -> 53.1 us  [exchange(): return lax.all_to_all(values, axis, split_axis=0, concat_axis=0, tiled=True)]
    all_gather x0 -> x1, blocking collectives: none -> 19.5 us  [reduce_weights(): parts = lax.all_gather(mine, 'wide')]
    all_to_all x8 -> x6, starting transfers between devices: 44.1 us -> 37.6 us  [exchange(): return lax.all_to_all(values, axis, split_axis=0, concat_axis=0, tiled=True)]
    pallas_call x1, Pallas kernels: 4.82 us -> 10.5 us  [weight_grad(): pl.pallas_call(functools.partial(weight_kernel, edge), grid=(2,), out_sha...]
    pallas_call x2, Pallas kernels: 11.4 us -> 16.9 us  [the longest x1 11.4 us: convs(): pl.pallas_call(functools.partial(convs_kernel, edge), grid=(3,), out_shap...]
    pallas_call x2 -> x1, Pallas kernels: 6.01 us -> 9.09 us  [forward_conv(): pl.pallas_call(functools.partial(forward_kernel, edge, slot), grid=(1,),...]
  transfers between devices with their start and end apart: 18 -> 17, of which waited for: 12 -> 10; matrix products, arithmetic and copies ran while one was open for 4% -> 3% of each run, Pallas kernels for 15% -> 14%
where the time goes in v3:
time: 284 us; the launch traced here: 282 us
  waiting for transfers between devices  119 us (42%)
  Pallas kernels  59.3 us (21%)
  starting transfers between devices  53.5 us (19%)
  blocking collectives  19.5 us (7%)
  between operations  15.6 us (5%)
  local copies, waits for them, and re-layouts  12.1 us (4%)
    unnamed x2, waiting for transfers between devices  57.9 us
    all_to_all x6, waiting for transfers between devices, exchange(): return lax.all_to_all(values, axis, split_axis=0, concat_axis=0, tiled=True)  53.1 us
    all_to_all x6, starting transfers between devices, exchange(): return lax.all_to_all(values, axis, split_axis=0, concat_axis=0, tiled=True)  37.6 us
    all_gather x1, blocking collectives, reduce_weights(): parts = lax.all_gather(mine, 'wide')  19.5 us
    pallas_call x1, Pallas kernels, convs(): pl.pallas_call(functools.partial(convs_kernel, edge), grid=(3,), out_shap...  11.4 us
    pallas_call x1, Pallas kernels, weight_grad(): pl.pallas_call(functools.partial(weight_kernel, edge), grid=(2,), out_sha...  10.5 us
    pallas_call x2, Pallas kernels, surface(): pl.pallas_call(functools.partial(surface_kernel, edge, with_stats, fill),...  10.4 us
    pallas_call x1, Pallas kernels, forward_conv(): pl.pallas_call(functools.partial(forward_kernel, edge, slot), grid=(1,),...  9.09 us
  transfers between devices with their start and end apart: 17, of which 10 were waited for; matrix products, arithmetic and copies ran while one was open for 3% of the time, Pallas kernels for 14%

profile of v3, /device:TPU:1, one launch (start us, length us, event | category | flops | bytes accessed | tf_op | source)
XLA Modules:
  0.0 281.5 jit_solution(4980772452931780827)
XLA Ops:
  7.2 0.0 copy-start
  7.2 4.4 %surface.3 = bf16[16,13,16,128]{3,2,1,0:T(8,128)(2,1)} custom-call(s32[2,16,16]{2,1,0:T(8,128)} %occ_ref.11, bf16[2,16,256,128]{3,2,1,0:T(8,128)(2,1)} %g_ref.3), custom_call_target="tpu_custom_call" | custom-call | bytes 3145728 | tf_op jit(solution)/shard_map/surface/pallas_call | solution.py:128
  11.6 10.1 %all-to-all-start = ((bf16[16,13,16,128]{3,2,1,0:T(8,128)(2,1)}), bf16[16,13,16,128]{3,2,1,0:T(8,128)(2,1)S(1)}, u32[]{:S(2)}, u32[]{:S(2)}) async-start(bf16[16,13,16,128]{3,2,1,0:T(8,128)(2,1)} %surface.3), calls=%async_computation | async-start | bytes 1703936 | tf_op jit(solution)/shard_map/all_to_all | solution.py:271
  22.3 6.0 %surface.2 = bf16[16,13,16,128]{3,2,1,0:T(8,128)(2,1)} custom-call(s32[2,16,16]{2,1,0:T(8,128)} %occ_ref.11, bf16[2,16,256,128]{3,2,1,0:T(8,128)(2,1)} %f_ref.7), custom_call_target="tpu_custom_call" | custom-call | bytes 3145728 | tf_op jit(solution)/shard_map/surface/pallas_call | solution.py:128
  28.3 1.0 rev.3
  29.4 2.4 copy.26
  31.8 1.9 copy.25
  33.8 0.2 fusion.12
  34.0 0.0 copy-done.9
  34.1 0.0 copy-start.3
  34.1 1.6 copy_bitcast_fusion
  35.7 10.0 %all-to-all-done.got_ref = bf16[16,13,16,128]{3,2,1,0:T(8,128)(2,1)S(1)} async-done(((bf16[16,13,16,128]{3,2,1,0:T(8,128)(2,1)}), bf16[16,13,16,128]{3,2,1,0:T(8,128)(2,1)S(1)}, u32[]{:S(2)}, u32[]{:S(2)}) %all-to-all-start) | async-done | bytes 852000 | tf_op jit(solution)/shard_map/all_to_all | solution.py:271
  45.7 3.5 %all-to-all-start.1 = ((bf16[16,13,16,128]{3,2,1,0:T(8,128)(2,1)}), bf16[16,13,16,128]{3,2,1,0:T(8,128)(2,1)S(1)}, u32[]{:S(2)}, u32[]{:S(2)}) async-start(bf16[16,13,16,128]{3,2,1,0:T(8,128)(2,1)} %surface.2), calls=%async_computation.1 | async-start | bytes 1703936 | tf_op jit(solution)/shard_map/all_to_all | solution.py:271
  49.2 1.2 trade.2
  50.4 3.2 %collective-permute-start = (bf16[18,16,128]{2,1,0:T(8,128)(2,1)S(1)}, bf16[18,16,128]{2,1,0:T(8,128)(2,1)S(1)}, u32[]{:S(2)}, u32[]{:S(2)}) collective-permute-start(bf16[18,16,128]{2,1,0:T(8,128)(2,1)S(1)} %get-tuple-element.35), channel_id=1, source_target_pairs={{0,16},{16,32},{32,48},{48,64},{64,80},{80,96},{96,112},{112,128},... | collective-permute-start | bytes 221192 | tf_op jit(solution)/shard_map/ppermute | solution.py:277
  53.6 1.3 collective-permute-start.1
  54.9 0.1 pad_add_fusion.place_ref
  55.0 0.4 collective-permute-done.lower_ref
  55.4 3.9 %collective-permute-done.1.upper_ref = bf16[18,16,128]{2,1,0:T(8,128)(2,1)S(1)} collective-permute-done((bf16[18,16,128]{2,1,0:T(8,128)(2,1)S(1)}, bf16[18,16,128]{2,1,0:T(8,128)(2,1)S(1)}, u32[]{:S(2)}, u32[]{:S(2)}) %collective-permute-start.1) | collective-permute-done | bytes 73760 | tf_op jit(solution)/shard_map/ppermute | solution.py:278
  59.3 4.4 %hub_rows.2 = bf16[16,2,7,16,128]{4,3,2,1,0:T(8,128)(2,1)} custom-call(s32[2]{0:T(128)S(1)} %pad_add_fusion.place_ref, s32[1,16]{1,0:T(1,128)S(1)} %copy-done.3, s32[16,27]{1,0:T(8,128)S(1)} %copy-done.2, bf16[16,13,16,128]{3,2,1,0:T(8,128)(2,1)S(1)} %all-to-all-done.got_ref, bf16[18,16,128]{2,1,0:T(8,128)(2,1)S(1)} %collective-permute-done.lower_ref, ...), custom_call_target="tpu_custom_call" | custom-call | bytes 8388608 | tf_op jit(solution)/shard_map/hub_rows/pallas_call | solution.py:255
  63.7 9.2 %all-to-all-done.1.got_ref = bf16[16,13,16,128]{3,2,1,0:T(8,128)(2,1)S(1)} async-done(((bf16[16,13,16,128]{3,2,1,0:T(8,128)(2,1)}), bf16[16,13,16,128]{3,2,1,0:T(8,128)(2,1)S(1)}, u32[]{:S(2)}, u32[]{:S(2)}) %all-to-all-start.1) | async-done | bytes 852000 | tf_op jit(solution)/shard_map/all_to_all | solution.py:271
  72.9 3.5 %all-to-all-start.2 = ((bf16[16,2,7,16,128]{4,3,2,1,0:T(8,128)(2,1)}), bf16[16,2,7,16,128]{4,3,2,1,0:T(8,128)(2,1)S(1)}, u32[]{:S(2)}, u32[]{:S(2)}) async-start(bf16[16,2,7,16,128]{4,3,2,1,0:T(8,128)(2,1)} %hub_rows.2), calls=%async_computation.2 | async-start | bytes 1835008 | tf_op jit(solution)/shard_map/all_to_all | solution.py:271
  76.5 0.6 trade.3
  77.1 2.8 %collective-permute-start.4 = (f32[8,128]{1,0:T(8,128)S(1)}, f32[8,128]{1,0:T(8,128)S(1)}, u32[]{:S(2)}, u32[]{:S(2)}) collective-permute-start(f32[8,128]{1,0:T(8,128)S(1)} %get-tuple-element.39), channel_id=1, source_target_pairs={{0,48},{16,32},{32,16},{48,0},{64,112},{80,96},{96,80},{112,64},{1... | collective-permute-start | bytes 12296 | tf_op jit(solution)/shard_map/ppermute | solution.py:769
  79.9 0.4 collective-permute-start.3
  80.3 0.3 collective-permute-start.2
  80.6 0.2 compare_reduce_fusion
  80.8 3.1 %collective-permute-start.5 = (bf16[18,16,128]{2,1,0:T(8,128)(2,1)S(1)}, bf16[18,16,128]{2,1,0:T(8,128)(2,1)S(1)}, u32[]{:S(2)}, u32[]{:S(2)}) collective-permute-start(bf16[18,16,128]{2,1,0:T(8,128)(2,1)S(1)} %get-tuple-element.40), channel_id=1, source_target_pairs={{0,16},{16,32},{32,48},{48,64},{64,80},{80,96},{96,112},{112,128},... | collective-permute-start | bytes 221192 | tf_op jit(solution)/shard_map/ppermute | solution.py:277
  83.9 1.3 collective-permute-start.6
  85.2 0.0 collective-permute-done.3
  85.2 0.0 collective-permute-done.5.lower_ref
  85.3 4.0 %collective-permute-done.6.upper_ref = bf16[18,16,128]{2,1,0:T(8,128)(2,1)S(1)} collective-permute-done((bf16[18,16,128]{2,1,0:T(8,128)(2,1)S(1)}, bf16[18,16,128]{2,1,0:T(8,128)(2,1)S(1)}, u32[]{:S(2)}, u32[]{:S(2)}) %collective-permute-start.6) | collective-permute-done | bytes 73760 | tf_op jit(solution)/shard_map/ppermute | solution.py:278
  89.3 2.8 collective-permute-start.9
  92.1 0.5 collective-permute-start.8
  92.6 0.1 collective-permute-start.7
  92.7 0.5 convert_element_type.17.live_ref
  93.2 4.4 %hub_rows.3 = bf16[16,2,7,16,128]{4,3,2,1,0:T(8,128)(2,1)} custom-call(s32[2]{0:T(128)S(1)} %pad_add_fusion.place_ref, s32[1,16]{1,0:T(1,128)S(1)} %copy-done.3, s32[16,27]{1,0:T(8,128)S(1)} %copy-done.2, bf16[16,13,16,128]{3,2,1,0:T(8,128)(2,1)S(1)} %all-to-all-done.1.got_ref, bf16[18,16,128]{2,1,0:T(8,128)(2,1)S(1)} %collective-permute-done.5.lower_ref, ...), custom_call_target="tpu_custom_call" | custom-call | bytes 8388608 | tf_op jit(solution)/shard_map/hub_rows/pallas_call | solution.py:255
  97.7 0.5 slice.33
  98.8 0.2 fusion
  99.1 0.6 stack.46.coef_ref
  99.7 1.8 all-to-all-done.2.rim_ref
  101.5 7.8 %all-to-all-start.3 = ((bf16[16,2,7,16,128]{4,3,2,1,0:T(8,128)(2,1)}), bf16[16,2,7,16,128]{4,3,2,1,0:T(8,128)(2,1)S(1)}, u32[]{:S(2)}, u32[]{:S(2)}) async-start(bf16[16,2,7,16,128]{4,3,2,1,0:T(8,128)(2,1)} %hub_rows.3), calls=%async_computation.3 | async-start | bytes 1835008 | tf_op jit(solution)/shard_map/all_to_all | solution.py:271
  109.3 0.2 reduce-scatter.4.cloned.1.call-start
  109.5 10.5 %weight_grad.1 = (f32[27,128,128]{2,1,0:T(8,128)}, bf16[2,18,18,16,128]{4,3,2,1,0:T(8,128)(2,1)}, bf16[2,2,3,18,16,128]{5,4,3,2,1,0:T(8,128)(2,1)}, bf16[2,16,256,128]{3,2,1,0:T(8,128)(2,1)}) custom-call(s32[2,16,16]{2,1,0:T(8,128)} %occ_ref.11, s32[2]{0:T(128)} %convert_element_type.17.live_ref, bf16[2,16,256,128]{3,2,1,0:T(8,128)(2,1)} %f_ref.7, ...), custom_call_target="tpu_custom_call" | custom-call | flops 20000000000 | bytes 8388608 | tf_op jit(solution)/shard_map/weight_grad/pallas_call | solution.py:430
  120.0 0.0 reduce-scatter.4.cloned.1.call-update
  120.0 14.6 %all-to-all-done.3.rim_hbm.rim_ref = bf16[16,2,7,16,128]{4,3,2,1,0:T(8,128)(2,1)S(1)} async-done(((bf16[16,2,7,16,128]{4,3,2,1,0:T(8,128)(2,1)}), bf16[16,2,7,16,128]{4,3,2,1,0:T(8,128)(2,1)S(1)}, u32[]{:S(2)}, u32[]{:S(2)}) %all-to-all-start.3) | async-done | bytes 917536 | tf_op jit(solution)/shard_map/all_to_all | solution.py:271
  134.6 0.9 copy-done.7
  135.5 11.4 %convs.1 = (f32[2,16,256,128]{3,2,1,0:T(8,128)}, f32[8,128]{1,0:T(8,128)}, bf16[2,16,256,128]{3,2,1,0:T(8,128)(2,1)}) custom-call(s32[2,16,16]{2,1,0:T(8,128)} %occ_ref.11, s32[2]{0:T(128)} %convert_element_type.17.live_ref, bf16[2,16,256,128]{3,2,1,0:T(8,128)(2,1)} %f_ref.7, bf16[2,18,18,16,128]{4,3,2,1,0:T(8,128)(2,1)} %get-tuple-element.53.pad_ref, ...), custom_call_target="tpu_custom_call" | custom-call | flops 30000001024 | bytes 16777216 | tf_op jit(solution)/shard_map/convs/pallas_call | solution.py:651
  147.0 57.9 %reduce-scatter.4.cloned.1.call-done = f32[216,128]{1,0:T(8,128)} async-done(((f32[3456,128]{1,0:T(8,128)}), f32[216,128]{1,0:T(8,128)}) %reduce-scatter.4.cloned.1.call-update) | async-done | bytes 110608
  204.9 0.9 pad.4
  205.8 0.7 broadcast_in_dim.9
  206.5 0.7 pad_maximum_fusion
  207.2 9.2 %all-to-all-start.4 = ((f32[16,24,128]{2,1,0:T(8,128)}), f32[16,24,128]{2,1,0:T(8,128)S(1)}, u32[]{:S(2)}, u32[]{:S(2)}) async-start(f32[16,24,128]{2,1,0:T(8,128)} %pad_maximum_fusion), calls=%async_computation.4 | async-start | bytes 393216 | tf_op jit(solution)/shard_map/all_to_all | solution.py:271
  216.4 0.1 pad.7.clone
  216.5 10.2 %all-to-all-done.4 = f32[16,24,128]{2,1,0:T(8,128)S(1)} async-done(((f32[16,24,128]{2,1,0:T(8,128)}), f32[16,24,128]{2,1,0:T(8,128)S(1)}, u32[]{:S(2)}, u32[]{:S(2)}) %all-to-all-start.4) | async-done | bytes 196640 | tf_op jit(solution)/shard_map/all_to_all | solution.py:271
  226.8 0.6 broadcast_in_dim.10
  227.4 3.4 %all-to-all-start.5 = ((bf16[16,16,128]{2,1,0:T(8,128)(2,1)}), bf16[16,16,128]{2,1,0:T(8,128)(2,1)S(1)}, u32[]{:S(2)}, u32[]{:S(2)}) async-start(bf16[16,16,128]{2,1,0:T(8,128)(2,1)} %broadcast_in_dim.10), calls=%async_computation.5 | async-start | bytes 131072 | tf_op jit(solution)/shard_map/all_to_all | solution.py:271
  230.9 7.3 %all-to-all-done.5 = bf16[16,16,128]{2,1,0:T(8,128)(2,1)S(1)} async-done(((bf16[16,16,128]{2,1,0:T(8,128)(2,1)}), bf16[16,16,128]{2,1,0:T(8,128)(2,1)S(1)}, u32[]{:S(2)}, u32[]{:S(2)}) %all-to-all-start.5) | async-done | bytes 65568 | tf_op jit(solution)/shard_map/all_to_all | solution.py:271
  238.2 0.1 maximum_maximum_fusion
  238.3 19.5 %all-gather = bf16[3584,128]{1,0:T(8,128)(2,1)S(1)} all-gather(bf16[224,128]{1,0:T(8,128)(2,1)S(1)} %maximum_maximum_fusion), channel_id=2, replica_groups=mesh['wide'=16,'narrow'=16] {'wide'}, dimensions={0}, use_global_device_ids=true | all-gather | bytes 974848 | tf_op jit(solution)/shard_map/all_gather | solution.py:822
  257.8 1.6 scale.1
  259.5 0.6 copy-done.4
  260.1 5.5 %finish.1 = bf16[2,16,256,128]{3,2,1,0:T(8,128)(2,1)} custom-call(s32[2,16,16]{2,1,0:T(8,128)} %occ_ref.11, s32[2]{0:T(128)} %convert_element_type.17.live_ref, bf16[2,16,256,128]{3,2,1,0:T(8,128)(2,1)} %f_ref.7, bf16[2,16,256,128]{3,2,1,0:T(8,128)(2,1)} %g_ref.3, f32[2,16,256,128]{3,2,1,0:T(8,128)} %get-tuple-element.61.hat_ref, f32[8,128]{1,0:T(8,128)} %stack.46.coef_ref, ...), custom_call_target="tpu_custom_call" | custom-call | bytes 12582912 | tf_op jit(solution)/shard_map/finish/pallas_call | solution.py:752
  265.6 9.1 %forward_conv.1 = bf16[2,16,256,128]{3,2,1,0:T(8,128)(2,1)} custom-call(s32[2,16,16]{2,1,0:T(8,128)} %occ_ref.11, s32[2]{0:T(128)} %convert_element_type.17.live_ref, bf16[2,16,256,128]{3,2,1,0:T(8,128)(2,1)} %f_ref.7, bf16[2,16,256,128]{3,2,1,0:T(8,128)(2,1)} %get-tuple-element.49.hid_hbm.hid_ref, ...), custom_call_target="tpu_custom_call", output_to_operand_aliasing={{}: (8, {})} | custom-call | flops 10000000000 | bytes 4194304 | tf_op jit(solution)/shard_map/forward_conv/pallas_call | solution.py:703
  (39 shorter events, 0.2 us)
Async XLA Ops:
  7.2 26.7 %copy-start = (f32[256,256]{1,0:T(8,128)S(1)}, f32[256,256]{1,0:T(8,128)}, u32[]{:S(2)}) copy-start(f32[256,256]{1,0:T(8,128)} %param.19) | copy-start | bytes 786436
  11.6 16.8 %copy-start.5 = (bf16[27,128,128]{2,1,0:T(8,128)(2,1)S(1)}, bf16[27,128,128]{2,1,0:T(8,128)(2,1)}, u32[]{:S(2)}) copy-start(bf16[27,128,128]{2,1,0:T(8,128)(2,1)} %param.20) | copy-start | bytes 2654212
  11.6 34.1 %all-to-all-start = ((bf16[16,13,16,128]{3,2,1,0:T(8,128)(2,1)}), bf16[16,13,16,128]{3,2,1,0:T(8,128)(2,1)S(1)}, u32[]{:S(2)}, u32[]{:S(2)}) async-start(bf16[16,13,16,128]{3,2,1,0:T(8,128)(2,1)} %surface.3), calls=%async_computation | async-start | bytes 1703936 | tf_op jit(solution)/shard_map/all_to_all | solution.py:271
  29.4 4.7 %copy-start.8 = (f32[128]{0:T(128)S(1)}, f32[128]{0:T(128)}, u32[]{:S(2)}) copy-start(f32[128]{0:T(128)} %param.18) | copy-start | bytes 1540
  29.4 4.7 %copy-start.9 = (f32[128]{0:T(128)S(1)}, f32[128]{0:T(128)}, u32[]{:S(2)}) copy-start(f32[128]{0:T(128)} %param.17) | copy-start | bytes 1540
  34.1 15.1 %copy-start.3 = (s32[1,16]{1,0:T(1,128)S(1)}, s32[1,16]{1,0:T(1,128)}, u32[]{:S(2)}) copy-start(s32[1,16]{1,0:T(1,128)} %live_ref.7) | copy-start | bytes 196
  35.7 23.6 %copy-start.2 = (s32[16,27]{1,0:T(8,128)S(1)}, s32[16,27]{1,0:T(8,128)}, u32[]{:S(2)}) copy-start(s32[16,27]{1,0:T(8,128)} %near_ref.3) | copy-start | bytes 5188
  45.7 27.2 %all-to-all-start.1 = ((bf16[16,13,16,128]{3,2,1,0:T(8,128)(2,1)}), bf16[16,13,16,128]{3,2,1,0:T(8,128)(2,1)S(1)}, u32[]{:S(2)}, u32[]{:S(2)}) async-start(bf16[16,13,16,128]{3,2,1,0:T(8,128)(2,1)} %surface.2), calls=%async_computation.1 | async-start | bytes 1703936 | tf_op jit(solution)/shard_map/all_to_all | solution.py:271
  50.4 5.0 %collective-permute-start = (bf16[18,16,128]{2,1,0:T(8,128)(2,1)S(1)}, bf16[18,16,128]{2,1,0:T(8,128)(2,1)S(1)}, u32[]{:S(2)}, u32[]{:S(2)}) collective-permute-start(bf16[18,16,128]{2,1,0:T(8,128)(2,1)S(1)} %get-tuple-element.35), channel_id=1, source_target_pairs={{0,16},{16,32},{32,48},{48,64},{64,80},{80,96},{96,112},{112,128},... | collective-permute-start | bytes 221192 | tf_op jit(solution)/shard_map/ppermute | solution.py:277
  53.6 5.6 %collective-permute-start.1 = (bf16[18,16,128]{2,1,0:T(8,128)(2,1)S(1)}, bf16[18,16,128]{2,1,0:T(8,128)(2,1)S(1)}, u32[]{:S(2)}, u32[]{:S(2)}) collective-permute-start(bf16[18,16,128]{2,1,0:T(8,128)(2,1)S(1)} %get-tuple-element.36), channel_id=1, source_target_pairs={{16,0},{32,16},{48,32},{64,48},{80,64},{96,80},{112,96},{128,112},... | collective-permute-start | bytes 221192 | tf_op jit(solution)/shard_map/ppermute | solution.py:278
  72.9 28.6 %all-to-all-start.2 = ((bf16[16,2,7,16,128]{4,3,2,1,0:T(8,128)(2,1)}), bf16[16,2,7,16,128]{4,3,2,1,0:T(8,128)(2,1)S(1)}, u32[]{:S(2)}, u32[]{:S(2)}) async-start(bf16[16,2,7,16,128]{4,3,2,1,0:T(8,128)(2,1)} %hub_rows.2), calls=%async_computation.2 | async-start | bytes 1835008 | tf_op jit(solution)/shard_map/all_to_all | solution.py:271
  77.1 8.1 %collective-permute-start.4 = (f32[8,128]{1,0:T(8,128)S(1)}, f32[8,128]{1,0:T(8,128)S(1)}, u32[]{:S(2)}, u32[]{:S(2)}) collective-permute-start(f32[8,128]{1,0:T(8,128)S(1)} %get-tuple-element.39), channel_id=1, source_target_pairs={{0,48},{16,32},{32,16},{48,0},{64,112},{80,96},{96,80},{112,64},{1... | collective-permute-start | bytes 12296 | tf_op jit(solution)/shard_map/ppermute | solution.py:769
  79.9 5.2 %collective-permute-start.3 = (f32[8,128]{1,0:T(8,128)S(1)}, f32[8,128]{1,0:T(8,128)S(1)}, u32[]{:S(2)}, u32[]{:S(2)}) collective-permute-start(f32[8,128]{1,0:T(8,128)S(1)} %get-tuple-element.39), channel_id=1, source_target_pairs={{0,32},{16,48},{32,0},{48,16},{64,96},{80,112},{96,64},{112,80},{1... | collective-permute-start | bytes 12296 | tf_op jit(solution)/shard_map/ppermute | solution.py:769
  80.3 4.9 %collective-permute-start.2 = (f32[8,128]{1,0:T(8,128)S(1)}, f32[8,128]{1,0:T(8,128)S(1)}, u32[]{:S(2)}, u32[]{:S(2)}) collective-permute-start(f32[8,128]{1,0:T(8,128)S(1)} %get-tuple-element.39), channel_id=1, source_target_pairs={{0,16},{16,0},{32,48},{48,32},{64,80},{80,64},{96,112},{112,96},{1... | collective-permute-start | bytes 12296 | tf_op jit(solution)/shard_map/ppermute | solution.py:769
  80.8 4.5 %collective-permute-start.5 = (bf16[18,16,128]{2,1,0:T(8,128)(2,1)S(1)}, bf16[18,16,128]{2,1,0:T(8,128)(2,1)S(1)}, u32[]{:S(2)}, u32[]{:S(2)}) collective-permute-start(bf16[18,16,128]{2,1,0:T(8,128)(2,1)S(1)} %get-tuple-element.40), channel_id=1, source_target_pairs={{0,16},{16,32},{32,48},{48,64},{64,80},{80,96},{96,112},{112,128},... | collective-permute-start | bytes 221192 | tf_op jit(solution)/shard_map/ppermute | solution.py:277
  83.9 5.4 %collective-permute-start.6 = (bf16[18,16,128]{2,1,0:T(8,128)(2,1)S(1)}, bf16[18,16,128]{2,1,0:T(8,128)(2,1)S(1)}, u32[]{:S(2)}, u32[]{:S(2)}) collective-permute-start(bf16[18,16,128]{2,1,0:T(8,128)(2,1)S(1)} %get-tuple-element.41), channel_id=1, source_target_pairs={{16,0},{32,16},{48,32},{64,48},{80,64},{96,80},{112,96},{128,112},... | collective-permute-start | bytes 221192 | tf_op jit(solution)/shard_map/ppermute | solution.py:278
  89.3 8.4 %collective-permute-start.9 = (f32[8,128]{1,0:T(8,128)S(1)}, f32[8,128]{1,0:T(8,128)S(1)}, u32[]{:S(2)}, u32[]{:S(2)}) collective-permute-start(f32[8,128]{1,0:T(8,128)S(1)} %add_add_fusion.1), channel_id=1, source_target_pairs={{0,192},{16,208},{32,224},{48,240},{64,128},{80,144},{96,160},{112... | collective-permute-start | bytes 12296 | tf_op jit(solution)/shard_map/ppermute | solution.py:769
  92.1 5.6 %collective-permute-start.8 = (f32[8,128]{1,0:T(8,128)S(1)}, f32[8,128]{1,0:T(8,128)S(1)}, u32[]{:S(2)}, u32[]{:S(2)}) collective-permute-start(f32[8,128]{1,0:T(8,128)S(1)} %add_add_fusion.1), channel_id=1, source_target_pairs={{0,128},{16,144},{32,160},{48,176},{64,192},{80,208},{96,224},{112... | collective-permute-start | bytes 12296 | tf_op jit(solution)/shard_map/ppermute | solution.py:769
  92.6 5.0 %collective-permute-start.7 = (f32[8,128]{1,0:T(8,128)S(1)}, f32[8,128]{1,0:T(8,128)S(1)}, u32[]{:S(2)}, u32[]{:S(2)}) collective-permute-start(f32[8,128]{1,0:T(8,128)S(1)} %add_add_fusion.1), channel_id=1, source_target_pairs={{0,64},{16,80},{32,96},{48,112},{64,0},{80,16},{96,32},{112,48},{1... | collective-permute-start | bytes 12296 | tf_op jit(solution)/shard_map/ppermute | solution.py:769
  101.5 8.1 %copy-start.6 = (bf16[16,2,7,16,128]{4,3,2,1,0:T(8,128)(2,1)}, bf16[16,2,7,16,128]{4,3,2,1,0:T(8,128)(2,1)S(1)}, u32[]{:S(2)}) copy-start(bf16[16,2,7,16,128]{4,3,2,1,0:T(8,128)(2,1)S(1)} %all-to-all-done.2.rim_ref) | copy-start | bytes 2752516
  101.5 33.1 %all-to-all-start.3 = ((bf16[16,2,7,16,128]{4,3,2,1,0:T(8,128)(2,1)}), bf16[16,2,7,16,128]{4,3,2,1,0:T(8,128)(2,1)S(1)}, u32[]{:S(2)}, u32[]{:S(2)}) async-start(bf16[16,2,7,16,128]{4,3,2,1,0:T(8,128)(2,1)} %hub_rows.3), calls=%async_computation.3 | async-start | bytes 1835008 | tf_op jit(solution)/shard_map/all_to_all | solution.py:271
  109.3 95.6 %reduce-scatter.4.cloned.1.call-start = ((), (), s32[]{:S(2)}) async-start(), calls=%async_computation.7 | async-start | bytes 1880064
  134.6 0.9 copy-start.7
  147.0 110.9 %copy-start.1 = (f32[8,128]{1,0:T(8,128)S(1)}, f32[8,128]{1,0:T(8,128)}, u32[]{:S(2)}) copy-start(f32[8,128]{1,0:T(8,128)} %stack.46.coef_ref) | copy-start | bytes 12292
  207.2 19.5 %all-to-all-start.4 = ((f32[16,24,128]{2,1,0:T(8,128)}), f32[16,24,128]{2,1,0:T(8,128)S(1)}, u32[]{:S(2)}, u32[]{:S(2)}) async-start(f32[16,24,128]{2,1,0:T(8,128)} %pad_maximum_fusion), calls=%async_computation.4 | async-start | bytes 393216 | tf_op jit(solution)/shard_map/all_to_all | solution.py:271
  227.4 10.7 %all-to-all-start.5 = ((bf16[16,16,128]{2,1,0:T(8,128)(2,1)}), bf16[16,16,128]{2,1,0:T(8,128)(2,1)S(1)}, u32[]{:S(2)}, u32[]{:S(2)}) async-start(bf16[16,16,128]{2,1,0:T(8,128)(2,1)} %broadcast_in_dim.10), calls=%async_computation.5 | async-start | bytes 131072 | tf_op jit(solution)/shard_map/all_to_all | solution.py:271
  259.5 0.6 copy-start.4
Sparse Core Ops, SparseCore 0:
  120.2 84.7 reduce-scatter.3

commit v4 on v3

--- a/solution.py
+++ b/solution.py
@@ -460,7 +460,7 @@
             pltpu.VMEM((2, cells, channels), f32),
         ],
         compiler_params=params(60, ("arbitrary",)),
-        cost_estimate=cost(20 * 10**9, 8 * MIB),
+        cost_estimate=cost(10**8, MIB),
         name="weight_grad",
     )(occupancy, live, features, cotangent, rim, coef)
 
@@ -556,7 +556,7 @@
     conv_pipeline(edge, pad_s, (), w_ref, side_s, found_s, plane, 0)
 
 
-def convs_kernel(edge, occ_ref, live_ref, f_ref, pad_ref, shift_ref, back_ref, coef_ref, bias_ref,
+def convs_kernel(edge, occ_ref, live_ref, f_ref, g_ref, pad_ref, shift_ref, back_ref, coef_ref, bias_ref,
                  hid_hbm, rim_hbm, forward_hbm, hat_hbm, sum_ref, out_ref,
                  side_s, found_s, hat_s, hid_s, rim_s, forward_s, pad_s, shift_s, xh_s, edge_s, sems):
     channels = f_ref.shape[-1]
@@ -587,7 +587,7 @@
             pre = normed * scale + shift
             gate = jax.nn.sigmoid(pre)
             hat = jnp.where(mask, back * (gate * (1.0 + pre * (1.0 - gate))) * scale, 0.0)
-            hat_s[turn, z] = hat
+            hat_s[turn, z] = g_ref[0, z].astype(f32) + rstd * hat
             first = first + jnp.sum(hat, axis=0, keepdims=True)
             second = second + jnp.sum(hat * normed, axis=0, keepdims=True)
             return (first, second)
@@ -598,6 +598,14 @@
         sum_ref[1:2, :] = sum_ref[1:2, :] + second
 
     for slot in range(2):
+
+        @pl.when(jnp.logical_and(turn == slot, live_ref[slot] == 0))
+        def _():
+            def plane(z, carry):
+                hat_s[slot, z] = g_ref[0, z].astype(f32)
+                return carry
+
+            lax.fori_loop(0, edge, plane, 0)
 
         @pl.when(turn == slot)
         def _():
@@ -639,7 +647,7 @@
     ]
 
 
-def convs(occupancy, live, features, padded, shifted, back_weight, coef, bias, hidden, rim, forward_weight):
+def convs(occupancy, live, features, cotangent, padded, shifted, back_weight, coef, bias, hidden, rim, forward_weight):
     edge, channels = features.shape[1], features.shape[-1]
     cells = edge * edge
     block = (1, edge, cells, channels)
@@ -660,6 +668,7 @@
             SMEM,
             SMEM,
             pl.BlockSpec(block, lambda t: (t % 2, 0, 0, 0)),
+            pl.BlockSpec(block, lambda t: (jnp.minimum(t, 1), 0, 0, 0)),
             pl.BlockSpec((1,) + padded.shape[1:], lambda t: (jnp.minimum(t, 1), 0, 0, 0, 0)),
             pl.BlockSpec((1,) + shifted.shape[1:], lambda t: (jnp.minimum(t, 1), 0, 0, 0, 0, 0)),
             pl.BlockSpec(back_weight.shape, lambda t: (0, 0)),
@@ -682,7 +691,7 @@
         compiler_params=params(60, ("arbitrary",)),
         cost_estimate=cost(30 * 10**9, 16 * MIB),
         name="convs",
-    )(occupancy, live, features, padded, shifted, back_weight, coef, bias, hidden, rim, forward_weight)
+    )(occupancy, live, features, cotangent, padded, shifted, back_weight, coef, bias, hidden, rim, forward_weight)
 
 
 def forward_kernel(edge, slot, occ_ref, live_ref, f_ref, hid_ref, rim_ref, w_ref, coef_ref, bias_ref, base_ref,
@@ -724,43 +733,6 @@
     )(occupancy, live, features, hidden, rim, weight, coef, bias, base)
 
 
-def finish_kernel(edge, occ_ref, live_ref, f_ref, g_ref, hat_ref, coef_ref, sums_ref, out_ref):
-    channels = f_ref.shape[-1]
-    slot = pl.program_id(0)
-    mean, rstd = coef_ref[0:1, :], coef_ref[1:2, :]
-    first, second = sums_ref[0:1, :], sums_ref[1:2, :]
-
-    @pl.when(live_ref[slot] == 0)
-    def _():
-        out_ref[...] = g_ref[...]
-
-    @pl.when(live_ref[slot] != 0)
-    def _():
-        def plane(z, carry):
-            mask = plane_mask(occ_ref, slot, z, edge, channels)
-            normed = (f_ref[0, z].astype(f32) - mean) * rstd
-            change = rstd * (hat_ref[0, z] - first - normed * second)
-            out_ref[0, z] = (g_ref[0, z].astype(f32) + jnp.where(mask, change, 0.0)).astype(bf16)
-            return carry
-
-        lax.fori_loop(0, edge, plane, 0)
-
-
-def finish(occupancy, live, features, cotangent, hat, coef, sums):
-    edge, channels = features.shape[1], features.shape[-1]
-    few = pl.BlockSpec((1, edge, edge * edge, channels), lambda s: (s, 0, 0, 0))
-    return pl.pallas_call(
-        functools.partial(finish_kernel, edge),
-        grid=(2,),
-        out_shape=jax.ShapeDtypeStruct(features.shape, bf16),
-        in_specs=[SMEM, SMEM, few, few, few] + [pl.BlockSpec((8, channels), lambda s: (0, 0))] * 2,
-        out_specs=few,
-        compiler_params=params(60, ("arbitrary",)),
-        cost_estimate=cost(0, 12 * MIB),
-        name="finish",
-    )(occupancy, live, features, cotangent, hat, coef, sums)
-
-
 def wide_round(values, step):
     count = lax.axis_size("wide")
     terms = [values]
@@ -777,18 +749,39 @@
     return jnp.dot(rows, same, precision=lax.Precision.HIGHEST)
 
 
-def scale_kernel(rows, parts_ref, coef_ref, out_ref, sums_ref):
-    channels = parts_ref.shape[-1]
-    tail = jnp.zeros((parts_ref.shape[1] - rows, channels), f32)
+def last_kernel(edge, rows, occ_ref, coef_ref, parts_hbm, f_hbm, hat_hbm, step_hbm, out_hbm,
+                parts_s, f_s, hat_s, step_s, out_s, sems):
+    channels = parts_s.shape[-1]
+    few = edge // 2
+    blocks = [(slot, pl.ds(half * few, few)) for slot in range(2) for half in range(2)]
+    fetch = pltpu.make_async_copy(parts_hbm, parts_s, sems.at[0])
+    fetches = [
+        (
+            pltpu.make_async_copy(f_hbm.at[block], f_s.at[block], sems.at[2 + 2 * i]),
+            pltpu.make_async_copy(hat_hbm.at[block], hat_s.at[block], sems.at[3 + 2 * i]),
+        )
+        for i, block in enumerate(blocks)
+    ]
+    stores = [
+        pltpu.make_async_copy(out_s.at[block], out_hbm.at[block], sems.at[10 + i]) for i, block in enumerate(blocks)
+    ]
+    store = pltpu.make_async_copy(step_s, step_hbm, sems.at[1])
+    fetch.start()
+    for pair in fetches:
+        pair[0].start()
+        pair[1].start()
+    fetch.wait()
+    tail = jnp.zeros((parts_s.shape[1] - rows, channels), f32)
     total = jnp.zeros((1, channels), f32)
-    for part in range(parts_ref.shape[0]):
-        values = parts_ref[part, 0:rows].astype(f32)
+    for part in range(parts_s.shape[0]):
+        values = parts_s[part, 0:rows].astype(f32)
         total = total + jnp.sum(values * values, axis=0, keepdims=True)
-        tail = tail + parts_ref[part, rows:].astype(f32)
-    mean = jnp.sum(total, axis=1, keepdims=True) / out_ref.size
+        tail = tail + parts_s[part, rows:].astype(f32)
+    mean = jnp.sum(total, axis=1, keepdims=True) / step_s.size
     factor = lax.rsqrt(mean + step_eps)
-    for part in range(parts_ref.shape[0]):
-        out_ref[part] = parts_ref[part, 0:rows].astype(f32) * factor
+    for part in range(parts_s.shape[0]):
+        step_s[part] = parts_s[part, 0:rows].astype(f32) * factor
+    store.start()
     first = tail[0:1] + tail[1:2] + tail[2:3]
     second = tail[3:4] + tail[4:5] + tail[5:6]
     both = jnp.concatenate([first, second] + [jnp.zeros_like(first)] * 6, axis=0)
@@ -796,15 +789,58 @@
     column = lax.broadcasted_iota(jnp.int32, (channels, channels), 1) // (channels // G)
     same = (row == column).astype(f32)
     grouped = jnp.dot(both, same, precision=lax.Precision.HIGHEST, preferred_element_type=f32)
-    sums_ref[...] = grouped / coef_ref[4:5, :]
-
-
-def reduce_weights(grads, sums, coef, tie):
+    mean, rstd = coef_ref[0:1, :], coef_ref[1:2, :]
+    first = grouped[0:1] / coef_ref[4:5, :]
+    second = grouped[1:2] / coef_ref[4:5, :]
+    for i, (slot, _) in enumerate(blocks):
+        fetches[i][0].wait()
+        fetches[i][1].wait()
+
+        def plane(z, carry):
+            mask = plane_mask(occ_ref, slot, z, edge, channels)
+            normed = (f_s[slot, z].astype(f32) - mean) * rstd
+            change = jnp.where(mask, rstd * (first + normed * second), 0.0)
+            out_s[slot, z] = (hat_s[slot, z] - change).astype(bf16)
+            return carry
+
+        lax.fori_loop(few * (i % 2), few * (i % 2) + few, plane, 0)
+        stores[i].start()
+    store.wait()
+    for each in stores:
+        each.wait()
+
+
+def last_step(occupancy, coef, parts, features, hat, rows):
+    wide, _, channels = parts.shape
+    any_space = pl.BlockSpec(memory_space=pl.ANY)
+    return pl.pallas_call(
+        functools.partial(last_kernel, features.shape[1], rows),
+        out_shape=(
+            jax.ShapeDtypeStruct((wide, rows, channels), f32),
+            jax.ShapeDtypeStruct(features.shape, bf16),
+        ),
+        in_specs=[SMEM, VMEM, any_space, any_space, any_space],
+        out_specs=(any_space, any_space),
+        scratch_shapes=[
+            pltpu.VMEM(parts.shape, bf16),
+            pltpu.VMEM(features.shape, bf16),
+            pltpu.VMEM(features.shape, f32),
+            pltpu.VMEM((wide, rows, channels), f32),
+            pltpu.VMEM(features.shape, bf16),
+            pltpu.SemaphoreType.DMA((14,)),
+        ],
+        compiler_params=params(60),
+        cost_estimate=cost(0, 12 * MIB),
+        name="last_step",
+    )(occupancy, coef, parts, features, hat)
+
+
+def reduce_weights(grads, sums, tie):
     shape = grads.shape
     channels = shape[2]
     wide, narrow = lax.axis_size("wide"), lax.axis_size("narrow")
     rows = shape[0] * shape[1] // wide
-    mine = lax.psum_scatter(grads.reshape(wide * rows, channels), "wide", scatter_dimension=0, tiled=True)
+    mine = jnp.sum(exchange(grads.reshape(wide, rows, channels), "wide"), axis=0)
     deep = -(-rows // (8 * narrow)) * 8
     mine = jnp.pad(mine, ((0, deep * narrow - rows), (0, 0))).reshape(narrow, deep, channels)
     sums = jnp.broadcast_to(sums[None], (narrow,) + sums.shape)
@@ -819,20 +855,8 @@
     mine = mine.reshape(narrow * deep, channels)[:rows]
     mine, tie = lax.optimization_barrier((mine, tie))
     mine = jnp.concatenate([mine, tail, jnp.zeros((2, channels), bf16)], axis=0)
-    parts = lax.all_gather(mine, "wide")
-    step, sums = pl.pallas_call(
-        functools.partial(scale_kernel, rows),
-        out_shape=(
-            jax.ShapeDtypeStruct((wide, rows, channels), f32),
-            jax.ShapeDtypeStruct((8, channels), f32),
-        ),
-        in_specs=[VMEM, VMEM],
-        out_specs=(VMEM, VMEM),
-        compiler_params=params(16),
-        cost_estimate=cost(0, 3 * MIB),
-        name="scale",
-    )(parts, coef)
-    return (step.reshape(shape), sums, tie)
+    parts = exchange(jnp.broadcast_to(mine[None], (wide,) + mine.shape), "wide")
+    return (parts, rows, tie)
 
 
 def local(
@@ -884,14 +908,16 @@
     coef = jnp.stack([mean, rstd, scale, shift, blank + voxel_count, blank, blank, blank])
 
     grads, padded, shifted, hidden = weight_grad(occupancy, live, features, out_cotangent, up_rim, coef)
+    grads, feat_rim = lax.optimization_barrier((grads, feat_rim))
     bias = conv_bias[None, :]
     hat, grad_sums, mixed = convs(
-        occupancy, live, features, padded, shifted, back_weight, coef, bias, hidden, feat_rim, forward_weight
+        occupancy, live, features, out_cotangent, padded, shifted, back_weight, coef, bias, hidden, feat_rim,
+        forward_weight,
     )
-    weight_step, grad_sums, mixed = reduce_weights(grads, grad_sums, coef, mixed)
+    parts, rows, mixed = reduce_weights(grads, grad_sums, mixed)
     mixed = forward_conv(1, occupancy, live, features, hidden, feat_rim, forward_weight, coef, bias, mixed)
-    feature_grad = finish(occupancy, live, features, out_cotangent, hat, coef, grad_sums)
-    return (mixed, feature_grad, weight_step)
+    weight_step, feature_grad = last_step(occupancy, coef, parts, features, hat, rows)
+    return (mixed, feature_grad, weight_step.reshape(conv_weight.shape))
 
 
 def solution(mesh):

time: 284 us -> 214 us (0.75)
  waiting for transfers between devices: 119 us -> 80.8 us
  blocking collectives: 19.5 us -> 0 us
  between operations: 15.6 us -> 2.49 us
  starting transfers between devices: 53.5 us -> 57.5 us
    unnamed x2 -> x0, waiting for transfers between devices: 57.9 us -> none
    all_gather x1 -> x0, blocking collectives: 19.5 us -> none  [reduce_weights(): parts = lax.all_gather(mine, 'wide')]
    all_to_all x6 -> x8, waiting for transfers between devices: 53.1 us -> 69.5 us  [exchange(): return lax.all_to_all(values, axis, split_axis=0, concat_axis=0, tiled=True)]
    all_to_all x6 -> x8, starting transfers between devices: 37.6 us -> 41.9 us  [exchange(): return lax.all_to_all(values, axis, split_axis=0, concat_axis=0, tiled=True)]
    ppermute x6, waiting for transfers between devices: 0.02 us -> 2.96 us  [wide_round(): terms.append(lax.ppermute(values, 'wide', route))]
    pallas_call x2 -> x1, Pallas kernels: 7.17 us -> 6.4 us  [last_step(): pl.pallas_call(functools.partial(last_kernel, features.shape[1], rows), o...]
  transfers between devices with their start and end apart: 17 -> 18, of which waited for: 10 -> 12; matrix products, arithmetic and copies ran while one was open for 3% -> 4% of each run, Pallas kernels for 14% -> 23%
where the time goes in v4:
time: 214 us; the launch traced here: 212 us
  waiting for transfers between devices  80.8 us (38%)
  Pallas kernels  59.5 us (28%)
  starting transfers between devices  57.5 us (27%)
  local copies, waits for them, and re-layouts  9.84 us (5%)
  between operations  2.49 us (1%)
    all_to_all x8, waiting for transfers between devices, exchange(): return lax.all_to_all(values, axis, split_axis=0, concat_axis=0, tiled=True)  69.5 us
    all_to_all x8, starting transfers between devices, exchange(): return lax.all_to_all(values, axis, split_axis=0, concat_axis=0, tiled=True)  41.9 us
    pallas_call x1, Pallas kernels, convs(): pl.pallas_call(functools.partial(convs_kernel, edge), grid=(3,), out_shap...  12.2 us
    pallas_call x2, Pallas kernels, surface(): pl.pallas_call(functools.partial(surface_kernel, edge, with_stats, fill),...  10.4 us
    pallas_call x1, Pallas kernels, weight_grad(): pl.pallas_call(functools.partial(weight_kernel, edge), grid=(2,), out_sha...  10.4 us
    pallas_call x1, Pallas kernels, forward_conv(): pl.pallas_call(functools.partial(forward_kernel, edge, slot), grid=(1,),...  9.35 us
    pallas_call x2, Pallas kernels, hub_rows(): pl.pallas_call(functools.partial(hub_kernel, edge, fill), out_shape=jax.S...  8.89 us
    ppermute x2, waiting for transfers between devices, hub_stage(): lax.ppermute(to_left, 'wide', [(i + 1, i) for i in range(count - 1)])  7.86 us
  transfers between devices with their start and end apart: 18, of which 12 were waited for; matrix products, arithmetic and copies ran while one was open for 4% of the time, Pallas kernels for 23%

profile of v4, /device:TPU:1, one launch (start us, length us, event | category | flops | bytes accessed | tf_op | source)
XLA Modules:
  0.0 212.3 jit_solution(66140097646952511)
XLA Ops:
  0.6 0.0 copy-start
  0.6 4.4 %surface.3 = bf16[16,13,16,128]{3,2,1,0:T(8,128)(2,1)} custom-call(s32[2,16,16]{2,1,0:T(8,128)} %occ_ref.11, bf16[2,16,256,128]{3,2,1,0:T(8,128)(2,1)} %g_ref.3), custom_call_target="tpu_custom_call" | custom-call | bytes 3145728 | tf_op jit(solution)/shard_map/surface/pallas_call | solution.py:128
  5.0 10.1 %all-to-all-start = ((bf16[16,13,16,128]{3,2,1,0:T(8,128)(2,1)}), bf16[16,13,16,128]{3,2,1,0:T(8,128)(2,1)S(1)}, u32[]{:S(2)}, u32[]{:S(2)}) async-start(bf16[16,13,16,128]{3,2,1,0:T(8,128)(2,1)} %surface.3), calls=%async_computation | async-start | bytes 1703936 | tf_op jit(solution)/shard_map/all_to_all | solution.py:271
  15.8 6.0 %surface.2 = bf16[16,13,16,128]{3,2,1,0:T(8,128)(2,1)} custom-call(s32[2,16,16]{2,1,0:T(8,128)} %occ_ref.11, bf16[2,16,256,128]{3,2,1,0:T(8,128)(2,1)} %f_hbm.1), custom_call_target="tpu_custom_call" | custom-call | bytes 3145728 | tf_op jit(solution)/shard_map/surface/pallas_call | solution.py:128
  21.8 1.0 rev.3
  22.8 2.4 %copy.23 = bf16[9,3,128,128]{2,1,3,0:T(4,128)(2,1)S(1)} copy(bf16[9,3,128,128]{3,2,1,0:T(8,128)(2,1)} %bitcast.38) | data formatting | bytes 1769472 | tf_op jit(solution)/shard_map/reshape | solution.py:884
  25.2 0.8 copy.22
  26.1 0.2 fusion.12
  26.3 0.0 copy-done.9
  26.3 0.0 copy-start.2
  26.4 1.7 copy_bitcast_fusion
  28.0 11.1 %all-to-all-done.got_ref = bf16[16,13,16,128]{3,2,1,0:T(8,128)(2,1)S(1)} async-done(((bf16[16,13,16,128]{3,2,1,0:T(8,128)(2,1)}), bf16[16,13,16,128]{3,2,1,0:T(8,128)(2,1)S(1)}, u32[]{:S(2)}, u32[]{:S(2)}) %all-to-all-start) | async-done | bytes 852000 | tf_op jit(solution)/shard_map/all_to_all | solution.py:271
  39.1 3.5 %all-to-all-start.1 = ((bf16[16,13,16,128]{3,2,1,0:T(8,128)(2,1)}), bf16[16,13,16,128]{3,2,1,0:T(8,128)(2,1)S(1)}, u32[]{:S(2)}, u32[]{:S(2)}) async-start(bf16[16,13,16,128]{3,2,1,0:T(8,128)(2,1)} %surface.2), calls=%async_computation.1 | async-start | bytes 1703936 | tf_op jit(solution)/shard_map/all_to_all | solution.py:271
  42.7 1.2 trade.2
  43.9 3.2 %collective-permute-start = (bf16[18,16,128]{2,1,0:T(8,128)(2,1)S(1)}, bf16[18,16,128]{2,1,0:T(8,128)(2,1)S(1)}, u32[]{:S(2)}, u32[]{:S(2)}) collective-permute-start(bf16[18,16,128]{2,1,0:T(8,128)(2,1)S(1)} %get-tuple-element.37), channel_id=1, source_target_pairs={{0,16},{16,32},{32,48},{48,64},{64,80},{80,96},{96,112},{112,128},... | collective-permute-start | bytes 221192 | tf_op jit(solution)/shard_map/ppermute | solution.py:277
  47.1 1.3 collective-permute-start.1
  48.4 0.1 pad_add_fusion.place_ref
  48.5 0.4 collective-permute-done.lower_ref
  48.9 3.9 %collective-permute-done.1.upper_ref = bf16[18,16,128]{2,1,0:T(8,128)(2,1)S(1)} collective-permute-done((bf16[18,16,128]{2,1,0:T(8,128)(2,1)S(1)}, bf16[18,16,128]{2,1,0:T(8,128)(2,1)S(1)}, u32[]{:S(2)}, u32[]{:S(2)}) %collective-permute-start.1) | collective-permute-done | bytes 73760 | tf_op jit(solution)/shard_map/ppermute | solution.py:278
  52.7 4.4 %hub_rows.2 = bf16[16,2,7,16,128]{4,3,2,1,0:T(8,128)(2,1)} custom-call(s32[2]{0:T(128)S(1)} %pad_add_fusion.place_ref, s32[1,16]{1,0:T(1,128)S(1)} %copy-done.2, s32[16,27]{1,0:T(8,128)S(1)} %copy-done.1, bf16[16,13,16,128]{3,2,1,0:T(8,128)(2,1)S(1)} %all-to-all-done.got_ref, bf16[18,16,128]{2,1,0:T(8,128)(2,1)S(1)} %collective-permute-done.lower_ref, ...), custom_call_target="tpu_custom_call" | custom-call | bytes 8388608 | tf_op jit(solution)/shard_map/hub_rows/pallas_call | solution.py:255
  57.2 9.2 %all-to-all-done.1.got_ref = bf16[16,13,16,128]{3,2,1,0:T(8,128)(2,1)S(1)} async-done(((bf16[16,13,16,128]{3,2,1,0:T(8,128)(2,1)}), bf16[16,13,16,128]{3,2,1,0:T(8,128)(2,1)S(1)}, u32[]{:S(2)}, u32[]{:S(2)}) %all-to-all-start.1) | async-done | bytes 852000 | tf_op jit(solution)/shard_map/all_to_all | solution.py:271
  66.4 3.5 %all-to-all-start.2 = ((bf16[16,2,7,16,128]{4,3,2,1,0:T(8,128)(2,1)}), bf16[16,2,7,16,128]{4,3,2,1,0:T(8,128)(2,1)S(1)}, u32[]{:S(2)}, u32[]{:S(2)}) async-start(bf16[16,2,7,16,128]{4,3,2,1,0:T(8,128)(2,1)} %hub_rows.2), calls=%async_computation.2 | async-start | bytes 1835008 | tf_op jit(solution)/shard_map/all_to_all | solution.py:271
  69.9 0.6 trade.3
  70.6 2.8 %collective-permute-start.4 = (f32[8,128]{1,0:T(8,128)S(1)}, f32[8,128]{1,0:T(8,128)S(1)}, u32[]{:S(2)}, u32[]{:S(2)}) collective-permute-start(f32[8,128]{1,0:T(8,128)S(1)} %get-tuple-element.41), channel_id=1, source_target_pairs={{0,48},{16,32},{32,16},{48,0},{64,112},{80,96},{96,80},{112,64},{1... | collective-permute-start | bytes 12296 | tf_op jit(solution)/shard_map/ppermute | solution.py:741
  73.4 0.4 collective-permute-start.3
  73.8 0.3 collective-permute-start.2
  74.1 3.1 %collective-permute-start.5 = (bf16[18,16,128]{2,1,0:T(8,128)(2,1)S(1)}, bf16[18,16,128]{2,1,0:T(8,128)(2,1)S(1)}, u32[]{:S(2)}, u32[]{:S(2)}) collective-permute-start(bf16[18,16,128]{2,1,0:T(8,128)(2,1)S(1)} %get-tuple-element.42), channel_id=1, source_target_pairs={{0,16},{16,32},{32,48},{48,64},{64,80},{80,96},{96,112},{112,128},... | collective-permute-start | bytes 221192 | tf_op jit(solution)/shard_map/ppermute | solution.py:277
  77.1 1.3 collective-permute-start.6
  78.4 0.0 collective-permute-done.4
  78.5 0.0 collective-permute-done.3
  78.5 0.0 collective-permute-done.5.lower_ref
  78.5 4.0 %collective-permute-done.6.upper_ref = bf16[18,16,128]{2,1,0:T(8,128)(2,1)S(1)} collective-permute-done((bf16[18,16,128]{2,1,0:T(8,128)(2,1)S(1)}, bf16[18,16,128]{2,1,0:T(8,128)(2,1)S(1)}, u32[]{:S(2)}, u32[]{:S(2)}) %collective-permute-start.6) | collective-permute-done | bytes 73760 | tf_op jit(solution)/shard_map/ppermute | solution.py:278
  82.5 4.4 %hub_rows.3 = bf16[16,2,7,16,128]{4,3,2,1,0:T(8,128)(2,1)} custom-call(s32[2]{0:T(128)S(1)} %pad_add_fusion.place_ref, s32[1,16]{1,0:T(1,128)S(1)} %copy-done.2, s32[16,27]{1,0:T(8,128)S(1)} %copy-done.1, bf16[16,13,16,128]{3,2,1,0:T(8,128)(2,1)S(1)} %all-to-all-done.1.got_ref, bf16[18,16,128]{2,1,0:T(8,128)(2,1)S(1)} %collective-permute-done.5.lower_ref, ...), custom_call_target="tpu_custom_call" | custom-call | bytes 8388608 | tf_op jit(solution)/shard_map/hub_rows/pallas_call | solution.py:255
  87.0 8.0 %all-to-all-done.2.rim_ref = bf16[16,2,7,16,128]{4,3,2,1,0:T(8,128)(2,1)S(1)} async-done(((bf16[16,2,7,16,128]{4,3,2,1,0:T(8,128)(2,1)}), bf16[16,2,7,16,128]{4,3,2,1,0:T(8,128)(2,1)S(1)}, u32[]{:S(2)}, u32[]{:S(2)}) %all-to-all-start.2) | async-done | bytes 917536 | tf_op jit(solution)/shard_map/all_to_all | solution.py:271
  94.9 3.5 %all-to-all-start.3 = ((bf16[16,2,7,16,128]{4,3,2,1,0:T(8,128)(2,1)}), bf16[16,2,7,16,128]{4,3,2,1,0:T(8,128)(2,1)S(1)}, u32[]{:S(2)}, u32[]{:S(2)}) async-start(bf16[16,2,7,16,128]{4,3,2,1,0:T(8,128)(2,1)} %hub_rows.3), calls=%async_computation.3 | async-start | bytes 1835008 | tf_op jit(solution)/shard_map/all_to_all | solution.py:271
  98.5 0.2 compare_reduce_fusion
  98.7 2.6 %collective-permute-start.9 = (f32[8,128]{1,0:T(8,128)S(1)}, f32[8,128]{1,0:T(8,128)S(1)}, u32[]{:S(2)}, u32[]{:S(2)}) collective-permute-start(f32[8,128]{1,0:T(8,128)S(1)} %add_add_fusion.1), channel_id=1, source_target_pairs={{0,192},{16,208},{32,224},{48,240},{64,128},{80,144},{96,160},{112... | collective-permute-start | bytes 12296 | tf_op jit(solution)/shard_map/ppermute | solution.py:741
  101.2 0.5 collective-permute-start.8
  101.8 0.3 collective-permute-start.7
  102.0 0.5 convert_element_type.17.live_ref
  102.6 2.9 %collective-permute-done.8 = f32[8,128]{1,0:T(8,128)S(1)} collective-permute-done((f32[8,128]{1,0:T(8,128)S(1)}, f32[8,128]{1,0:T(8,128)S(1)}, u32[]{:S(2)}, u32[]{:S(2)}) %collective-permute-start.8) | collective-permute-done | bytes 4128 | tf_op jit(solution)/shard_map/ppermute | solution.py:741
  105.5 0.5 slice.33
  106.7 0.2 fusion
  106.9 0.6 stack.46.coef_ref
  107.6 10.4 %weight_grad.1 = (f32[27,128,128]{2,1,0:T(8,128)}, bf16[2,18,18,16,128]{4,3,2,1,0:T(8,128)(2,1)}, bf16[2,2,3,18,16,128]{5,4,3,2,1,0:T(8,128)(2,1)}, bf16[2,16,256,128]{3,2,1,0:T(8,128)(2,1)}) custom-call(s32[2,16,16]{2,1,0:T(8,128)} %occ_ref.11, s32[2]{0:T(128)} %convert_element_type.17.live_ref, bf16[2,16,256,128]{3,2,1,0:T(8,128)(2,1)} %f_hbm.1, ...), custom_call_target="tpu_custom_call" | custom-call | flops 100000000 | bytes 1048576 | tf_op jit(solution)/shard_map/weight_grad/pallas_call | solution.py:430
  117.9 5.7 %all-to-all-done.3.rim_hbm.rim_ref = bf16[16,2,7,16,128]{4,3,2,1,0:T(8,128)(2,1)S(1)} async-done(((bf16[16,2,7,16,128]{4,3,2,1,0:T(8,128)(2,1)}), bf16[16,2,7,16,128]{4,3,2,1,0:T(8,128)(2,1)S(1)}, u32[]{:S(2)}, u32[]{:S(2)}) %all-to-all-start.3) | async-done | bytes 917536 | tf_op jit(solution)/shard_map/all_to_all | solution.py:271
  123.6 6.8 %all-to-all-start.4 = ((f32[16,216,128]{2,1,0:T(8,128)}), f32[16,216,128]{2,1,0:T(8,128)S(1)}, u32[]{:S(2)}, u32[]{:S(2)}) async-start(f32[16,216,128]{2,1,0:T(8,128)} %bitcast.39), calls=%async_computation.4 | async-start | bytes 3538944 | tf_op jit(solution)/shard_map/all_to_all | solution.py:271
  130.4 12.2 %convs.1 = (f32[2,16,256,128]{3,2,1,0:T(8,128)}, f32[8,128]{1,0:T(8,128)}, bf16[2,16,256,128]{3,2,1,0:T(8,128)(2,1)}) custom-call(s32[2,16,16]{2,1,0:T(8,128)} %occ_ref.11, s32[2]{0:T(128)} %convert_element_type.17.live_ref, bf16[2,16,256,128]{3,2,1,0:T(8,128)(2,1)} %f_hbm.1, bf16[2,16,256,128]{3,2,1,0:T(8,128)(2,1)} %g_ref.3, ...), custom_call_target="tpu_custom_call" | custom-call | flops 30000001024 | bytes 16777216 | tf_op jit(solution)/shard_map/convs/pallas_call | solution.py:659
  142.6 13.7 %all-to-all-done.4 = f32[16,216,128]{2,1,0:T(8,128)S(1)} async-done(((f32[16,216,128]{2,1,0:T(8,128)}), f32[16,216,128]{2,1,0:T(8,128)S(1)}, u32[]{:S(2)}, u32[]{:S(2)}) %all-to-all-start.4) | async-done | bytes 1769504 | tf_op jit(solution)/shard_map/all_to_all | solution.py:271
  156.2 0.1 reduce_sum.18
  156.4 0.7 pad_maximum_fusion
  157.1 5.9 %all-to-all-start.5 = ((f32[16,24,128]{2,1,0:T(8,128)}), f32[16,24,128]{2,1,0:T(8,128)S(1)}, u32[]{:S(2)}, u32[]{:S(2)}) async-start(f32[16,24,128]{2,1,0:T(8,128)} %pad_maximum_fusion), calls=%async_computation.5 | async-start | bytes 393216 | tf_op jit(solution)/shard_map/all_to_all | solution.py:271
  163.0 0.1 pad.7.clone
  163.0 10.2 %all-to-all-done.5 = f32[16,24,128]{2,1,0:T(8,128)S(1)} async-done(((f32[16,24,128]{2,1,0:T(8,128)}), f32[16,24,128]{2,1,0:T(8,128)S(1)}, u32[]{:S(2)}, u32[]{:S(2)}) %all-to-all-start.5) | async-done | bytes 196640 | tf_op jit(solution)/shard_map/all_to_all | solution.py:271
  173.3 0.6 broadcast_in_dim.12
  174.0 3.4 %all-to-all-start.6 = ((bf16[16,16,128]{2,1,0:T(8,128)(2,1)}), bf16[16,16,128]{2,1,0:T(8,128)(2,1)S(1)}, u32[]{:S(2)}, u32[]{:S(2)}) async-start(bf16[16,16,128]{2,1,0:T(8,128)(2,1)} %broadcast_in_dim.12), calls=%async_computation.6 | async-start | bytes 131072 | tf_op jit(solution)/shard_map/all_to_all | solution.py:271
  177.4 7.3 %all-to-all-done.6 = bf16[16,16,128]{2,1,0:T(8,128)(2,1)S(1)} async-done(((bf16[16,16,128]{2,1,0:T(8,128)(2,1)}), bf16[16,16,128]{2,1,0:T(8,128)(2,1)S(1)}, u32[]{:S(2)}, u32[]{:S(2)}) %all-to-all-start.6) | async-done | bytes 65568 | tf_op jit(solution)/shard_map/all_to_all | solution.py:271
  184.7 0.1 maximum_maximum_fusion
  184.8 1.0 broadcast_in_dim.14
  185.9 5.1 %all-to-all-start.7 = ((bf16[16,224,128]{2,1,0:T(8,128)(2,1)}), bf16[16,224,128]{2,1,0:T(8,128)(2,1)S(1)}, u32[]{:S(2)}, u32[]{:S(2)}) async-start(bf16[16,224,128]{2,1,0:T(8,128)(2,1)} %broadcast_in_dim.14), calls=%async_computation.7 | async-start | bytes 1835008 | tf_op jit(solution)/shard_map/all_to_all | solution.py:271
  191.0 9.3 %forward_conv.1 = bf16[2,16,256,128]{3,2,1,0:T(8,128)(2,1)} custom-call(s32[2,16,16]{2,1,0:T(8,128)} %occ_ref.11, s32[2]{0:T(128)} %convert_element_type.17.live_ref, bf16[2,16,256,128]{3,2,1,0:T(8,128)(2,1)} %f_hbm.1, bf16[2,16,256,128]{3,2,1,0:T(8,128)(2,1)} %get-tuple-element.51.hid_hbm.hid_ref, ...), custom_call_target="tpu_custom_call", output_to_operand_aliasing={{}: (8, {})} | custom-call | flops 10000000000 | bytes 4194304 | tf_op jit(solution)/shard_map/forward_conv/pallas_call | solution.py:712
  200.3 4.4 %all-to-all-done.7.parts_hbm = bf16[16,224,128]{2,1,0:T(8,128)(2,1)S(1)} async-done(((bf16[16,224,128]{2,1,0:T(8,128)(2,1)}), bf16[16,224,128]{2,1,0:T(8,128)(2,1)S(1)}, u32[]{:S(2)}, u32[]{:S(2)}) %all-to-all-start.7) | async-done | bytes 917536 | tf_op jit(solution)/shard_map/all_to_all | solution.py:271
  204.8 1.0 copy-done.3
  205.7 6.4 %last_step.1 = (f32[16,216,128]{2,1,0:T(8,128)}, bf16[2,16,256,128]{3,2,1,0:T(8,128)(2,1)}) custom-call(s32[2,16,16]{2,1,0:T(8,128)} %occ_ref.11, f32[8,128]{1,0:T(8,128)} %stack.46.coef_ref, bf16[16,224,128]{2,1,0:T(8,128)(2,1)} %copy-done.3, bf16[2,16,256,128]{3,2,1,0:T(8,128)(2,1)} %f_hbm.1, f32[2,16,256,128]{3,2,1,0:T(8,128)} %get-tuple-element.66.hat_hbm), custom_call_target="tpu_custom_call" | custom-call | bytes 12582912 | tf_op jit(solution)/shard_map/last_step/pallas_call | solution.py:816
  (40 shorter events, 0.3 us)
Async XLA Ops:
  0.6 25.5 %copy-start = (f32[256,256]{1,0:T(8,128)S(1)}, f32[256,256]{1,0:T(8,128)}, u32[]{:S(2)}) copy-start(f32[256,256]{1,0:T(8,128)} %param.19) | copy-start | bytes 786436
  5.0 16.8 %copy-start.5 = (bf16[27,128,128]{2,1,0:T(8,128)(2,1)S(1)}, bf16[27,128,128]{2,1,0:T(8,128)(2,1)}, u32[]{:S(2)}) copy-start(bf16[27,128,128]{2,1,0:T(8,128)(2,1)} %param.20) | copy-start | bytes 2654212
  5.0 34.1 %all-to-all-start = ((bf16[16,13,16,128]{3,2,1,0:T(8,128)(2,1)}), bf16[16,13,16,128]{3,2,1,0:T(8,128)(2,1)S(1)}, u32[]{:S(2)}, u32[]{:S(2)}) async-start(bf16[16,13,16,128]{3,2,1,0:T(8,128)(2,1)} %surface.3), calls=%async_computation | async-start | bytes 1703936 | tf_op jit(solution)/shard_map/all_to_all | solution.py:271
  22.8 3.5 %copy-start.8 = (f32[128]{0:T(128)S(1)}, f32[128]{0:T(128)}, u32[]{:S(2)}) copy-start(f32[128]{0:T(128)} %param.18) | copy-start | bytes 1540
  22.8 3.5 %copy-start.9 = (f32[128]{0:T(128)S(1)}, f32[128]{0:T(128)}, u32[]{:S(2)}) copy-start(f32[128]{0:T(128)} %param.17) | copy-start | bytes 1540
  26.3 16.3 %copy-start.2 = (s32[1,16]{1,0:T(1,128)S(1)}, s32[1,16]{1,0:T(1,128)}, u32[]{:S(2)}) copy-start(s32[1,16]{1,0:T(1,128)} %live_ref.7) | copy-start | bytes 196
  28.0 24.7 %copy-start.1 = (s32[16,27]{1,0:T(8,128)S(1)}, s32[16,27]{1,0:T(8,128)}, u32[]{:S(2)}) copy-start(s32[16,27]{1,0:T(8,128)} %near_ref.3) | copy-start | bytes 5188
  39.1 27.2 %all-to-all-start.1 = ((bf16[16,13,16,128]{3,2,1,0:T(8,128)(2,1)}), bf16[16,13,16,128]{3,2,1,0:T(8,128)(2,1)S(1)}, u32[]{:S(2)}, u32[]{:S(2)}) async-start(bf16[16,13,16,128]{3,2,1,0:T(8,128)(2,1)} %surface.2), calls=%async_computation.1 | async-start | bytes 1703936 | tf_op jit(solution)/shard_map/all_to_all | solution.py:271
  43.9 5.0 %collective-permute-start = (bf16[18,16,128]{2,1,0:T(8,128)(2,1)S(1)}, bf16[18,16,128]{2,1,0:T(8,128)(2,1)S(1)}, u32[]{:S(2)}, u32[]{:S(2)}) collective-permute-start(bf16[18,16,128]{2,1,0:T(8,128)(2,1)S(1)} %get-tuple-element.37), channel_id=1, source_target_pairs={{0,16},{16,32},{32,48},{48,64},{64,80},{80,96},{96,112},{112,128},... | collective-permute-start | bytes 221192 | tf_op jit(solution)/shard_map/ppermute | solution.py:277
  47.1 5.6 %collective-permute-start.1 = (bf16[18,16,128]{2,1,0:T(8,128)(2,1)S(1)}, bf16[18,16,128]{2,1,0:T(8,128)(2,1)S(1)}, u32[]{:S(2)}, u32[]{:S(2)}) collective-permute-start(bf16[18,16,128]{2,1,0:T(8,128)(2,1)S(1)} %get-tuple-element.38), channel_id=1, source_target_pairs={{16,0},{32,16},{48,32},{64,48},{80,64},{96,80},{112,96},{128,112},... | collective-permute-start | bytes 221192 | tf_op jit(solution)/shard_map/ppermute | solution.py:278
  66.4 28.6 %all-to-all-start.2 = ((bf16[16,2,7,16,128]{4,3,2,1,0:T(8,128)(2,1)}), bf16[16,2,7,16,128]{4,3,2,1,0:T(8,128)(2,1)S(1)}, u32[]{:S(2)}, u32[]{:S(2)}) async-start(bf16[16,2,7,16,128]{4,3,2,1,0:T(8,128)(2,1)} %hub_rows.2), calls=%async_computation.2 | async-start | bytes 1835008 | tf_op jit(solution)/shard_map/all_to_all | solution.py:271
  70.6 7.9 %collective-permute-start.4 = (f32[8,128]{1,0:T(8,128)S(1)}, f32[8,128]{1,0:T(8,128)S(1)}, u32[]{:S(2)}, u32[]{:S(2)}) collective-permute-start(f32[8,128]{1,0:T(8,128)S(1)} %get-tuple-element.41), channel_id=1, source_target_pairs={{0,48},{16,32},{32,16},{48,0},{64,112},{80,96},{96,80},{112,64},{1... | collective-permute-start | bytes 12296 | tf_op jit(solution)/shard_map/ppermute | solution.py:741
  73.4 5.1 %collective-permute-start.3 = (f32[8,128]{1,0:T(8,128)S(1)}, f32[8,128]{1,0:T(8,128)S(1)}, u32[]{:S(2)}, u32[]{:S(2)}) collective-permute-start(f32[8,128]{1,0:T(8,128)S(1)} %get-tuple-element.41), channel_id=1, source_target_pairs={{0,32},{16,48},{32,0},{48,16},{64,96},{80,112},{96,64},{112,80},{1... | collective-permute-start | bytes 12296 | tf_op jit(solution)/shard_map/ppermute | solution.py:741
  73.8 4.7 %collective-permute-start.2 = (f32[8,128]{1,0:T(8,128)S(1)}, f32[8,128]{1,0:T(8,128)S(1)}, u32[]{:S(2)}, u32[]{:S(2)}) collective-permute-start(f32[8,128]{1,0:T(8,128)S(1)} %get-tuple-element.41), channel_id=1, source_target_pairs={{0,16},{16,0},{32,48},{48,32},{64,80},{80,64},{96,112},{112,96},{1... | collective-permute-start | bytes 12296 | tf_op jit(solution)/shard_map/ppermute | solution.py:741
  74.1 4.5 %collective-permute-start.5 = (bf16[18,16,128]{2,1,0:T(8,128)(2,1)S(1)}, bf16[18,16,128]{2,1,0:T(8,128)(2,1)S(1)}, u32[]{:S(2)}, u32[]{:S(2)}) collective-permute-start(bf16[18,16,128]{2,1,0:T(8,128)(2,1)S(1)} %get-tuple-element.42), channel_id=1, source_target_pairs={{0,16},{16,32},{32,48},{48,64},{64,80},{80,96},{96,112},{112,128},... | collective-permute-start | bytes 221192 | tf_op jit(solution)/shard_map/ppermute | solution.py:277
  77.1 5.4 %collective-permute-start.6 = (bf16[18,16,128]{2,1,0:T(8,128)(2,1)S(1)}, bf16[18,16,128]{2,1,0:T(8,128)(2,1)S(1)}, u32[]{:S(2)}, u32[]{:S(2)}) collective-permute-start(bf16[18,16,128]{2,1,0:T(8,128)(2,1)S(1)} %get-tuple-element.43), channel_id=1, source_target_pairs={{16,0},{32,16},{48,32},{64,48},{80,64},{96,80},{112,96},{128,112},... | collective-permute-start | bytes 221192 | tf_op jit(solution)/shard_map/ppermute | solution.py:278
  94.9 12.6 %copy-start.4 = (bf16[16,2,7,16,128]{4,3,2,1,0:T(8,128)(2,1)}, bf16[16,2,7,16,128]{4,3,2,1,0:T(8,128)(2,1)S(1)}, u32[]{:S(2)}) copy-start(bf16[16,2,7,16,128]{4,3,2,1,0:T(8,128)(2,1)S(1)} %all-to-all-done.2.rim_ref) | copy-start | bytes 2752516
  94.9 28.6 %all-to-all-start.3 = ((bf16[16,2,7,16,128]{4,3,2,1,0:T(8,128)(2,1)}), bf16[16,2,7,16,128]{4,3,2,1,0:T(8,128)(2,1)S(1)}, u32[]{:S(2)}, u32[]{:S(2)}) async-start(bf16[16,2,7,16,128]{4,3,2,1,0:T(8,128)(2,1)} %hub_rows.3), calls=%async_computation.3 | async-start | bytes 1835008 | tf_op jit(solution)/shard_map/all_to_all | solution.py:271
  98.7 3.9 %collective-permute-start.9 = (f32[8,128]{1,0:T(8,128)S(1)}, f32[8,128]{1,0:T(8,128)S(1)}, u32[]{:S(2)}, u32[]{:S(2)}) collective-permute-start(f32[8,128]{1,0:T(8,128)S(1)} %add_add_fusion.1), channel_id=1, source_target_pairs={{0,192},{16,208},{32,224},{48,240},{64,128},{80,144},{96,160},{112... | collective-permute-start | bytes 12296 | tf_op jit(solution)/shard_map/ppermute | solution.py:741
  101.2 4.3 %collective-permute-start.8 = (f32[8,128]{1,0:T(8,128)S(1)}, f32[8,128]{1,0:T(8,128)S(1)}, u32[]{:S(2)}, u32[]{:S(2)}) collective-permute-start(f32[8,128]{1,0:T(8,128)S(1)} %add_add_fusion.1), channel_id=1, source_target_pairs={{0,128},{16,144},{32,160},{48,176},{64,192},{80,208},{96,224},{112... | collective-permute-start | bytes 12296 | tf_op jit(solution)/shard_map/ppermute | solution.py:741
  101.8 3.7 %collective-permute-start.7 = (f32[8,128]{1,0:T(8,128)S(1)}, f32[8,128]{1,0:T(8,128)S(1)}, u32[]{:S(2)}, u32[]{:S(2)}) collective-permute-start(f32[8,128]{1,0:T(8,128)S(1)} %add_add_fusion.1), channel_id=1, source_target_pairs={{0,64},{16,80},{32,96},{48,112},{64,0},{80,16},{96,32},{112,48},{1... | collective-permute-start | bytes 12296 | tf_op jit(solution)/shard_map/ppermute | solution.py:741
  123.6 6.8 %copy-start.6 = (bf16[16,2,7,16,128]{4,3,2,1,0:T(8,128)(2,1)}, bf16[16,2,7,16,128]{4,3,2,1,0:T(8,128)(2,1)S(1)}, u32[]{:S(2)}) copy-start(bf16[16,2,7,16,128]{4,3,2,1,0:T(8,128)(2,1)S(1)} %all-to-all-done.3.rim_hbm.rim_ref) | copy-start | bytes 2752516
  123.6 32.6 %all-to-all-start.4 = ((f32[16,216,128]{2,1,0:T(8,128)}), f32[16,216,128]{2,1,0:T(8,128)S(1)}, u32[]{:S(2)}, u32[]{:S(2)}) async-start(f32[16,216,128]{2,1,0:T(8,128)} %bitcast.39), calls=%async_computation.4 | async-start | bytes 3538944 | tf_op jit(solution)/shard_map/all_to_all | solution.py:271
  142.6 13.8 %copy-start.7 = (f32[8,128]{1,0:T(8,128)S(1)}, f32[8,128]{1,0:T(8,128)}, u32[]{:S(2)}) copy-start(f32[8,128]{1,0:T(8,128)} %get-tuple-element.62) | copy-start | bytes 12292
  157.1 16.2 %all-to-all-start.5 = ((f32[16,24,128]{2,1,0:T(8,128)}), f32[16,24,128]{2,1,0:T(8,128)S(1)}, u32[]{:S(2)}, u32[]{:S(2)}) async-start(f32[16,24,128]{2,1,0:T(8,128)} %pad_maximum_fusion), calls=%async_computation.5 | async-start | bytes 393216 | tf_op jit(solution)/shard_map/all_to_all | solution.py:271
  174.0 10.7 %all-to-all-start.6 = ((bf16[16,16,128]{2,1,0:T(8,128)(2,1)}), bf16[16,16,128]{2,1,0:T(8,128)(2,1)S(1)}, u32[]{:S(2)}, u32[]{:S(2)}) async-start(bf16[16,16,128]{2,1,0:T(8,128)(2,1)} %broadcast_in_dim.12), calls=%async_computation.6 | async-start | bytes 131072 | tf_op jit(solution)/shard_map/all_to_all | solution.py:271
  185.9 18.9 %all-to-all-start.7 = ((bf16[16,224,128]{2,1,0:T(8,128)(2,1)}), bf16[16,224,128]{2,1,0:T(8,128)(2,1)S(1)}, u32[]{:S(2)}, u32[]{:S(2)}) async-start(bf16[16,224,128]{2,1,0:T(8,128)(2,1)} %broadcast_in_dim.14), calls=%async_computation.7 | async-start | bytes 1835008 | tf_op jit(solution)/shard_map/all_to_all | solution.py:271
  204.8 1.0 copy-start.3

commit v5 on v4

--- a/solution.py
+++ b/solution.py
@@ -75,13 +75,13 @@
         values = v_ref[0, z].astype(f32)
         return (mask, values, jnp.where(mask, values, fill))
 
-    def step(z, carry):
+    def plane(z, place, carry):
         mask, values, shown = coded(z)
-        plane_s[...] = shown
+        plane_s[place] = shown
         for side in range(2):
             row = side * last
             out_ref[z, 4 + 2 * slot + side] = shown[row * edge : (row + 1) * edge].astype(bf16)
-            out_ref[z, 8 + 2 * slot + side] = plane_s[pl.ds(row, edge, stride=edge), :].astype(bf16)
+            out_ref[z, 8 + 2 * slot + side] = plane_s[place, pl.ds(row, edge, stride=edge), :].astype(bf16)
         if not with_stats:
             return carry
         total, squares, count = carry
@@ -91,8 +91,13 @@
         count = count + jnp.sum(mask.astype(f32), axis=0, keepdims=True)
         return (total, squares, count)
 
+    def step(i, carry):
+        for place in range(4):
+            carry = plane(4 * i + place, place, carry)
+        return carry
+
     zero = jnp.zeros((1, channels), f32)
-    found = lax.fori_loop(0, edge, step, (zero, zero, zero) if with_stats else 0)
+    found = lax.fori_loop(0, edge // 4, step, (zero, zero, zero) if with_stats else 0)
     if with_stats:
         for index in range(3):
             stat_s[index : index + 1, :] = stat_s[index : index + 1, :] + found[index]
@@ -132,7 +137,7 @@
         in_specs=[SMEM, pl.BlockSpec((1, edge, cells, channels), lambda s: (s, 0, 0, 0))],
         out_specs=pl.BlockSpec((edge, tiles, edge, channels), lambda s: (0, 0, 0, 0)),
         scratch_shapes=[
-            pltpu.VMEM((cells, channels), f32),
+            pltpu.VMEM((4, cells, channels), f32),
             pltpu.VMEM((edge, 16, channels), f32),
             pltpu.VMEM((8, channels), f32),
         ],
@@ -897,7 +902,7 @@
     up_rows, feat_got = lax.optimization_barrier((up_rows, feat_got))
     up_rim = exchange(up_rows, "narrow")
     feat_rows, stats = hub_stage(place, live_slots, neighbours, feat_got, float("inf"), True)
-    feat_rows, up_rim = lax.optimization_barrier((feat_rows, up_rim))
+    feat_rows, up_rim, stats = lax.optimization_barrier((feat_rows, up_rim, stats))
     feat_rim = exchange(feat_rows, "narrow")
 
     voxel_count = stats[2, 0] * group_width

time: 214 us -> 214 us (level)
  waiting for transfers between devices: 80.8 us -> 98 us
  Pallas kernels: 59.5 us -> 42.6 us
    all_to_all x8, waiting for transfers between devices: 69.5 us -> 89.6 us  [exchange(): return lax.all_to_all(values, axis, split_axis=0, concat_axis=0, tiled=True)]
    pallas_call x1, Pallas kernels: 9.35 us -> 3.27 us  [forward_conv(): pl.pallas_call(functools.partial(forward_kernel, edge, slot), grid=(1,),...]
    pallas_call x1, Pallas kernels: 10.4 us -> 4.83 us  [weight_grad(): pl.pallas_call(functools.partial(weight_kernel, edge), grid=(2,), out_sha...]
    pallas_call x1, Pallas kernels: 12.2 us -> 7.46 us  [convs(): pl.pallas_call(functools.partial(convs_kernel, edge), grid=(3,), out_shap...]
    ppermute x6, waiting for transfers between devices: 2.96 us -> 0.02 us  [wide_round(): terms.append(lax.ppermute(values, 'wide', route))]
  transfers between devices with their start and end apart: 18 -> 18, of which waited for: 12 -> 11; matrix products, arithmetic and copies ran while one was open for 4% -> 4% of each run, Pallas kernels for 23% -> 15%
where the time goes in v5:
time: 214 us; the launch traced here: 212 us
  waiting for transfers between devices  98 us (46%)
  starting transfers between devices  57.2 us (27%)
  Pallas kernels  42.6 us (20%)
  local copies, waits for them, and re-layouts  9.84 us (5%)
  between operations  2.48 us (1%)
    all_to_all x8, waiting for transfers between devices, exchange(): return lax.all_to_all(values, axis, split_axis=0, concat_axis=0, tiled=True)  89.6 us
    all_to_all x8, starting transfers between devices, exchange(): return lax.all_to_all(values, axis, split_axis=0, concat_axis=0, tiled=True)  41.5 us
    pallas_call x2, Pallas kernels, surface(): pl.pallas_call(functools.partial(surface_kernel, edge, with_stats, fill),...  9.84 us
    pallas_call x2, Pallas kernels, hub_rows(): pl.pallas_call(functools.partial(hub_kernel, edge, fill), out_shape=jax.S...  8.89 us
    ppermute x2, waiting for transfers between devices, hub_stage(): lax.ppermute(to_left, 'wide', [(i + 1, i) for i in range(count - 1)])  7.86 us
    pallas_call x1, Pallas kernels, convs(): pl.pallas_call(functools.partial(convs_kernel, edge), grid=(3,), out_shap...  7.46 us
    ppermute x6, starting transfers between devices, wide_round(): terms.append(lax.ppermute(values, 'wide', route))  6.88 us
    pallas_call x1, Pallas kernels, last_step(): pl.pallas_call(functools.partial(last_kernel, features.shape[1], rows), o...  6.4 us
  transfers between devices with their start and end apart: 18, of which 11 were waited for; matrix products, arithmetic and copies ran while one was open for 4% of the time, Pallas kernels for 15%

profile of v5, /device:TPU:1, one launch (start us, length us, event | category | flops | bytes accessed | tf_op | source)
XLA Modules:
  0.0 212.3 jit_solution(3004195855868893616)
XLA Ops:
  0.6 0.0 copy-start
  0.6 4.2 %surface.3 = bf16[16,13,16,128]{3,2,1,0:T(8,128)(2,1)} custom-call(s32[2,16,16]{2,1,0:T(8,128)} %occ_ref.11, bf16[2,16,256,128]{3,2,1,0:T(8,128)(2,1)} %g_ref.3), custom_call_target="tpu_custom_call" | custom-call | bytes 3145728 | tf_op jit(solution)/shard_map/surface/pallas_call | solution.py:133
  4.8 10.1 %all-to-all-start = ((bf16[16,13,16,128]{3,2,1,0:T(8,128)(2,1)}), bf16[16,13,16,128]{3,2,1,0:T(8,128)(2,1)S(1)}, u32[]{:S(2)}, u32[]{:S(2)}) async-start(bf16[16,13,16,128]{3,2,1,0:T(8,128)(2,1)} %surface.3), calls=%async_computation | async-start | bytes 1703936 | tf_op jit(solution)/shard_map/all_to_all | solution.py:276
  15.6 5.7 %surface.2 = bf16[16,13,16,128]{3,2,1,0:T(8,128)(2,1)} custom-call(s32[2,16,16]{2,1,0:T(8,128)} %occ_ref.11, bf16[2,16,256,128]{3,2,1,0:T(8,128)(2,1)} %f_hbm.1), custom_call_target="tpu_custom_call" | custom-call | bytes 3145728 | tf_op jit(solution)/shard_map/surface/pallas_call | solution.py:133
  21.3 1.0 rev.3
  22.2 2.4 %copy.23 = bf16[9,3,128,128]{2,1,3,0:T(4,128)(2,1)S(1)} copy(bf16[9,3,128,128]{3,2,1,0:T(8,128)(2,1)} %bitcast.38) | data formatting | bytes 1769472 | tf_op jit(solution)/shard_map/reshape | solution.py:889
  24.7 0.8 copy.22
  25.5 0.2 fusion.12
  25.7 0.0 copy-done.9
  25.8 0.0 copy-start.2
  25.8 1.7 copy_bitcast_fusion
  27.5 11.4 %all-to-all-done.got_ref = bf16[16,13,16,128]{3,2,1,0:T(8,128)(2,1)S(1)} async-done(((bf16[16,13,16,128]{3,2,1,0:T(8,128)(2,1)}), bf16[16,13,16,128]{3,2,1,0:T(8,128)(2,1)S(1)}, u32[]{:S(2)}, u32[]{:S(2)}) %all-to-all-start) | async-done | bytes 852000 | tf_op jit(solution)/shard_map/all_to_all | solution.py:276
  38.9 3.5 %all-to-all-start.1 = ((bf16[16,13,16,128]{3,2,1,0:T(8,128)(2,1)}), bf16[16,13,16,128]{3,2,1,0:T(8,128)(2,1)S(1)}, u32[]{:S(2)}, u32[]{:S(2)}) async-start(bf16[16,13,16,128]{3,2,1,0:T(8,128)(2,1)} %surface.2), calls=%async_computation.1 | async-start | bytes 1703936 | tf_op jit(solution)/shard_map/all_to_all | solution.py:276
  42.5 1.2 trade.2
  43.7 3.2 %collective-permute-start = (bf16[18,16,128]{2,1,0:T(8,128)(2,1)S(1)}, bf16[18,16,128]{2,1,0:T(8,128)(2,1)S(1)}, u32[]{:S(2)}, u32[]{:S(2)}) collective-permute-start(bf16[18,16,128]{2,1,0:T(8,128)(2,1)S(1)} %get-tuple-element.38), channel_id=1, source_target_pairs={{0,16},{16,32},{32,48},{48,64},{64,80},{80,96},{96,112},{112,128},... | collective-permute-start | bytes 221192 | tf_op jit(solution)/shard_map/ppermute | solution.py:282
  46.9 1.3 collective-permute-start.1
  48.2 0.1 pad_add_fusion.place_ref
  48.3 0.4 collective-permute-done.lower_ref
  48.7 3.9 %collective-permute-done.1.upper_ref = bf16[18,16,128]{2,1,0:T(8,128)(2,1)S(1)} collective-permute-done((bf16[18,16,128]{2,1,0:T(8,128)(2,1)S(1)}, bf16[18,16,128]{2,1,0:T(8,128)(2,1)S(1)}, u32[]{:S(2)}, u32[]{:S(2)}) %collective-permute-start.1) | collective-permute-done | bytes 73760 | tf_op jit(solution)/shard_map/ppermute | solution.py:283
  52.5 4.4 %hub_rows.2 = bf16[16,2,7,16,128]{4,3,2,1,0:T(8,128)(2,1)} custom-call(s32[2]{0:T(128)S(1)} %pad_add_fusion.place_ref, s32[1,16]{1,0:T(1,128)S(1)} %copy-done.2, s32[16,27]{1,0:T(8,128)S(1)} %copy-done.1, bf16[16,13,16,128]{3,2,1,0:T(8,128)(2,1)S(1)} %all-to-all-done.got_ref, bf16[18,16,128]{2,1,0:T(8,128)(2,1)S(1)} %collective-permute-done.lower_ref, ...), custom_call_target="tpu_custom_call" | custom-call | bytes 8388608 | tf_op jit(solution)/shard_map/hub_rows/pallas_call | solution.py:260
  57.0 9.2 %all-to-all-done.1.got_ref = bf16[16,13,16,128]{3,2,1,0:T(8,128)(2,1)S(1)} async-done(((bf16[16,13,16,128]{3,2,1,0:T(8,128)(2,1)}), bf16[16,13,16,128]{3,2,1,0:T(8,128)(2,1)S(1)}, u32[]{:S(2)}, u32[]{:S(2)}) %all-to-all-start.1) | async-done | bytes 852000 | tf_op jit(solution)/shard_map/all_to_all | solution.py:276
  66.2 3.5 %all-to-all-start.2 = ((bf16[16,2,7,16,128]{4,3,2,1,0:T(8,128)(2,1)}), bf16[16,2,7,16,128]{4,3,2,1,0:T(8,128)(2,1)S(1)}, u32[]{:S(2)}, u32[]{:S(2)}) async-start(bf16[16,2,7,16,128]{4,3,2,1,0:T(8,128)(2,1)} %hub_rows.2), calls=%async_computation.2 | async-start | bytes 1835008 | tf_op jit(solution)/shard_map/all_to_all | solution.py:276
  69.7 0.6 trade.3
  70.4 2.8 %collective-permute-start.4 = (f32[8,128]{1,0:T(8,128)S(1)}, f32[8,128]{1,0:T(8,128)S(1)}, u32[]{:S(2)}, u32[]{:S(2)}) collective-permute-start(f32[8,128]{1,0:T(8,128)S(1)} %get-tuple-element.42), channel_id=1, source_target_pairs={{0,48},{16,32},{32,16},{48,0},{64,112},{80,96},{96,80},{112,64},{1... | collective-permute-start | bytes 12296 | tf_op jit(solution)/shard_map/ppermute | solution.py:746
  73.2 0.4 collective-permute-start.3
  73.6 0.3 collective-permute-start.2
  73.9 3.1 %collective-permute-start.5 = (bf16[18,16,128]{2,1,0:T(8,128)(2,1)S(1)}, bf16[18,16,128]{2,1,0:T(8,128)(2,1)S(1)}, u32[]{:S(2)}, u32[]{:S(2)}) collective-permute-start(bf16[18,16,128]{2,1,0:T(8,128)(2,1)S(1)} %get-tuple-element.43), channel_id=1, source_target_pairs={{0,16},{16,32},{32,48},{48,64},{64,80},{80,96},{96,112},{112,128},... | collective-permute-start | bytes 221192 | tf_op jit(solution)/shard_map/ppermute | solution.py:282
  76.9 1.3 collective-permute-start.6
  78.2 0.0 collective-permute-done.4
  78.2 0.0 collective-permute-done.3
  78.3 0.0 collective-permute-done.5.lower_ref
  78.3 4.0 %collective-permute-done.6.upper_ref = bf16[18,16,128]{2,1,0:T(8,128)(2,1)S(1)} collective-permute-done((bf16[18,16,128]{2,1,0:T(8,128)(2,1)S(1)}, bf16[18,16,128]{2,1,0:T(8,128)(2,1)S(1)}, u32[]{:S(2)}, u32[]{:S(2)}) %collective-permute-start.6) | collective-permute-done | bytes 73760 | tf_op jit(solution)/shard_map/ppermute | solution.py:283
  82.3 2.8 %collective-permute-start.9 = (f32[8,128]{1,0:T(8,128)S(1)}, f32[8,128]{1,0:T(8,128)S(1)}, u32[]{:S(2)}, u32[]{:S(2)}) collective-permute-start(f32[8,128]{1,0:T(8,128)S(1)} %add_add_fusion.1), channel_id=1, source_target_pairs={{0,192},{16,208},{32,224},{48,240},{64,128},{80,144},{96,160},{112... | collective-permute-start | bytes 12296 | tf_op jit(solution)/shard_map/ppermute | solution.py:746
  85.1 0.5 collective-permute-start.8
  85.6 0.1 collective-permute-start.7
  85.7 4.4 %hub_rows.3 = bf16[16,2,7,16,128]{4,3,2,1,0:T(8,128)(2,1)} custom-call(s32[2]{0:T(128)S(1)} %pad_add_fusion.place_ref, s32[1,16]{1,0:T(1,128)S(1)} %copy-done.2, s32[16,27]{1,0:T(8,128)S(1)} %copy-done.1, bf16[16,13,16,128]{3,2,1,0:T(8,128)(2,1)S(1)} %all-to-all-done.1.got_ref, bf16[18,16,128]{2,1,0:T(8,128)(2,1)S(1)} %collective-permute-done.5.lower_ref, ...), custom_call_target="tpu_custom_call" | custom-call | bytes 8388608 | tf_op jit(solution)/shard_map/hub_rows/pallas_call | solution.py:260
  90.2 0.0 collective-permute-done.7
  90.2 4.6 %all-to-all-done.2.rim_ref = bf16[16,2,7,16,128]{4,3,2,1,0:T(8,128)(2,1)S(1)} async-done(((bf16[16,2,7,16,128]{4,3,2,1,0:T(8,128)(2,1)}), bf16[16,2,7,16,128]{4,3,2,1,0:T(8,128)(2,1)S(1)}, u32[]{:S(2)}, u32[]{:S(2)}) %all-to-all-start.2) | async-done | bytes 917536 | tf_op jit(solution)/shard_map/all_to_all | solution.py:276
  94.7 5.1 %all-to-all-start.3 = ((bf16[16,2,7,16,128]{4,3,2,1,0:T(8,128)(2,1)}), bf16[16,2,7,16,128]{4,3,2,1,0:T(8,128)(2,1)S(1)}, u32[]{:S(2)}, u32[]{:S(2)}) async-start(bf16[16,2,7,16,128]{4,3,2,1,0:T(8,128)(2,1)} %hub_rows.3), calls=%async_computation.3 | async-start | bytes 1835008 | tf_op jit(solution)/shard_map/all_to_all | solution.py:276
  99.8 0.2 compare_reduce_fusion
  100.0 0.5 convert_element_type.17.live_ref
  100.6 0.5 slice.33
  101.7 0.2 fusion
  102.0 0.6 stack.46.coef_ref
  102.6 4.8 %weight_grad.1 = (f32[27,128,128]{2,1,0:T(8,128)}, bf16[2,18,18,16,128]{4,3,2,1,0:T(8,128)(2,1)}, bf16[2,2,3,18,16,128]{5,4,3,2,1,0:T(8,128)(2,1)}, bf16[2,16,256,128]{3,2,1,0:T(8,128)(2,1)}) custom-call(s32[2,16,16]{2,1,0:T(8,128)} %occ_ref.11, s32[2]{0:T(128)} %convert_element_type.17.live_ref, bf16[2,16,256,128]{3,2,1,0:T(8,128)(2,1)} %f_hbm.1, ...), custom_call_target="tpu_custom_call" | custom-call | flops 100000000 | bytes 1048576 | tf_op jit(solution)/shard_map/weight_grad/pallas_call | solution.py:435
  107.4 17.7 %all-to-all-done.3.rim_hbm.rim_ref = bf16[16,2,7,16,128]{4,3,2,1,0:T(8,128)(2,1)S(1)} async-done(((bf16[16,2,7,16,128]{4,3,2,1,0:T(8,128)(2,1)}), bf16[16,2,7,16,128]{4,3,2,1,0:T(8,128)(2,1)S(1)}, u32[]{:S(2)}, u32[]{:S(2)}) %all-to-all-start.3) | async-done | bytes 917536 | tf_op jit(solution)/shard_map/all_to_all | solution.py:276
  125.1 8.0 %all-to-all-start.4 = ((f32[16,216,128]{2,1,0:T(8,128)}), f32[16,216,128]{2,1,0:T(8,128)S(1)}, u32[]{:S(2)}, u32[]{:S(2)}) async-start(f32[16,216,128]{2,1,0:T(8,128)} %bitcast.39), calls=%async_computation.4 | async-start | bytes 3538944 | tf_op jit(solution)/shard_map/all_to_all | solution.py:276
  133.1 7.5 %convs.1 = (f32[2,16,256,128]{3,2,1,0:T(8,128)}, f32[8,128]{1,0:T(8,128)}, bf16[2,16,256,128]{3,2,1,0:T(8,128)(2,1)}) custom-call(s32[2,16,16]{2,1,0:T(8,128)} %occ_ref.11, s32[2]{0:T(128)} %convert_element_type.17.live_ref, bf16[2,16,256,128]{3,2,1,0:T(8,128)(2,1)} %f_hbm.1, bf16[2,16,256,128]{3,2,1,0:T(8,128)(2,1)} %g_ref.3, ...), custom_call_target="tpu_custom_call" | custom-call | flops 30000001024 | bytes 16777216 | tf_op jit(solution)/shard_map/convs/pallas_call | solution.py:664
  140.6 18.7 %all-to-all-done.4 = f32[16,216,128]{2,1,0:T(8,128)S(1)} async-done(((f32[16,216,128]{2,1,0:T(8,128)}), f32[16,216,128]{2,1,0:T(8,128)S(1)}, u32[]{:S(2)}, u32[]{:S(2)}) %all-to-all-start.4) | async-done | bytes 1769504 | tf_op jit(solution)/shard_map/all_to_all | solution.py:276
  159.3 0.1 reduce_sum.18
  159.5 0.7 pad_maximum_fusion
  160.1 4.2 %all-to-all-start.5 = ((f32[16,24,128]{2,1,0:T(8,128)}), f32[16,24,128]{2,1,0:T(8,128)S(1)}, u32[]{:S(2)}, u32[]{:S(2)}) async-start(f32[16,24,128]{2,1,0:T(8,128)} %pad_maximum_fusion), calls=%async_computation.5 | async-start | bytes 393216 | tf_op jit(solution)/shard_map/all_to_all | solution.py:276
  164.3 0.1 pad.7.clone
  164.4 10.2 %all-to-all-done.5 = f32[16,24,128]{2,1,0:T(8,128)S(1)} async-done(((f32[16,24,128]{2,1,0:T(8,128)}), f32[16,24,128]{2,1,0:T(8,128)S(1)}, u32[]{:S(2)}, u32[]{:S(2)}) %all-to-all-start.5) | async-done | bytes 196640 | tf_op jit(solution)/shard_map/all_to_all | solution.py:276
  174.7 0.6 broadcast_in_dim.12
  175.3 3.4 %all-to-all-start.6 = ((bf16[16,16,128]{2,1,0:T(8,128)(2,1)}), bf16[16,16,128]{2,1,0:T(8,128)(2,1)S(1)}, u32[]{:S(2)}, u32[]{:S(2)}) async-start(bf16[16,16,128]{2,1,0:T(8,128)(2,1)} %broadcast_in_dim.12), calls=%async_computation.6 | async-start | bytes 131072 | tf_op jit(solution)/shard_map/all_to_all | solution.py:276
  178.8 7.3 %all-to-all-done.6 = bf16[16,16,128]{2,1,0:T(8,128)(2,1)S(1)} async-done(((bf16[16,16,128]{2,1,0:T(8,128)(2,1)}), bf16[16,16,128]{2,1,0:T(8,128)(2,1)S(1)}, u32[]{:S(2)}, u32[]{:S(2)}) %all-to-all-start.6) | async-done | bytes 65568 | tf_op jit(solution)/shard_map/all_to_all | solution.py:276
  186.1 0.1 maximum_maximum_fusion
  186.2 1.0 broadcast_in_dim.14
  187.2 3.7 %all-to-all-start.7 = ((bf16[16,224,128]{2,1,0:T(8,128)(2,1)}), bf16[16,224,128]{2,1,0:T(8,128)(2,1)S(1)}, u32[]{:S(2)}, u32[]{:S(2)}) async-start(bf16[16,224,128]{2,1,0:T(8,128)(2,1)} %broadcast_in_dim.14), calls=%async_computation.7 | async-start | bytes 1835008 | tf_op jit(solution)/shard_map/all_to_all | solution.py:276
  190.9 3.3 %forward_conv.1 = bf16[2,16,256,128]{3,2,1,0:T(8,128)(2,1)} custom-call(s32[2,16,16]{2,1,0:T(8,128)} %occ_ref.11, s32[2]{0:T(128)} %convert_element_type.17.live_ref, bf16[2,16,256,128]{3,2,1,0:T(8,128)(2,1)} %f_hbm.1, bf16[2,16,256,128]{3,2,1,0:T(8,128)(2,1)} %get-tuple-element.53.hid_hbm.hid_ref, ...), custom_call_target="tpu_custom_call", output_to_operand_aliasing={{}: (8, {})} | custom-call | flops 10000000000 | bytes 4194304 | tf_op jit(solution)/shard_map/forward_conv/pallas_call | solution.py:717
  194.2 10.5 %all-to-all-done.7.parts_hbm = bf16[16,224,128]{2,1,0:T(8,128)(2,1)S(1)} async-done(((bf16[16,224,128]{2,1,0:T(8,128)(2,1)}), bf16[16,224,128]{2,1,0:T(8,128)(2,1)S(1)}, u32[]{:S(2)}, u32[]{:S(2)}) %all-to-all-start.7) | async-done | bytes 917536 | tf_op jit(solution)/shard_map/all_to_all | solution.py:276
  204.7 1.0 copy-done.3
  205.7 6.4 %last_step.1 = (f32[16,216,128]{2,1,0:T(8,128)}, bf16[2,16,256,128]{3,2,1,0:T(8,128)(2,1)}) custom-call(s32[2,16,16]{2,1,0:T(8,128)} %occ_ref.11, f32[8,128]{1,0:T(8,128)} %stack.46.coef_ref, bf16[16,224,128]{2,1,0:T(8,128)(2,1)} %copy-done.3, bf16[2,16,256,128]{3,2,1,0:T(8,128)(2,1)} %f_hbm.1, f32[2,16,256,128]{3,2,1,0:T(8,128)} %get-tuple-element.68.hat_hbm), custom_call_target="tpu_custom_call" | custom-call | bytes 12582912 | tf_op jit(solution)/shard_map/last_step/pallas_call | solution.py:821
  (40 shorter events, 0.3 us)
Async XLA Ops:
  0.6 24.9 %copy-start = (f32[256,256]{1,0:T(8,128)S(1)}, f32[256,256]{1,0:T(8,128)}, u32[]{:S(2)}) copy-start(f32[256,256]{1,0:T(8,128)} %param.19) | copy-start | bytes 786436
  4.8 16.4 %copy-start.5 = (bf16[27,128,128]{2,1,0:T(8,128)(2,1)S(1)}, bf16[27,128,128]{2,1,0:T(8,128)(2,1)}, u32[]{:S(2)}) copy-start(bf16[27,128,128]{2,1,0:T(8,128)(2,1)} %param.20) | copy-start | bytes 2654212
  4.8 34.1 %all-to-all-start = ((bf16[16,13,16,128]{3,2,1,0:T(8,128)(2,1)}), bf16[16,13,16,128]{3,2,1,0:T(8,128)(2,1)S(1)}, u32[]{:S(2)}, u32[]{:S(2)}) async-start(bf16[16,13,16,128]{3,2,1,0:T(8,128)(2,1)} %surface.3), calls=%async_computation | async-start | bytes 1703936 | tf_op jit(solution)/shard_map/all_to_all | solution.py:276
  22.2 3.5 %copy-start.8 = (f32[128]{0:T(128)S(1)}, f32[128]{0:T(128)}, u32[]{:S(2)}) copy-start(f32[128]{0:T(128)} %param.18) | copy-start | bytes 1540
  22.2 3.5 %copy-start.9 = (f32[128]{0:T(128)S(1)}, f32[128]{0:T(128)}, u32[]{:S(2)}) copy-start(f32[128]{0:T(128)} %param.17) | copy-start | bytes 1540
  25.8 16.7 %copy-start.2 = (s32[1,16]{1,0:T(1,128)S(1)}, s32[1,16]{1,0:T(1,128)}, u32[]{:S(2)}) copy-start(s32[1,16]{1,0:T(1,128)} %live_ref.7) | copy-start | bytes 196
  27.5 25.0 %copy-start.1 = (s32[16,27]{1,0:T(8,128)S(1)}, s32[16,27]{1,0:T(8,128)}, u32[]{:S(2)}) copy-start(s32[16,27]{1,0:T(8,128)} %near_ref.3) | copy-start | bytes 5188
  38.9 27.2 %all-to-all-start.1 = ((bf16[16,13,16,128]{3,2,1,0:T(8,128)(2,1)}), bf16[16,13,16,128]{3,2,1,0:T(8,128)(2,1)S(1)}, u32[]{:S(2)}, u32[]{:S(2)}) async-start(bf16[16,13,16,128]{3,2,1,0:T(8,128)(2,1)} %surface.2), calls=%async_computation.1 | async-start | bytes 1703936 | tf_op jit(solution)/shard_map/all_to_all | solution.py:276
  43.7 5.0 %collective-permute-start = (bf16[18,16,128]{2,1,0:T(8,128)(2,1)S(1)}, bf16[18,16,128]{2,1,0:T(8,128)(2,1)S(1)}, u32[]{:S(2)}, u32[]{:S(2)}) collective-permute-start(bf16[18,16,128]{2,1,0:T(8,128)(2,1)S(1)} %get-tuple-element.38), channel_id=1, source_target_pairs={{0,16},{16,32},{32,48},{48,64},{64,80},{80,96},{96,112},{112,128},... | collective-permute-start | bytes 221192 | tf_op jit(solution)/shard_map/ppermute | solution.py:282
  46.9 5.6 %collective-permute-start.1 = (bf16[18,16,128]{2,1,0:T(8,128)(2,1)S(1)}, bf16[18,16,128]{2,1,0:T(8,128)(2,1)S(1)}, u32[]{:S(2)}, u32[]{:S(2)}) collective-permute-start(bf16[18,16,128]{2,1,0:T(8,128)(2,1)S(1)} %get-tuple-element.39), channel_id=1, source_target_pairs={{16,0},{32,16},{48,32},{64,48},{80,64},{96,80},{112,96},{128,112},... | collective-permute-start | bytes 221192 | tf_op jit(solution)/shard_map/ppermute | solution.py:283
  66.2 28.6 %all-to-all-start.2 = ((bf16[16,2,7,16,128]{4,3,2,1,0:T(8,128)(2,1)}), bf16[16,2,7,16,128]{4,3,2,1,0:T(8,128)(2,1)S(1)}, u32[]{:S(2)}, u32[]{:S(2)}) async-start(bf16[16,2,7,16,128]{4,3,2,1,0:T(8,128)(2,1)} %hub_rows.2), calls=%async_computation.2 | async-start | bytes 1835008 | tf_op jit(solution)/shard_map/all_to_all | solution.py:276
  70.4 7.9 %collective-permute-start.4 = (f32[8,128]{1,0:T(8,128)S(1)}, f32[8,128]{1,0:T(8,128)S(1)}, u32[]{:S(2)}, u32[]{:S(2)}) collective-permute-start(f32[8,128]{1,0:T(8,128)S(1)} %get-tuple-element.42), channel_id=1, source_target_pairs={{0,48},{16,32},{32,16},{48,0},{64,112},{80,96},{96,80},{112,64},{1... | collective-permute-start | bytes 12296 | tf_op jit(solution)/shard_map/ppermute | solution.py:746
  73.2 5.1 %collective-permute-start.3 = (f32[8,128]{1,0:T(8,128)S(1)}, f32[8,128]{1,0:T(8,128)S(1)}, u32[]{:S(2)}, u32[]{:S(2)}) collective-permute-start(f32[8,128]{1,0:T(8,128)S(1)} %get-tuple-element.42), channel_id=1, source_target_pairs={{0,32},{16,48},{32,0},{48,16},{64,96},{80,112},{96,64},{112,80},{1... | collective-permute-start | bytes 12296 | tf_op jit(solution)/shard_map/ppermute | solution.py:746
  73.6 4.7 %collective-permute-start.2 = (f32[8,128]{1,0:T(8,128)S(1)}, f32[8,128]{1,0:T(8,128)S(1)}, u32[]{:S(2)}, u32[]{:S(2)}) collective-permute-start(f32[8,128]{1,0:T(8,128)S(1)} %get-tuple-element.42), channel_id=1, source_target_pairs={{0,16},{16,0},{32,48},{48,32},{64,80},{80,64},{96,112},{112,96},{1... | collective-permute-start | bytes 12296 | tf_op jit(solution)/shard_map/ppermute | solution.py:746
  73.9 4.5 %collective-permute-start.5 = (bf16[18,16,128]{2,1,0:T(8,128)(2,1)S(1)}, bf16[18,16,128]{2,1,0:T(8,128)(2,1)S(1)}, u32[]{:S(2)}, u32[]{:S(2)}) collective-permute-start(bf16[18,16,128]{2,1,0:T(8,128)(2,1)S(1)} %get-tuple-element.43), channel_id=1, source_target_pairs={{0,16},{16,32},{32,48},{48,64},{64,80},{80,96},{96,112},{112,128},... | collective-permute-start | bytes 221192 | tf_op jit(solution)/shard_map/ppermute | solution.py:282
  76.9 5.4 %collective-permute-start.6 = (bf16[18,16,128]{2,1,0:T(8,128)(2,1)S(1)}, bf16[18,16,128]{2,1,0:T(8,128)(2,1)S(1)}, u32[]{:S(2)}, u32[]{:S(2)}) collective-permute-start(bf16[18,16,128]{2,1,0:T(8,128)(2,1)S(1)} %get-tuple-element.44), channel_id=1, source_target_pairs={{16,0},{32,16},{48,32},{64,48},{80,64},{96,80},{112,96},{128,112},... | collective-permute-start | bytes 221192 | tf_op jit(solution)/shard_map/ppermute | solution.py:283
  82.3 7.8 %collective-permute-start.9 = (f32[8,128]{1,0:T(8,128)S(1)}, f32[8,128]{1,0:T(8,128)S(1)}, u32[]{:S(2)}, u32[]{:S(2)}) collective-permute-start(f32[8,128]{1,0:T(8,128)S(1)} %add_add_fusion.1), channel_id=1, source_target_pairs={{0,192},{16,208},{32,224},{48,240},{64,128},{80,144},{96,160},{112... | collective-permute-start | bytes 12296 | tf_op jit(solution)/shard_map/ppermute | solution.py:746
  85.1 5.0 %collective-permute-start.8 = (f32[8,128]{1,0:T(8,128)S(1)}, f32[8,128]{1,0:T(8,128)S(1)}, u32[]{:S(2)}, u32[]{:S(2)}) collective-permute-start(f32[8,128]{1,0:T(8,128)S(1)} %add_add_fusion.1), channel_id=1, source_target_pairs={{0,128},{16,144},{32,160},{48,176},{64,192},{80,208},{96,224},{112... | collective-permute-start | bytes 12296 | tf_op jit(solution)/shard_map/ppermute | solution.py:746
  85.6 4.5 %collective-permute-start.7 = (f32[8,128]{1,0:T(8,128)S(1)}, f32[8,128]{1,0:T(8,128)S(1)}, u32[]{:S(2)}, u32[]{:S(2)}) collective-permute-start(f32[8,128]{1,0:T(8,128)S(1)} %add_add_fusion.1), channel_id=1, source_target_pairs={{0,64},{16,80},{32,96},{48,112},{64,0},{80,16},{96,32},{112,48},{1... | collective-permute-start | bytes 12296 | tf_op jit(solution)/shard_map/ppermute | solution.py:746
  94.7 7.9 %copy-start.4 = (bf16[16,2,7,16,128]{4,3,2,1,0:T(8,128)(2,1)}, bf16[16,2,7,16,128]{4,3,2,1,0:T(8,128)(2,1)S(1)}, u32[]{:S(2)}) copy-start(bf16[16,2,7,16,128]{4,3,2,1,0:T(8,128)(2,1)S(1)} %all-to-all-done.2.rim_ref) | copy-start | bytes 2752516
  94.7 30.4 %all-to-all-start.3 = ((bf16[16,2,7,16,128]{4,3,2,1,0:T(8,128)(2,1)}), bf16[16,2,7,16,128]{4,3,2,1,0:T(8,128)(2,1)S(1)}, u32[]{:S(2)}, u32[]{:S(2)}) async-start(bf16[16,2,7,16,128]{4,3,2,1,0:T(8,128)(2,1)} %hub_rows.3), calls=%async_computation.3 | async-start | bytes 1835008 | tf_op jit(solution)/shard_map/all_to_all | solution.py:276
  125.1 8.0 %copy-start.6 = (bf16[16,2,7,16,128]{4,3,2,1,0:T(8,128)(2,1)}, bf16[16,2,7,16,128]{4,3,2,1,0:T(8,128)(2,1)S(1)}, u32[]{:S(2)}) copy-start(bf16[16,2,7,16,128]{4,3,2,1,0:T(8,128)(2,1)S(1)} %all-to-all-done.3.rim_hbm.rim_ref) | copy-start | bytes 2752516
  125.1 34.2 %all-to-all-start.4 = ((f32[16,216,128]{2,1,0:T(8,128)}), f32[16,216,128]{2,1,0:T(8,128)S(1)}, u32[]{:S(2)}, u32[]{:S(2)}) async-start(f32[16,216,128]{2,1,0:T(8,128)} %bitcast.39), calls=%async_computation.4 | async-start | bytes 3538944 | tf_op jit(solution)/shard_map/all_to_all | solution.py:276
  140.6 18.8 %copy-start.7 = (f32[8,128]{1,0:T(8,128)S(1)}, f32[8,128]{1,0:T(8,128)}, u32[]{:S(2)}) copy-start(f32[8,128]{1,0:T(8,128)} %get-tuple-element.64) | copy-start | bytes 12292
  160.1 14.5 %all-to-all-start.5 = ((f32[16,24,128]{2,1,0:T(8,128)}), f32[16,24,128]{2,1,0:T(8,128)S(1)}, u32[]{:S(2)}, u32[]{:S(2)}) async-start(f32[16,24,128]{2,1,0:T(8,128)} %pad_maximum_fusion), calls=%async_computation.5 | async-start | bytes 393216 | tf_op jit(solution)/shard_map/all_to_all | solution.py:276
  175.3 10.7 %all-to-all-start.6 = ((bf16[16,16,128]{2,1,0:T(8,128)(2,1)}), bf16[16,16,128]{2,1,0:T(8,128)(2,1)S(1)}, u32[]{:S(2)}, u32[]{:S(2)}) async-start(bf16[16,16,128]{2,1,0:T(8,128)(2,1)} %broadcast_in_dim.12), calls=%async_computation.6 | async-start | bytes 131072 | tf_op jit(solution)/shard_map/all_to_all | solution.py:276
  187.2 17.5 %all-to-all-start.7 = ((bf16[16,224,128]{2,1,0:T(8,128)(2,1)}), bf16[16,224,128]{2,1,0:T(8,128)(2,1)S(1)}, u32[]{:S(2)}, u32[]{:S(2)}) async-start(bf16[16,224,128]{2,1,0:T(8,128)(2,1)} %broadcast_in_dim.14), calls=%async_computation.7 | async-start | bytes 1835008 | tf_op jit(solution)/shard_map/all_to_all | solution.py:276
  204.7 1.0 copy-start.3
